TPU v7x, 128 devices: a whole 4x4x4 slice. The times are simulated.
128 devices in a mesh: row: 32 (over z_lo, x, y), rep: 4 (over z_hi, core).
Axes of the slice: x: 4, y: 4, z: 4 (z_hi: 2, z_lo: 2; z = z_hi * 2 + z_lo), core: 2. Of those that a mesh axis runs over, the one named last changes fastest.
Arguments:
- features: bfloat16 [65536, 256], P(('row', 'rep')), may hold values from -6 to 6
- self_weight: bfloat16 [256, 256], replicated, may hold values from -0.375 to 0.375
- neigh_weight: bfloat16 [256, 256], replicated, may hold values from -0.375 to 0.375
- tile_rows: int32 [40960], P(('row', 'rep')), may hold values from 0 to 15, as said below
- tile_cols: int32 [40960], P(('row', 'rep')), may hold values from 0 to 511, as said below
- tile_masks: int32 [40960, 128, 128], P(('row', 'rep')), may hold values from 0 to 1, as said below
- cotangent: bfloat16 [65536, 256], P(('row', 'rep'))
Outputs:
- output: bfloat16 [65536, 256], P(('row', 'rep'))
- grad_features: bfloat16 [65536, 256], P(('row', 'rep'))
- grad_self_weight: float32 [256, 256], replicated
- grad_neigh_weight: float32 [256, 256], replicated
Inputs may be any that keep to these rules, and one draw needn't show every extreme that they name: `tile_rows`: within one device's slots, a tile's block row inside that device's row block of 2048 nodes. `tile_cols`: on the device with rep index r, every slot's column c has (c // 4) % (number of rep devices) == r. Live tiles fill the first slots of a device, the rest are empty (zero masks); at most 320 tiles are live on a device and some device has all 320 live. `tile_masks`: every live tile has at least one nonzero; empty slots are all zero.
All inputs are finite; a program needn't handle non-finite values.
Results may differ from a plain program's by a relative error of at most 0.025.
Values may be sent and summed in bfloat16 or wider, within the bound.
No kernel may reach another device: no remote copies, remote signals or barrier semaphores. Data moves between devices by JAX's collectives and lax.ppermute only.
A program may use at most 192 MiB of HBM per device.

v0:
```python
import jax
import jax.numpy as jnp
from jax import lax
from jax.sharding import PartitionSpec as P

group_size = 32


def pick_matrix(index, count):
    return (index[:, None] == jnp.arange(count, dtype=jnp.int32)[None, :]).astype(jnp.bfloat16)


def place_rows(placer, values):
    contract_first = (((0,), (0,)), ((), ()))
    high_part = values.astype(jnp.bfloat16)
    low_part = (values - high_part.astype(jnp.float32)).astype(jnp.bfloat16)
    first = lax.dot_general(placer, high_part, contract_first, preferred_element_type=jnp.float32)
    second = lax.dot_general(placer, low_part, contract_first, preferred_element_type=jnp.float32)
    return first + second


def local(features, self_weight, neigh_weight, tile_rows, tile_cols, tile_masks, cotangent):
    node_dev = features.shape[0]
    width = features.shape[1]
    tile = tile_masks.shape[1]
    slots = tile_masks.shape[0]
    nrep = lax.axis_size("rep")
    nrow = lax.axis_size("row")
    per_section = node_dev // tile
    per_block = node_dev * nrep // tile
    section_count = nrow * per_section
    contract_first = (((0,), (0,)), ((), ()))
    turns = slots // group_size

    def slot_group(turn):
        start = turn * group_size
        masks = lax.dynamic_slice_in_dim(tile_masks, start, group_size, 0)
        rows = lax.dynamic_slice_in_dim(tile_rows, start, group_size, 0)
        cols = lax.dynamic_slice_in_dim(tile_cols, start, group_size, 0)
        local_cols = cols // (per_section * nrep) * per_section + cols % per_section
        return (masks, rows, local_cols)

    gathered = lax.all_gather(features, "row", axis=0, tiled=True)
    section_flat = gathered.reshape(section_count, tile * width)

    def forward_turn(turn, carry):
        summed, degree = carry
        masks, rows, local_cols = slot_group(turn)
        chooser = pick_matrix(local_cols, section_count)
        picked = (
            jnp.dot(chooser, section_flat, preferred_element_type=jnp.float32)
            .astype(jnp.bfloat16)
            .reshape(group_size, tile, width)
        )
        mask_bf = masks.astype(jnp.bfloat16)
        prod = jnp.einsum("tij,tjh->tih", mask_bf, picked, preferred_element_type=jnp.float32)
        placer = pick_matrix(rows, per_block)
        summed = summed + place_rows(placer, prod.reshape(group_size, tile * width))
        counts = jnp.sum(masks, axis=2).astype(jnp.bfloat16)
        degree = degree + lax.dot_general(
            placer, counts, contract_first, preferred_element_type=jnp.float32
        )
        return (summed, degree)

    init = (
        jnp.zeros((per_block, tile * width), jnp.float32),
        jnp.zeros((per_block, tile), jnp.float32),
    )
    summed, degree = lax.fori_loop(0, turns, forward_turn, init)
    quarter_sum, quarter_degree = (
        lax.psum_scatter(
            summed.reshape(per_block * tile, width).astype(jnp.bfloat16),
            "rep",
            scatter_dimension=0,
            tiled=True,
        ).astype(jnp.float32),
        lax.psum_scatter(
            degree.reshape(per_block * tile).astype(jnp.bfloat16),
            "rep",
            scatter_dimension=0,
            tiled=True,
        ).astype(jnp.float32),
    )
    scale = lax.rsqrt(jnp.maximum(quarter_degree, 1.0))
    agg = (quarter_sum * scale[:, None]).astype(jnp.bfloat16)
    pre = jnp.dot(features, self_weight, preferred_element_type=jnp.float32) + jnp.dot(
        agg, neigh_weight, preferred_element_type=jnp.float32
    )
    sig = jax.nn.sigmoid(pre)
    output = (pre * sig).astype(jnp.bfloat16)
    grad_pre = (cotangent.astype(jnp.float32) * sig * (1.0 + pre * (1.0 - sig))).astype(
        jnp.bfloat16
    )
    contract_rows = (((0,), (0,)), ((), ()))
    contract_cols = (((1,), (1,)), ((), ()))
    self_part = lax.dot_general(
        features, grad_pre, contract_rows, preferred_element_type=jnp.float32
    )
    neigh_part = lax.dot_general(agg, grad_pre, contract_rows, preferred_element_type=jnp.float32)
    self_total, neigh_total = lax.psum((self_part, neigh_part), ("row", "rep"))
    node_total = node_dev * nrow * nrep
    norm = node_total ** (-0.5)
    grad_mean = (
        lax.dot_general(grad_pre, neigh_weight, contract_cols, preferred_element_type=jnp.float32)
        * scale[:, None]
    ).astype(jnp.bfloat16)
    block_grad = lax.all_gather(grad_mean, "rep", axis=0, tiled=True)
    grad_flat = block_grad.reshape(per_block, tile * width)

    def backward_turn(turn, spread):
        masks, rows, local_cols = slot_group(turn)
        chooser = pick_matrix(rows, per_block)
        picked = (
            jnp.dot(chooser, grad_flat, preferred_element_type=jnp.float32)
            .astype(jnp.bfloat16)
            .reshape(group_size, tile, width)
        )
        prod = jnp.einsum(
            "tij,tih->tjh", masks.astype(jnp.bfloat16), picked, preferred_element_type=jnp.float32
        )
        placer = pick_matrix(local_cols, section_count)
        return spread + place_rows(placer, prod.reshape(group_size, tile * width))

    spread = lax.fori_loop(
        0, turns, backward_turn, jnp.zeros((section_count, tile * width), jnp.float32)
    )
    spread = spread.reshape(nrow * node_dev, width)
    incoming = lax.psum_scatter(
        spread.astype(jnp.bfloat16), "row", scatter_dimension=0, tiled=True
    ).astype(jnp.float32)
    grad_feat = (
        lax.dot_general(grad_pre, self_weight, contract_cols, preferred_element_type=jnp.float32)
        + incoming
    ).astype(jnp.bfloat16)
    return (output, grad_feat, self_total * norm, neigh_total * norm)


def solution(mesh):
    in_specs = (
        P(("row", "rep"), None),
        P(),
        P(),
        P(("row", "rep")),
        P(("row", "rep")),
        P(("row", "rep"), None, None),
        P(("row", "rep"), None),
    )
    out_specs = (P(("row", "rep"), None), P(("row", "rep"), None), P(), P())
    return jax.shard_map(local, mesh=mesh, in_specs=in_specs, out_specs=out_specs, check_vma=False)
```

profile of v0, /device:TPU:0, one launch (start us, length us, event | category | flops | bytes accessed | tf_op | source)
XLA Modules:
  0.0 1081.9 jit_solution(3889998122669597756)
XLA Ops:
  8.0 171.3 %all-gather.3.cloned.1.call-done = bf16[16384,256]{1,0:T(8,128)(2,1)} async-done(((bf16[512,256]{1,0:T(8,128)(2,1)}), bf16[16384,256]{1,0:T(8,128)(2,1)}) %all-gather.3.cloned.1.call-update) | async-done | bytes 8388624 | tf_op jit(solution)/shard_map/all_gather | solution.py:43
  179.3 13.5 %reshape.65 = bf16[128,32768]{1,0:T(8,128)(2,1)} reshape(bf16[16384,256]{1,0:T(8,128)(2,1)} %all-gather.3.cloned.1.call-done) | data formatting | bytes 16777216 | tf_op jit(solution)/shard_map/reshape | solution.py:44
  192.8 210.5 %while.34 = (s32[]{:T(128)}, f32[16,32768]{1,0:T(8,128)}, f32[16,128]{1,0:T(8,128)S(1)}, s32[320]{0:T(512)S(1)}, s32[320,128,128]{2,1,0:T(8,128)}, /*index=5*/s3...) while((s32[]{:T(128)}, f32[16,32768]{1,0:T(8,128)}, ...), condition=%wide.region_2.3_spmd.clone, body=%wide.region_0.2_spmd.clone.sunk | while | flops 613034240 | bytes 67159256 | solution.py:69
  205.3 5.6 fusion.63
  225.8 6.2 fusion.63
  234.5 4.6 convolution_convert_fusion.4
  246.9 6.2 fusion.63
  255.6 4.6 convolution_convert_fusion.4
  268.0 6.2 fusion.63
  276.7 4.6 convolution_convert_fusion.4
  289.1 6.2 fusion.63
  297.8 4.6 convolution_convert_fusion.4
  310.3 6.2 fusion.63
  319.0 4.6 convolution_convert_fusion.4
  331.4 6.2 fusion.63
  340.1 4.6 convolution_convert_fusion.4
  352.5 6.2 fusion.63
  361.2 4.6 convolution_convert_fusion.4
  373.6 6.2 fusion.63
  382.3 4.6 convolution_convert_fusion.4
  394.7 6.2 fusion.63
  408.0 7.2 all-reduce
  415.3 24.2 %reduce-scatter.3.cloned.1.call-done = bf16[512,256]{1,0:T(8,128)(2,1)} async-done(((bf16[2048,256]{1,0:T(8,128)(2,1)}), bf16[512,256]{1,0:T(8,128)(2,1)}) %reduce-scatter.3.cloned.1.call-update) | async-done | bytes 262160 | tf_op jit(solution)/shard_map/reduce_scatter | solution.py:71
  445.0 17.9 %all-gather.5.cloned.1.call-done = bf16[2048,256]{1,0:T(8,128)(2,1)} async-done(((bf16[512,256]{1,0:T(8,128)(2,1)}), bf16[2048,256]{1,0:T(8,128)(2,1)}) %all-gather.5.cloned.1.call-update) | async-done | bytes 1048592 | tf_op jit(solution)/shard_map/all_gather | solution.py:107
  464.4 407.3 %while.35 = (s32[]{:T(128)}, f32[128,32768]{1,0:T(8,128)}, s32[320]{0:T(512)S(1)}, s32[320,128,128]{2,1,0:T(8,128)}, s32[320]{0:T(512)S(1)}, /*index=5*/bf16[16,...) while((s32[]{:T(128)}, f32[128,32768]{1,0:T(8,128)}, s32[320]{0:T(512)S(1)}, ...), condition=%wide.region_6.7_spmd.clone, body=%wide.region_5.6_spmd.clone.sunk | while | flops 858268928 | bytes 124781640 | solution.py:124
  476.1 8.2 fusion.70
  484.3 16.5 %fusion.71 = f32[128,32768]{1,0:T(8,128)} fusion(f32[128,32768]{1,0:T(8,128)} %fusion.70, f32[128,32768]{1,0:T(8,128)} %get-tuple-element.565, pred[]{:T(512)S(6)} %compare.29, f32[32,32768]{1,0:T(8,128)} %bitcast.54, s32[32]{0:T(128)S(1)} %fusion.69), kind=kOutput, calls=%fused_computation.27.clone.1 | convolution fusion | flops 285216768 | bytes 54526080 | tf_op jit(solution)/shard_map/while/body/eval_jaxpr/dot_general | solution.py:18
  512.5 8.2 fusion.70
  520.7 21.3 %fusion.71 = f32[128,32768]{1,0:T(8,128)} fusion(f32[128,32768]{1,0:T(8,128)} %fusion.70, f32[128,32768]{1,0:T(8,128)} %get-tuple-element.565, pred[]{:T(512)S(6)} %compare.29, f32[32,32768]{1,0:T(8,128)} %bitcast.54, s32[32]{0:T(128)S(1)} %fusion.69), kind=kOutput, calls=%fused_computation.27.clone.1 | convolution fusion | flops 285216768 | bytes 54526080 | tf_op jit(solution)/shard_map/while/body/eval_jaxpr/dot_general | solution.py:18
  553.7 8.2 fusion.70
  561.9 21.3 %fusion.71 = f32[128,32768]{1,0:T(8,128)} fusion(f32[128,32768]{1,0:T(8,128)} %fusion.70, f32[128,32768]{1,0:T(8,128)} %get-tuple-element.565, pred[]{:T(512)S(6)} %compare.29, f32[32,32768]{1,0:T(8,128)} %bitcast.54, s32[32]{0:T(128)S(1)} %fusion.69), kind=kOutput, calls=%fused_computation.27.clone.1 | convolution fusion | flops 285216768 | bytes 54526080 | tf_op jit(solution)/shard_map/while/body/eval_jaxpr/dot_general | solution.py:18
  595.0 8.2 fusion.70
  603.2 21.3 %fusion.71 = f32[128,32768]{1,0:T(8,128)} fusion(f32[128,32768]{1,0:T(8,128)} %fusion.70, f32[128,32768]{1,0:T(8,128)} %get-tuple-element.565, pred[]{:T(512)S(6)} %compare.29, f32[32,32768]{1,0:T(8,128)} %bitcast.54, s32[32]{0:T(128)S(1)} %fusion.69), kind=kOutput, calls=%fused_computation.27.clone.1 | convolution fusion | flops 285216768 | bytes 54526080 | tf_op jit(solution)/shard_map/while/body/eval_jaxpr/dot_general | solution.py:18
  636.2 8.2 fusion.70
  644.4 21.3 %fusion.71 = f32[128,32768]{1,0:T(8,128)} fusion(f32[128,32768]{1,0:T(8,128)} %fusion.70, f32[128,32768]{1,0:T(8,128)} %get-tuple-element.565, pred[]{:T(512)S(6)} %compare.29, f32[32,32768]{1,0:T(8,128)} %bitcast.54, s32[32]{0:T(128)S(1)} %fusion.69), kind=kOutput, calls=%fused_computation.27.clone.1 | convolution fusion | flops 285216768 | bytes 54526080 | tf_op jit(solution)/shard_map/while/body/eval_jaxpr/dot_general | solution.py:18
  677.4 8.2 fusion.70
  685.6 21.3 %fusion.71 = f32[128,32768]{1,0:T(8,128)} fusion(f32[128,32768]{1,0:T(8,128)} %fusion.70, f32[128,32768]{1,0:T(8,128)} %get-tuple-element.565, pred[]{:T(512)S(6)} %compare.29, f32[32,32768]{1,0:T(8,128)} %bitcast.54, s32[32]{0:T(128)S(1)} %fusion.69), kind=kOutput, calls=%fused_computation.27.clone.1 | convolution fusion | flops 285216768 | bytes 54526080 | tf_op jit(solution)/shard_map/while/body/eval_jaxpr/dot_general | solution.py:18
  718.6 8.2 fusion.70
  726.8 21.3 %fusion.71 = f32[128,32768]{1,0:T(8,128)} fusion(f32[128,32768]{1,0:T(8,128)} %fusion.70, f32[128,32768]{1,0:T(8,128)} %get-tuple-element.565, pred[]{:T(512)S(6)} %compare.29, f32[32,32768]{1,0:T(8,128)} %bitcast.54, s32[32]{0:T(128)S(1)} %fusion.69), kind=kOutput, calls=%fused_computation.27.clone.1 | convolution fusion | flops 285216768 | bytes 54526080 | tf_op jit(solution)/shard_map/while/body/eval_jaxpr/dot_general | solution.py:18
  759.8 8.2 fusion.70
  768.0 21.3 %fusion.71 = f32[128,32768]{1,0:T(8,128)} fusion(f32[128,32768]{1,0:T(8,128)} %fusion.70, f32[128,32768]{1,0:T(8,128)} %get-tuple-element.565, pred[]{:T(512)S(6)} %compare.29, f32[32,32768]{1,0:T(8,128)} %bitcast.54, s32[32]{0:T(128)S(1)} %fusion.69), kind=kOutput, calls=%fused_computation.27.clone.1 | convolution fusion | flops 285216768 | bytes 54526080 | tf_op jit(solution)/shard_map/while/body/eval_jaxpr/dot_general | solution.py:18
  801.0 8.2 fusion.70
  809.2 21.3 %fusion.71 = f32[128,32768]{1,0:T(8,128)} fusion(f32[128,32768]{1,0:T(8,128)} %fusion.70, f32[128,32768]{1,0:T(8,128)} %get-tuple-element.565, pred[]{:T(512)S(6)} %compare.29, f32[32,32768]{1,0:T(8,128)} %bitcast.54, s32[32]{0:T(128)S(1)} %fusion.69), kind=kOutput, calls=%fused_computation.27.clone.1 | convolution fusion | flops 285216768 | bytes 54526080 | tf_op jit(solution)/shard_map/while/body/eval_jaxpr/dot_general | solution.py:18
  842.2 8.2 fusion.70
  850.4 21.3 %fusion.71 = f32[128,32768]{1,0:T(8,128)} fusion(f32[128,32768]{1,0:T(8,128)} %fusion.70, f32[128,32768]{1,0:T(8,128)} %get-tuple-element.565, pred[]{:T(512)S(6)} %compare.29, f32[32,32768]{1,0:T(8,128)} %bitcast.54, s32[32]{0:T(128)S(1)} %fusion.69), kind=kOutput, calls=%fused_computation.27.clone.1 | convolution fusion | flops 285216768 | bytes 54526080 | tf_op jit(solution)/shard_map/while/body/eval_jaxpr/dot_general | solution.py:18
  871.7 8.9 convert_element_type.178
  880.6 13.5 %convert_element_type.179 = bf16[16384,256]{1,0:T(8,128)(2,1)} reshape(bf16[128,32768]{1,0:T(8,128)(2,1)} %convert_element_type.178) | data formatting | bytes 16777216 | tf_op jit(solution)/shard_map/convert_element_type | solution.py:129
  896.9 176.5 %reduce-scatter.5.cloned.1.call-done = bf16[512,256]{1,0:T(8,128)(2,1)} async-done(((bf16[16384,256]{1,0:T(8,128)(2,1)}), bf16[512,256]{1,0:T(8,128)(2,1)}) %reduce-scatter.5.cloned.1.call-update) | async-done | bytes 262160 | tf_op jit(solution)/shard_map/reduce_scatter | solution.py:128
  (255 shorter events, 245.1 us)
Async XLA Ops:
  7.2 432.2 %copy-start = (bf16[256,256]{1,0:T(8,128)(2,1)S(1)}, bf16[256,256]{1,0:T(8,128)(2,1)}, u32[]{:S(2)}) copy-start(bf16[256,256]{1,0:T(8,128)(2,1)} %param.13) | copy-start | bytes 393220
  7.2 172.1 %all-gather.3.cloned.1.call-start = ((), (), s32[]{:S(2)}) async-start(), calls=%async_computation.2 | async-start | bytes 8650752 | tf_op jit(solution)/shard_map/all_gather | solution.py:43
  7.9 431.5 %reduce-scatter.3.cloned.1.call-start = ((), (), s32[]{:S(2)}) async-start(), calls=%async_computation.3 | async-start | bytes 1310720 | tf_op jit(solution)/shard_map/reduce_scatter | solution.py:71
  8.0 184.8 %copy-start.11 = (s32[320]{0:T(512)S(1)}, s32[320]{0:T(512)}, u32[]{:S(2)}) copy-start(s32[320]{0:T(512)} %param.14) | copy-start | bytes 3844
  8.0 184.8 %copy-start.12 = (s32[320]{0:T(512)S(1)}, s32[320]{0:T(512)}, u32[]{:S(2)}) copy-start(s32[320]{0:T(512)} %param.15) | copy-start | bytes 3844
  202.7 2.0 copy-start.2
  223.3 2.0 copy-start.2
  244.4 2.0 copy-start.2
  265.5 2.0 copy-start.2
  286.6 2.0 copy-start.2
  307.7 2.0 copy-start.2
  328.8 2.0 copy-start.2
  349.9 2.0 copy-start.2
  371.1 2.0 copy-start.2
  392.2 2.0 copy-start.2
  403.3 3.2 copy-start.13
  403.3 4.4 copy-start.6
  403.3 4.4 copy-start.7
  403.3 36.1 %copy-start.10 = (bf16[512,256]{1,0:T(8,128)(2,1)S(1)}, bf16[512,256]{1,0:T(8,128)(2,1)}, u32[]{:S(2)}) copy-start(bf16[512,256]{1,0:T(8,128)(2,1)} %param.17) | copy-start | bytes 786436
  406.4 56.4 %all-gather.5.cloned.1.call-start = ((), (), s32[]{:S(2)}) async-start(), calls=%async_computation.4 | async-start | bytes 1310720 | tf_op jit(solution)/shard_map/all_gather | solution.py:107
  439.4 4.2 copy-start.9
  441.6 22.8 %copy-start.4 = (bf16[512,256]{1,0:T(8,128)(2,1)}, bf16[512,256]{1,0:T(8,128)(2,1)S(1)}, u32[]{:S(2)}) copy-start(bf16[512,256]{1,0:T(8,128)(2,1)S(1)} %get-tuple-element.437) | copy-start | bytes 786436
  442.6 451.6 %all-reduce.4.cloned.1.call-start = ((), (), s32[]{:S(2)}) async-start(), calls=%async_computation.6 | async-start | bytes 1048576 | tf_op jit(solution)/shard_map/psum | solution.py:100
  444.7 628.7 %reduce-scatter.5.cloned.1.call-start = ((), (), s32[]{:S(2)}) async-start(), calls=%async_computation.5 | async-start | bytes 8650752 | tf_op jit(solution)/shard_map/reduce_scatter | solution.py:128
  476.0 8.3 copy-start.3
  512.4 8.3 copy-start.3
  553.6 8.3 copy-start.3
  594.9 8.3 copy-start.3
  636.1 8.3 copy-start.3
  677.3 8.3 copy-start.3
  718.5 8.3 copy-start.3
  759.7 8.3 copy-start.3
  800.9 8.3 copy-start.3
  842.1 8.3 copy-start.3
  894.1 181.3 %copy-start.1 = (bf16[256,256]{1,0:T(8,128)(2,1)S(1)}, bf16[256,256]{1,0:T(8,128)(2,1)}, u32[]{:S(2)}) copy-start(bf16[256,256]{1,0:T(8,128)(2,1)} %param.13) | copy-start | bytes 393220
  894.1 179.3 %copy-start.5 = (bf16[512,256]{1,0:T(8,128)(2,1)S(1)}, bf16[512,256]{1,0:T(8,128)(2,1)}, u32[]{:S(2)}) copy-start(bf16[512,256]{1,0:T(8,128)(2,1)} %copy-done.4) | copy-start | bytes 786436
  894.1 179.3 %copy-start.8 = (bf16[256,256]{1,0:T(8,128)(2,1)S(1)}, bf16[256,256]{1,0:T(8,128)(2,1)}, u32[]{:S(2)}) copy-start(bf16[256,256]{1,0:T(8,128)(2,1)} %param.12) | copy-start | bytes 393220
Sparse Core Ops, SparseCore 0:
  9.7 169.5 all-gather.2
  406.6 32.8 reduce-scatter.2
  442.7 20.1 all-gather.4
  469.0 144.0 all-reduce.3
  894.2 179.1 reduce-scatter.4
where the time goes:
time: 1080 us
  matrix products  473 us (44%)
  waiting for transfers between devices  391 us (36%)
  local copies, waits for them, and re-layouts  160 us (15%)
  other arithmetic  35.6 us (3%)
  between operations  14.6 us (1%)
    dot_general x20, matrix products, place_rows(): lax.dot_general(placer, low_part, contract_first, preferred_element_type=...  269 us
    reduce_scatter x1, waiting for transfers between devices, local(): lax.psum_scatter(spread.astype(jnp.bfloat16), 'row', scatter_dimension=0,...  176 us
    all_gather x1, waiting for transfers between devices, local(): gathered = lax.all_gather(features, 'row', axis=0, tiled=True)  171 us
    while x80, local copies, waits for them, and re-layouts  90.8 us
    dot_general x20, matrix products, place_rows(): lax.dot_general(placer, high_part, contract_first, preferred_element_type...  87.3 us
    dot_general x10, matrix products, forward_turn(): jnp.dot(chooser, section_flat, preferred_element_type=jnp.float32)  46.4 us
    dynamic_slice x20, local copies, waits for them, and re-layouts, slot_group(): masks = lax.dynamic_slice_in_dim(tile_masks, start, group_size, 0)  35.7 us
    dot_general x10, matrix products, backward_turn(): jnp.einsum('tij,tih->tjh', masks.astype(jnp.bfloat16), picked, preferred_...  29.2 us
  transfers between devices with their start and end apart: 5, of which 4 were waited for; matrix products, arithmetic and copies ran while one was open for 40% of the time, Pallas kernels for 0%

commit v1 on v0

v1 whole, which is shorter than its diff:
```python
import functools

import jax
import jax.numpy as jnp
from jax import lax
from jax.experimental import pallas as pl
from jax.experimental.pallas import tpu as pltpu
from jax.sharding import PartitionSpec as P

TILE = 128
GROUP = 8
CLASSES = 4
PIECES = 4
PIECE_BLOCKS = 8
CLASS_BLOCKS = PIECES * PIECE_BLOCKS
BLOCK_TILES = 16
BOTH = ("row", "rep")
MIB = 1024 * 1024


def pairs(step):
    out = []
    for z in range(2):
        for x in range(4):
            for y in range(4):
                for h in range(2):
                    for c in range(2):
                        src = (z * 16 + x * 4 + y) * 4 + h * 2 + c
                        z2, x2, y2, h2, c2 = step(z, x, y, h, c)
                        dst = ((z2 % 2) * 16 + (x2 % 4) * 4 + y2 % 4) * 4 + (h2 % 2) * 2 + c2 % 2
                        out.append((src, dst))
    return out


def move(value, step):
    return lax.ppermute(value, BOTH, pairs(step))


def swap_core(value):
    return move(value, lambda z, x, y, h, c: (z, x, y, h, c + 1))


def swap_high(value):
    return move(value, lambda z, x, y, h, c: (z, x, y, h + 1, c))


def swap_low(value):
    return move(value, lambda z, x, y, h, c: (z + 1, x, y, h, c))


def move_p(value, by):
    return move(value, lambda z, x, y, h, c: (z, x + by, y, h, c) if c == 0 else (z, x, y + by, h, c))


def move_q(value, by):
    return move(value, lambda z, x, y, h, c: (z, x, y + by, h, c) if c == 0 else (z, x + by, y, h, c))


def params(mib):
    return pltpu.CompilerParams(vmem_limit_bytes=mib * MIB)


def prep_kernel(rows_ref, mask_ref, plain_ref, turned_ref, degree_ref):
    step = pl.program_id(0)

    @pl.when(step == 0)
    def _():
        degree_ref[...] = jnp.zeros_like(degree_ref)

    for k in range(BLOCK_TILES):
        wide = mask_ref[k].astype(jnp.float32)
        plain_ref[k] = wide.astype(jnp.bfloat16)
        turned = wide.T
        turned_ref[k] = turned.astype(jnp.bfloat16)
        row = rows_ref[step * BLOCK_TILES + k]
        degree_ref[pl.ds(row, 1), :] += jnp.sum(turned, axis=0, keepdims=True)


def prep(tile_rows, tile_masks, block_count):
    slots = tile_masks.shape[0]
    block = pl.BlockSpec((BLOCK_TILES, TILE, TILE), lambda i: (i, 0, 0))
    return pl.pallas_call(
        prep_kernel,
        grid=(slots // BLOCK_TILES,),
        in_specs=[pl.BlockSpec(memory_space=pltpu.SMEM), block],
        out_specs=[block, block, pl.BlockSpec((block_count, TILE), lambda i: (0, 0))],
        out_shape=[
            jax.ShapeDtypeStruct((slots, TILE, TILE), jnp.bfloat16),
            jax.ShapeDtypeStruct((slots, TILE, TILE), jnp.bfloat16),
            jax.ShapeDtypeStruct((block_count, TILE), jnp.float32),
        ],
        compiler_params=params(16),
        cost_estimate=pl.CostEstimate(flops=0, bytes_accessed=slots * TILE * TILE * 8, transcendentals=0),
        name="prep",
    )(tile_rows, tile_masks)


def unpack(meta):
    return meta & 1023, (meta >> 10) & 31, meta >> 15


def each_group(first, last, meta_ref, masks_ref, buf, sems, body):
    def fetch(group):
        slot = lax.rem(group, 3)
        for u in range(GROUP):
            tile = unpack(meta_ref[group * GROUP + u])[0]
            pltpu.make_async_copy(masks_ref.at[tile], buf.at[slot, u], sems.at[slot]).start()

    for ahead in range(2):

        @pl.when(first + ahead < last)
        def _():
            fetch(first + ahead)

    def turn(group, carry):
        @pl.when(group + 2 < last)
        def _():
            fetch(group + 2)

        slot = lax.rem(group, 3)
        pltpu.make_async_copy(masks_ref.at[pl.ds(0, GROUP)], buf.at[slot], sems.at[slot]).wait()
        body(group, slot)
        return carry

    lax.fori_loop(first, last, turn, 0)


def forward_kernel(which, first_call, last_call, meta_ref, bounds_ref, masks_ref, *refs):
    pieces = refs[:PIECES]
    refs = refs[PIECES:]
    before = None
    if not first_call:
        before, refs = refs[0], refs[1:]
    if last_call:
        keep_ref, give_ref, feats, buf, sems, feat_sems, total = refs
    else:
        total, feats, buf, sems, feat_sems = refs
    rows = PIECE_BLOCKS * TILE
    copies = []
    for k, piece in enumerate(pieces):
        source = piece.at[0] if len(piece.shape) == 3 else piece
        copies.append(pltpu.make_async_copy(source, feats.at[pl.ds(k * rows, rows)], feat_sems.at[k]))
    if first_call:
        total[...] = jnp.zeros_like(total)
    else:
        copies.append(pltpu.make_async_copy(before, total, feat_sems.at[PIECES]))
    for copy in copies:
        copy.start()
    for copy in copies:
        copy.wait()

    def body(group, slot):
        for u in range(GROUP):
            _, row, block = unpack(meta_ref[group * GROUP + u])
            part = jnp.dot(
                buf[slot, u],
                feats[pl.ds(pl.multiple_of(block * TILE, TILE), TILE), :],
                preferred_element_type=jnp.float32,
            )
            total[pl.ds(pl.multiple_of(row * TILE, TILE), TILE), :] += part

    each_group(bounds_ref[which], bounds_ref[which + 1], meta_ref, masks_ref, buf, sems, body)
    if last_call:
        quarter = keep_ref.shape[1]
        core, high = bounds_ref[CLASSES + 1], bounds_ref[CLASSES + 2]
        for h in range(2):
            side = (high + h) % 2
            kept = pl.multiple_of((side * 2 + core) * quarter, quarter)
            given = pl.multiple_of((side * 2 + 1 - core) * quarter, quarter)
            keep_ref[h] = total[pl.ds(kept, quarter), :].astype(jnp.bfloat16)
            give_ref[h] = total[pl.ds(given, quarter), :].astype(jnp.bfloat16)


def forward_class(which, meta, bounds, masks, pieces, before, row_blocks):
    width = pieces[0].shape[-1]
    first_call, last_call = before is None, which == CLASSES - 1
    total_rows = (row_blocks + 1) * TILE
    feat_rows = (CLASS_BLOCKS + 1) * TILE
    scratch = [
        pltpu.VMEM((feat_rows, width), jnp.bfloat16),
        pltpu.VMEM((3, GROUP, TILE, TILE), jnp.bfloat16),
        pltpu.SemaphoreType.DMA((3,)),
        pltpu.SemaphoreType.DMA((PIECES + 1,)),
    ]
    vmem = pl.BlockSpec(memory_space=pltpu.VMEM)
    if last_call:
        half = jax.ShapeDtypeStruct((2, row_blocks * TILE // 4, width), jnp.bfloat16)
        out_shape, out_specs = [half, half], [vmem, vmem]
        scratch.append(pltpu.VMEM((total_rows, width), jnp.float32))
    else:
        out_shape, out_specs = jax.ShapeDtypeStruct((total_rows, width), jnp.float32), vmem
    smem = pl.BlockSpec(memory_space=pltpu.SMEM)
    anywhere = pl.BlockSpec(memory_space=pl.ANY)
    extra = [] if first_call else [before]
    tiles = masks.shape[0] // CLASSES
    return pl.pallas_call(
        functools.partial(forward_kernel, which, first_call, last_call),
        in_specs=[smem, smem] + [anywhere] * (1 + len(pieces) + len(extra)),
        out_specs=out_specs,
        out_shape=out_shape,
        scratch_shapes=scratch,
        compiler_params=params(16),
        cost_estimate=pl.CostEstimate(
            flops=tiles * TILE * TILE * width * 2 * 4, bytes_accessed=8 * MIB, transcendentals=0
        ),
        name=f"forward_class{which}",
    )(meta, bounds, masks, *pieces, *extra)


def backward_kernel(which, meta_ref, bounds_ref, masks_ref, own, far, near, cross, *refs):
    outs = refs[:PIECES]
    grads, buf, sems, grad_sems, total = refs[PIECES:]
    quarter = own.shape[0]
    core, high = bounds_ref[CLASSES + 1], bounds_ref[CLASSES + 2]
    copies = []
    for k, (piece, h, c) in enumerate(((own, 0, 0), (far, 1, 0), (near, 0, 1), (cross, 1, 1))):
        place = ((high + h) % 2) * 2 + (core + c) % 2
        target = grads.at[pl.ds(pl.multiple_of(place * quarter, quarter), quarter)]
        copies.append(pltpu.make_async_copy(piece, target, grad_sems.at[k]))
    for copy in copies:
        copy.start()
    total[...] = jnp.zeros_like(total)
    for copy in copies:
        copy.wait()

    def body(group, slot):
        for u in range(GROUP):
            _, row, block = unpack(meta_ref[group * GROUP + u])
            part = jnp.dot(
                buf[slot, u],
                grads[pl.ds(pl.multiple_of(row * TILE, TILE), TILE), :],
                preferred_element_type=jnp.float32,
            )
            total[pl.ds(pl.multiple_of(block * TILE, TILE), TILE), :] += part

    each_group(bounds_ref[which], bounds_ref[which + 1], meta_ref, masks_ref, buf, sems, body)
    rows = PIECE_BLOCKS * TILE
    for k, out in enumerate(outs):
        out[...] = total[k * rows : (k + 1) * rows, :].astype(jnp.bfloat16)


def backward_class(which, meta, bounds, masks, grads):
    quarter, width = grads[0].shape
    vmem = pl.BlockSpec(memory_space=pltpu.VMEM)
    smem = pl.BlockSpec(memory_space=pltpu.SMEM)
    anywhere = pl.BlockSpec(memory_space=pl.ANY)
    piece = jax.ShapeDtypeStruct((PIECE_BLOCKS * TILE, width), jnp.bfloat16)
    tiles = masks.shape[0] // CLASSES
    return pl.pallas_call(
        functools.partial(backward_kernel, which),
        in_specs=[smem, smem] + [anywhere] * 5,
        out_specs=[vmem] * PIECES,
        out_shape=[piece] * PIECES,
        scratch_shapes=[
            pltpu.VMEM((4 * quarter + TILE, width), jnp.bfloat16),
            pltpu.VMEM((3, GROUP, TILE, TILE), jnp.bfloat16),
            pltpu.SemaphoreType.DMA((3,)),
            pltpu.SemaphoreType.DMA((4,)),
            pltpu.VMEM(((CLASS_BLOCKS + 1) * TILE, width), jnp.float32),
        ],
        compiler_params=params(16),
        cost_estimate=pl.CostEstimate(
            flops=tiles * TILE * TILE * width * 2 * 4, bytes_accessed=8 * MIB, transcendentals=0
        ),
        name=f"backward_class{which}",
    )(meta, bounds, masks, *grads)


def dense_kernel(
    feat_ref, self_ref, neigh_ref, cot_ref, scale_ref, keep_ref, near_ref, far_ref,
    out_ref, back_ref, mean_ref, weight_ref,
):
    rows_first = (((0,), (0,)), ((), ()))
    cols_both = (((1,), (1,)), ((), ()))
    f32 = jnp.float32
    summed = keep_ref[0].astype(f32) + near_ref[0].astype(f32) + far_ref[...].astype(f32)
    scale = scale_ref[...]
    agg = (summed * scale).astype(jnp.bfloat16)
    feats = feat_ref[...]
    pre = jnp.dot(feats, self_ref[...], preferred_element_type=f32) + jnp.dot(
        agg, neigh_ref[...], preferred_element_type=f32
    )
    sig = jax.nn.sigmoid(pre)
    out_ref[...] = (pre * sig).astype(jnp.bfloat16)
    grad = (cot_ref[...].astype(f32) * sig * (1.0 + pre * (1.0 - sig))).astype(jnp.bfloat16)
    mean = lax.dot_general(grad, neigh_ref[...], cols_both, preferred_element_type=f32) * scale
    mean_ref[...] = mean.astype(jnp.bfloat16)
    width = feats.shape[1]
    weight_ref[:width, :] = lax.dot_general(feats, grad, rows_first, preferred_element_type=f32)
    weight_ref[width:, :] = lax.dot_general(agg, grad, rows_first, preferred_element_type=f32)
    back_ref[...] = lax.dot_general(grad, self_ref[...], cols_both, preferred_element_type=f32)


def dense(features, self_weight, neigh_weight, cotangent, scale, keep, near, far):
    rows, width = features.shape
    vmem = pl.BlockSpec(memory_space=pltpu.VMEM)
    return pl.pallas_call(
        dense_kernel,
        in_specs=[vmem] * 8,
        out_specs=[vmem] * 4,
        out_shape=[
            jax.ShapeDtypeStruct((rows, width), jnp.bfloat16),
            jax.ShapeDtypeStruct((rows, width), jnp.float32),
            jax.ShapeDtypeStruct((rows, width), jnp.bfloat16),
            jax.ShapeDtypeStruct((2 * width, width), jnp.float32),
        ],
        compiler_params=params(32),
        cost_estimate=pl.CostEstimate(
            flops=6 * 2 * rows * width * width, bytes_accessed=4 * MIB, transcendentals=rows * width
        ),
        name="dense",
    )(features, self_weight, neigh_weight, cotangent, scale, keep, near, far)


def plan_tiles(tile_rows, tile_cols, row_blocks):
    slots = tile_rows.shape[0]
    row_index, rep_index = lax.axis_index("row"), lax.axis_index("rep")
    z, x, y = row_index // 16, row_index // 4 % 4, row_index % 4
    core, high = rep_index % 2, rep_index // 2
    section, t = tile_cols // 16, tile_cols % 4
    stream = t // 2
    far_z = (section // 16 != z).astype(jnp.int32)
    dx, dy = (section // 4 % 4 - x) % 4, (section % 4 - y) % 4
    dp, dq = jnp.where(stream == 0, dx, dy), jnp.where(stream == 0, dy, dx)
    kind = jnp.where(dq == 0, 0, jnp.where(dq == 2, 3, 1 + far_z))
    pair = jnp.where(dq % 2 == 0, far_z, (dq == 1).astype(jnp.int32))
    piece = pair * 2 + (stream != core).astype(jnp.int32)
    place = jnp.where(dp == 0, 0, jnp.where(dp == 3, 1, jnp.where(dp == 1, 2, 3)))
    block = piece * PIECE_BLOCKS + place * 2 + t % 2
    slot = jnp.arange(slots, dtype=jnp.int32)
    code = slot + tile_rows * 1024 + block * 32768
    classes = jnp.arange(CLASSES, dtype=jnp.int32)
    counts = jnp.sum((kind[:, None] == classes[None, :]).astype(jnp.int32), axis=0)
    groups = (counts + GROUP - 1) // GROUP
    starts = jnp.sum(
        jnp.where(jnp.arange(CLASSES + 1)[:, None] > classes[None, :], groups[None, :], 0), axis=1
    )
    same_before = (kind[:, None] == kind[None, :]) & (slot[None, :] < slot[:, None])
    rank = jnp.sum(same_before.astype(jnp.int32), axis=1)
    start = jnp.sum(jnp.where(kind[:, None] == classes[None, :], starts[None, :CLASSES], 0), axis=1)
    position = start * GROUP + rank
    places = -(-(slots + CLASSES * (GROUP - 1)) // GROUP) * GROUP
    hit = jnp.arange(places, dtype=jnp.int32)[:, None] == position[None, :]
    pad = row_blocks * 1024 + CLASS_BLOCKS * 32768
    meta = pad + jnp.sum(jnp.where(hit, code[None, :] - pad, 0), axis=1)
    bounds = jnp.concatenate([starts, core[None], high[None]]).astype(jnp.int32)
    return meta.astype(jnp.int32), bounds, core, high


def gather(features, core):
    rows, width = features.shape
    half = rows // 2
    mine = lax.dynamic_slice_in_dim(features, core * half, half, 0)
    theirs = lax.dynamic_slice_in_dim(features, (1 - core) * half, half, 0)
    own = jnp.stack([mine, swap_core(theirs)])
    sides = []
    for start in (own, swap_low(own)):
        near = [start, move_p(start, 1), move_p(start, -1), move_p(start, 2)]
        block = jnp.stack(near, axis=1).reshape(2, 4 * half, width)
        below, above = move_q(block, 1), move_q(block, -1)
        sides.append((block, below, above, move_q(below[0], 1), move_q(above[1], -1)))
    classes = [[], [], [], []]
    for s, (block, below, above, far0, far1) in enumerate(sides):
        classes[0] += [block, swap_core(block[1])]
        classes[1 + s] += [below, swap_core(below[1]), above, swap_core(above[1])]
        classes[3] += [far0, swap_core(far1)]
    return classes


def add(*values):
    return sum(value.astype(jnp.float32) for value in values).astype(jnp.bfloat16)


def scatter(run_class, core):
    far = run_class(3)
    sides = [None, None]
    for s in (1, 0):
        from_below = move_q(far[2 * s], 1)
        from_above = move_q(swap_core(far[2 * s + 1]), -1)
        down, down_other, up, up_other = run_class(1 + s)
        to_above = jnp.stack([add(up, from_below), swap_core(up_other)])
        to_below = jnp.stack([down, add(swap_core(down_other), from_above)])
        sides[s] = (move_q(to_above, 1), move_q(to_below, -1))
    here = run_class(0)
    ends = [None, None]
    for s in (1, 0):
        total = add(jnp.stack([here[2 * s], swap_core(here[2 * s + 1])]), *sides[s])
        parts = total.reshape(2, 4, -1, total.shape[-1])
        ends[s] = sum(
            value.astype(jnp.float32)
            for value in (
                parts[:, 0],
                move_p(parts[:, 1], -1),
                move_p(parts[:, 2], 1),
                move_p(parts[:, 3], 2),
            )
        )
    end = ends[0] + swap_low(ends[1].astype(jnp.bfloat16)).astype(jnp.float32)
    mine = end[0]
    other = swap_core(end[1].astype(jnp.bfloat16)).astype(jnp.float32)
    first = jnp.where(core == 0, mine, other)
    second = jnp.where(core == 0, other, mine)
    return jnp.concatenate([first, second], axis=0)


def local(features, self_weight, neigh_weight, tile_rows, tile_cols, tile_masks, cotangent):
    rows, width = features.shape
    row_blocks = rows * 4 // TILE
    meta, bounds, core, high = plan_tiles(tile_rows, tile_cols, row_blocks)
    classes = gather(features, core)
    plain, turned, degree = prep(tile_rows, tile_masks, row_blocks)
    degree = degree + swap_core(degree)
    degree = degree + swap_high(degree)
    own_degree = lax.dynamic_slice_in_dim(
        degree, (high * 2 + core) * (row_blocks // 4), row_blocks // 4, 0
    )
    scale = jnp.broadcast_to(
        lax.rsqrt(jnp.maximum(own_degree, 1.0)).reshape(rows, 1), (rows, width)
    )
    total = None
    for which in range(CLASSES):
        total = forward_class(which, meta, bounds, plain, classes[which], total, row_blocks)
    keep, give = total
    near = swap_core(give)
    far = swap_high(add(keep[1], near[1]))
    output, back, mean, weight = dense(
        features, self_weight, neigh_weight, cotangent, scale, keep, near, far
    )
    weight = lax.psum(weight, BOTH) * ((rows * lax.axis_size(BOTH)) ** (-0.5))
    mean_far = swap_high(mean)
    grads = (mean, mean_far, swap_core(mean), swap_core(mean_far))
    incoming = scatter(
        lambda which: backward_class(which, meta, bounds, turned, grads), core
    )
    grad_feat = (back + incoming).astype(jnp.bfloat16)
    return (output, grad_feat, weight[:width], weight[width:])


def solution(mesh):
    in_specs = (
        P(BOTH, None),
        P(),
        P(),
        P(BOTH),
        P(BOTH),
        P(BOTH, None, None),
        P(BOTH, None),
    )
    out_specs = (P(BOTH, None), P(BOTH, None), P(), P())
    return jax.shard_map(local, mesh=mesh, in_specs=in_specs, out_specs=out_specs, check_vma=False)
```

time: 1080 us -> 388 us (0.36)
  matrix products: 473 us -> 0 us
  waiting for transfers between devices: 391 us -> 167 us
  local copies, waits for them, and re-layouts: 160 us -> 16.6 us
  starting transfers between devices: 0.38 us -> 88.1 us
  Pallas kernels: 0 us -> 87 us
  other arithmetic: 35.6 us -> 12.9 us
    dot_general x96 -> x0, matrix products: 473 us -> none  [the longest x20 269 us: place_rows(): lax.dot_general(placer, low_part, contract_first, preferred_element_type=...]
    reduce_scatter x2 -> x0, waiting for transfers between devices: 201 us -> none  [the longest x1 176 us: local(): lax.psum_scatter(spread.astype(jnp.bfloat16), 'row', scatter_dimension=0,...]
    all_gather x2 -> x0, waiting for transfers between devices: 189 us -> none  [the longest x1 171 us: local(): gathered = lax.all_gather(features, 'row', axis=0, tiled=True)]
    psum x1, waiting for transfers between devices: 0.02 us -> 119 us  [local(): weight = lax.psum(weight, BOTH) * (rows * lax.axis_size(BOTH)) ** (-0.5)]
    while x80 -> x0, local copies, waits for them, and re-layouts: 90.8 us -> none
    ppermute x0 -> x55, starting transfers between devices: none -> 88.1 us  [move(): return lax.ppermute(value, BOTH, pairs(step))]
    pallas_call x0 -> x10, Pallas kernels: none -> 87 us  [the longest x4 34.7 us: forward_class(): pl.pallas_call(functools.partial(forward_kernel, which, first_call, last_...]
    ppermute x0 -> x55, waiting for transfers between devices: none -> 48.5 us  [move(): return lax.ppermute(value, BOTH, pairs(step))]
  transfers between devices with their start and end apart: 5 -> 56, of which waited for: 4 -> 16; matrix products, arithmetic and copies ran while one was open for 40% -> 5% of each run, Pallas kernels for 0% -> 19%
where the time goes in v1:
time: 388 us; the launch traced here: 387 us
  waiting for transfers between devices  167 us (43%)
  starting transfers between devices  88.1 us (23%)
  Pallas kernels  87 us (22%)
  local copies, waits for them, and re-layouts  16.6 us (4%)
  between operations  14.7 us (4%)
  other arithmetic  12.9 us (3%)
    psum x1, waiting for transfers between devices, local(): weight = lax.psum(weight, BOTH) * (rows * lax.axis_size(BOTH)) ** (-0.5)  119 us
    ppermute x55, starting transfers between devices, move(): return lax.ppermute(value, BOTH, pairs(step))  88.1 us
    ppermute x55, waiting for transfers between devices, move(): return lax.ppermute(value, BOTH, pairs(step))  48.5 us
    pallas_call x4, Pallas kernels, forward_class(): pl.pallas_call(functools.partial(forward_kernel, which, first_call, last_...  34.7 us
    pallas_call x4, Pallas kernels, backward_class(): pl.pallas_call(functools.partial(backward_kernel, which), in_specs=[smem,...  33.7 us
    pallas_call x1, Pallas kernels, prep(): pl.pallas_call(prep_kernel, grid=(slots // BLOCK_TILES,), in_specs=[pl.Bl...  17.2 us
    unnamed x40, local copies, waits for them, and re-layouts  9.65 us
  transfers between devices with their start and end apart: 56, of which 16 were waited for; matrix products, arithmetic and copies ran while one was open for 5% of the time, Pallas kernels for 19%

profile of v1, /device:TPU:0, one launch (start us, length us, event | category | flops | bytes accessed | tf_op | source)
XLA Modules:
  0.0 386.6 jit_solution(8217889880197731680)
XLA Ops:
  9.7 1.6 collective-permute-start.3
  11.3 1.7 collective-permute-start.4
  13.0 1.9 collective-permute-start.5
  14.9 1.9 collective-permute-start.11
  17.7 3.5 collective-permute-done.5
  21.4 3.1 collective-permute-start.8
  25.9 1.8 collective-permute-start.13
  28.7 5.2 %collective-permute-done.12 = bf16[2,256,256]{2,1,0:T(8,128)(2,1)S(1)} collective-permute-done((bf16[2,256,256]{2,1,0:T(8,128)(2,1)S(1)}, bf16[2,256,256]{2,1,0:T(8,128)(2,1)S(1)}, u32[]{:S(2)}, u32[]{:S(2)}) %collective-permute-start.12) | collective-permute-done | bytes 262176 | tf_op jit(solution)/shard_map/ppermute | solution.py:36
  35.2 5.7 %collective-permute-done.14 = bf16[2,256,256]{2,1,0:T(8,128)(2,1)S(1)} collective-permute-done((bf16[2,256,256]{2,1,0:T(8,128)(2,1)S(1)}, bf16[2,256,256]{2,1,0:T(8,128)(2,1)S(1)}, u32[]{:S(2)}, u32[]{:S(2)}) %collective-permute-start.14) | collective-permute-done | bytes 262176 | tf_op jit(solution)/shard_map/ppermute | solution.py:36
  41.5 2.1 collective-permute-start.15
  47.0 8.9 %collective-permute-done.17.refs_2_ = bf16[2,1024,256]{2,1,0:T(8,128)(2,1)S(1)} collective-permute-done((bf16[2,1024,256]{2,1,0:T(8,128)(2,1)S(1)}, bf16[2,1024,256]{2,1,0:T(8,128)(2,1)S(1)}, u32[]{:S(2)}, u32[]{:S(2)}) %collective-permute-start.17) | collective-permute-done | bytes 1048608 | tf_op jit(solution)/shard_map/ppermute | solution.py:36
  56.0 1.4 collective-permute-start.9
  62.0 2.7 collective-permute-start.21
  64.8 17.2 %prep.1 = (bf16[320,128,128]{2,1,0:T(8,128)(2,1)S(1)}, bf16[320,128,128]{2,1,0:T(8,128)(2,1)S(1)}, f32[16,128]{1,0:T(8,128)S(1)}) custom-call(s32[320]{0:T(512)S(1)} %copy-done.16, s32[320,128,128]{2,1,0:T(8,128)} %mask_ref.1), custom_call_target="tpu_custom_call" | custom-call | bytes 41943040 | tf_op jit(solution)/shard_map/prep/pallas_call | solution.py:82
  82.0 4.0 %copy-done = bf16[320,128,128]{2,1,0:T(8,128)(2,1)} copy-done((bf16[320,128,128]{2,1,0:T(8,128)(2,1)}, bf16[320,128,128]{2,1,0:T(8,128)(2,1)S(1)}, u32[]{:S(2)}) %copy-start) | copy-done | bytes 10485784
  86.7 13.3 %forward_class0.1.refs_4_ = f32[2176,256]{1,0:T(8,128)S(1)} custom-call(s32[352]{0:T(512)S(1)} %broadcast_add_fusion.meta_ref, s32[7]{0:T(128)S(1)} %pad_add_fusion.bounds_ref, bf16[320,128,128]{2,1,0:T(8,128)(2,1)S(1)} %get-tuple-element.30.masks_ref, bf16[2,1024,256]{2,1,0:T(8,128)(2,1)S(1)} %bitcast.101, bf16[1024,256]{1,0:T(8,128)(2,1)S(1)} %copy-done.10, ...), custom_call_target="tpu_custom_call" | custom-call | flops 2684354560 | bytes 8388608 | tf_op jit(solution)/shard_map/forward_class0/pallas_call | solution.py:196
  100.0 7.3 %forward_class1.1.refs_4_ = f32[2176,256]{1,0:T(8,128)S(1)} custom-call(s32[352]{0:T(512)S(1)} %broadcast_add_fusion.meta_ref, s32[7]{0:T(128)S(1)} %pad_add_fusion.bounds_ref, bf16[320,128,128]{2,1,0:T(8,128)(2,1)S(1)} %get-tuple-element.30.masks_ref, bf16[2,1024,256]{2,1,0:T(8,128)(2,1)S(1)} %collective-permute-done.6.refs_0_, ...), custom_call_target="tpu_custom_call" | custom-call | flops 2684354560 | bytes 8388608 | tf_op jit(solution)/shard_map/forward_class1/pallas_call | solution.py:196
  107.4 7.2 %forward_class2.1.refs_4_ = f32[2176,256]{1,0:T(8,128)S(1)} custom-call(s32[352]{0:T(512)S(1)} %broadcast_add_fusion.meta_ref, s32[7]{0:T(128)S(1)} %pad_add_fusion.bounds_ref, bf16[320,128,128]{2,1,0:T(8,128)(2,1)S(1)} %get-tuple-element.30.masks_ref, bf16[2,1024,256]{2,1,0:T(8,128)(2,1)S(1)} %collective-permute-done.15.refs_0_, ...), custom_call_target="tpu_custom_call" | custom-call | flops 2684354560 | bytes 8388608 | tf_op jit(solution)/shard_map/forward_class2/pallas_call | solution.py:196
  114.6 6.9 %forward_class3.1 = (bf16[2,512,256]{2,1,0:T(8,128)(2,1)S(1)}, bf16[2,512,256]{2,1,0:T(8,128)(2,1)S(1)}) custom-call(s32[352]{0:T(512)S(1)} %broadcast_add_fusion.meta_ref, s32[7]{0:T(128)S(1)} %pad_add_fusion.bounds_ref, bf16[320,128,128]{2,1,0:T(8,128)(2,1)S(1)} %get-tuple-element.30.masks_ref, bf16[1024,256]{1,0:T(8,128)(2,1)S(1)} %collective-permute-done.7.refs_0_, ...), custom_call_target="tpu_custom_call" | custom-call | flops 2684354560 | bytes 8388608 | tf_op jit(solution)/shard_map/forward_class3/pallas_call | solution.py:196
  121.6 1.9 collective-permute-done.26.near_ref
  123.6 4.0 %collective-permute-start.27 = (bf16[512,256]{1,0:T(8,128)(2,1)S(1)}, bf16[512,256]{1,0:T(8,128)(2,1)S(1)}, u32[]{:S(2)}, u32[]{:S(2)}) collective-permute-start(bf16[512,256]{1,0:T(8,128)(2,1)S(1)} %fusion.12), channel_id=1, source_target_pairs={{0,2},{1,3},{2,0},{3,1},{4,6},{5,7},{6,4},{7,5},{8,10},{9,11},{10,... | collective-permute-start | bytes 786440 | tf_op jit(solution)/shard_map/ppermute | solution.py:36
  128.9 5.7 %collective-permute-done.1 = f32[16,128]{1,0:T(8,128)S(1)} collective-permute-done((f32[16,128]{1,0:T(8,128)S(1)}, f32[16,128]{1,0:T(8,128)S(1)}, u32[]{:S(2)}, u32[]{:S(2)}) %collective-permute-start.1) | collective-permute-done | bytes 8224 | tf_op jit(solution)/shard_map/ppermute | solution.py:36
  134.8 1.6 dense.1
  136.3 3.2 collective-permute-start.28
  139.6 6.3 %collective-permute-done.28.far = bf16[512,256]{1,0:T(8,128)(2,1)S(1)} collective-permute-done((bf16[512,256]{1,0:T(8,128)(2,1)S(1)}, bf16[512,256]{1,0:T(8,128)(2,1)S(1)}, u32[]{:S(2)}, u32[]{:S(2)}) %collective-permute-start.28) | collective-permute-done | bytes 262176 | tf_op jit(solution)/shard_map/ppermute | solution.py:36
  145.8 1.5 collective-permute-done.30.cross
  147.4 4.0 %copy-done.1 = bf16[320,128,128]{2,1,0:T(8,128)(2,1)S(1)} copy-done((bf16[320,128,128]{2,1,0:T(8,128)(2,1)S(1)}, bf16[320,128,128]{2,1,0:T(8,128)(2,1)}, u32[]{:S(2)}) %copy-start.1) | copy-done | bytes 10485784
  151.4 6.7 %backward_class3.1 = (bf16[1024,256]{1,0:T(8,128)(2,1)S(1)}, bf16[1024,256]{1,0:T(8,128)(2,1)S(1)}, bf16[1024,256]{1,0:T(8,128)(2,1)S(1)}, bf16[1024,256]{1,0:T(8,128)(2,1)S(1)}) custom-call(s32[352]{0:T(512)S(1)} %broadcast_add_fusion.meta_ref, s32[7]{0:T(128)S(1)} %pad_add_fusion.bounds_ref, bf16[320,128,128]{2,1,0:T(8,128)(2,1)S(1)} %copy-done.1, ...), custom_call_target="tpu_custom_call" | custom-call | flops 2684354560 | bytes 8388608 | tf_op jit(solution)/shard_map/backward_class3/pallas_call | solution.py:249
  158.1 2.3 collective-permute-start.47
  161.2 6.7 %backward_class2.1 = (bf16[1024,256]{1,0:T(8,128)(2,1)S(1)}, bf16[1024,256]{1,0:T(8,128)(2,1)S(1)}, bf16[1024,256]{1,0:T(8,128)(2,1)S(1)}, bf16[1024,256]{1,0:T(8,128)(2,1)S(1)}) custom-call(s32[352]{0:T(512)S(1)} %broadcast_add_fusion.meta_ref, s32[7]{0:T(128)S(1)} %pad_add_fusion.bounds_ref, bf16[320,128,128]{2,1,0:T(8,128)(2,1)S(1)} %copy-done.1, ...), custom_call_target="tpu_custom_call" | custom-call | flops 2684354560 | bytes 8388608 | tf_op jit(solution)/shard_map/backward_class2/pallas_call | solution.py:249
  168.7 6.7 %backward_class1.1 = (bf16[1024,256]{1,0:T(8,128)(2,1)S(1)}, bf16[1024,256]{1,0:T(8,128)(2,1)S(1)}, bf16[1024,256]{1,0:T(8,128)(2,1)S(1)}, bf16[1024,256]{1,0:T(8,128)(2,1)S(1)}) custom-call(s32[352]{0:T(512)S(1)} %broadcast_add_fusion.meta_ref, s32[7]{0:T(128)S(1)} %pad_add_fusion.bounds_ref, bf16[320,128,128]{2,1,0:T(8,128)(2,1)S(1)} %copy-done.1, ...), custom_call_target="tpu_custom_call" | custom-call | flops 2684354560 | bytes 8388608 | tf_op jit(solution)/shard_map/backward_class1/pallas_call | solution.py:249
  175.4 6.5 %collective-permute-start.48 = (bf16[1024,256]{1,0:T(8,128)(2,1)S(1)}, bf16[1024,256]{1,0:T(8,128)(2,1)S(1)}, u32[]{:S(2)}, u32[]{:S(2)}) collective-permute-start(bf16[1024,256]{1,0:T(8,128)(2,1)S(1)} %collective-permute-done.47), channel_id=1, source_target_pairs={{0,12},{1,49},{2,14},{3,51},{4,0},{5,53},{6,2},{7,55},{8,4},{9,57}... | collective-permute-start | bytes 1572872 | tf_op jit(solution)/shard_map/ppermute | solution.py:36
  181.9 13.6 %backward_class0.1 = (bf16[1024,256]{1,0:T(8,128)(2,1)S(1)}, bf16[1024,256]{1,0:T(8,128)(2,1)S(1)}, bf16[1024,256]{1,0:T(8,128)(2,1)S(1)}, bf16[1024,256]{1,0:T(8,128)(2,1)S(1)}) custom-call(s32[352]{0:T(512)S(1)} %broadcast_add_fusion.meta_ref, s32[7]{0:T(128)S(1)} %pad_add_fusion.bounds_ref, bf16[320,128,128]{2,1,0:T(8,128)(2,1)S(1)} %copy-done.1, ...), custom_call_target="tpu_custom_call" | custom-call | flops 2684354560 | bytes 8388608 | tf_op jit(solution)/shard_map/backward_class0/pallas_call | solution.py:249
  195.7 3.1 collective-permute-start.33
  199.9 5.1 %collective-permute-start.45 = (bf16[2,1024,256]{2,1,0:T(8,128)(2,1)}, bf16[2,1024,256]{2,1,0:T(8,128)(2,1)}, u32[]{:S(2)}, u32[]{:S(2)}) collective-permute-start(bf16[2,1024,256]{2,1,0:T(8,128)(2,1)} %pad_maximum_fusion.4), channel_id=1, source_target_pairs={{0,4},{1,17},{2,6},{3,19},{4,8},{5,21},{6,10},{7,23},{8,12},{9,25}... | collective-permute-start | bytes 3145736 | tf_op jit(solution)/shard_map/ppermute | solution.py:36
  206.4 6.7 %collective-permute-start.42 = (bf16[1024,256]{1,0:T(8,128)(2,1)S(1)}, bf16[1024,256]{1,0:T(8,128)(2,1)S(1)}, u32[]{:S(2)}, u32[]{:S(2)}) collective-permute-start(bf16[1024,256]{1,0:T(8,128)(2,1)S(1)} %get-tuple-element.46), channel_id=1, source_target_pairs={{0,1},{1,0},{2,3},{3,2},{4,5},{5,4},{6,7},{7,6},{8,9},{9,8},{10,11... | collective-permute-start | bytes 1572872 | tf_op jit(solution)/shard_map/ppermute | solution.py:36
  214.1 1.8 collective-permute-start.34
  217.2 1.5 collective-permute-start.38
  218.7 3.2 collective-permute-start.31
  221.8 3.7 collective-permute-done.49
  225.5 2.0 add_convert_fusion
  227.5 8.6 %collective-permute-start.50 = (bf16[2,256,256]{2,1,0:T(8,128)(2,1)S(1)}, bf16[2,256,256]{2,1,0:T(8,128)(2,1)S(1)}, u32[]{:S(2)}, u32[]{:S(2)}) collective-permute-start(bf16[2,256,256]{2,1,0:T(8,128)(2,1)S(1)} %get-tuple-element.59), channel_id=1, source_target_pairs={{0,48},{1,13},{2,50},{3,15},{4,52},{5,1},{6,54},{7,3},{8,56},{9,5}... | collective-permute-start | bytes 786440 | tf_op jit(solution)/shard_map/ppermute | solution.py:36
  236.1 1.6 collective-permute-start.52
  237.7 2.0 collective-permute-done.38
  239.7 1.9 add_convert_fusion.1
  242.5 11.9 %collective-permute-start.39 = (bf16[2,256,256]{2,1,0:T(8,128)(2,1)}, bf16[2,256,256]{2,1,0:T(8,128)(2,1)S(1)}, u32[]{:S(2)}, u32[]{:S(2)}) collective-permute-start(bf16[2,256,256]{2,1,0:T(8,128)(2,1)} %get-tuple-element.56), channel_id=1, source_target_pairs={{0,48},{1,13},{2,50},{3,15},{4,52},{5,1},{6,54},{7,3},{8,56},{9,5}... | collective-permute-start | bytes 786440 | tf_op jit(solution)/shard_map/ppermute | solution.py:36
  254.4 1.5 collective-permute-start.41
  257.3 118.7 %all-reduce.2.cloned.1.call-done = f32[512,256]{1,0:T(8,128)} async-done(((f32[512,256]{1,0:T(8,128)}), f32[512,256]{1,0:T(8,128)}) %all-reduce.2.cloned.1.call-update) | async-done | bytes 524304 | tf_op jit(solution)/shard_map/psum | solution.py:429
  (161 shorter events, 30.9 us)
Async XLA Ops:
  7.2 368.9 %all-reduce.2.cloned.1.call-start = ((), (), s32[]{:S(2)}) async-start(), calls=%async_computation | async-start | bytes 1048576 | tf_op jit(solution)/shard_map/psum | solution.py:429
  9.7 7.8 %collective-permute-start.3 = (bf16[2,256,256]{2,1,0:T(8,128)(2,1)S(1)}, bf16[2,256,256]{2,1,0:T(8,128)(2,1)S(1)}, u32[]{:S(2)}, u32[]{:S(2)}) collective-permute-start(bf16[2,256,256]{2,1,0:T(8,128)(2,1)S(1)} %get-tuple-element.71), channel_id=1, source_target_pairs={{0,16},{1,5},{2,18},{3,7},{4,20},{5,9},{6,22},{7,11},{8,24},{9,13}... | collective-permute-start | bytes 786440 | tf_op jit(solution)/shard_map/ppermute | solution.py:36
  11.3 6.4 %collective-permute-start.4 = (bf16[2,256,256]{2,1,0:T(8,128)(2,1)S(1)}, bf16[2,256,256]{2,1,0:T(8,128)(2,1)S(1)}, u32[]{:S(2)}, u32[]{:S(2)}) collective-permute-start(bf16[2,256,256]{2,1,0:T(8,128)(2,1)S(1)} %get-tuple-element.71), channel_id=1, source_target_pairs={{0,48},{1,13},{2,50},{3,15},{4,52},{5,1},{6,54},{7,3},{8,56},{9,5}... | collective-permute-start | bytes 786440 | tf_op jit(solution)/shard_map/ppermute | solution.py:36
  13.0 8.2 %collective-permute-start.5 = (bf16[2,256,256]{2,1,0:T(8,128)(2,1)S(1)}, bf16[2,256,256]{2,1,0:T(8,128)(2,1)S(1)}, u32[]{:S(2)}, u32[]{:S(2)}) collective-permute-start(bf16[2,256,256]{2,1,0:T(8,128)(2,1)S(1)} %get-tuple-element.71), channel_id=1, source_target_pairs={{0,32},{1,9},{2,34},{3,11},{4,36},{5,13},{6,38},{7,15},{8,40},{9,1... | collective-permute-start | bytes 786440 | tf_op jit(solution)/shard_map/ppermute | solution.py:36
  14.9 9.6 %collective-permute-start.11 = (bf16[2,256,256]{2,1,0:T(8,128)(2,1)S(1)}, bf16[2,256,256]{2,1,0:T(8,128)(2,1)S(1)}, u32[]{:S(2)}, u32[]{:S(2)}) collective-permute-start(bf16[2,256,256]{2,1,0:T(8,128)(2,1)S(1)} %get-tuple-element.71), channel_id=1, source_target_pairs={{0,64},{1,65},{2,66},{3,67},{4,68},{5,69},{6,70},{7,71},{8,72},{9,... | collective-permute-start | bytes 786440 | tf_op jit(solution)/shard_map/ppermute | solution.py:36
  21.4 22.4 %collective-permute-start.8 = (bf16[2,1024,256]{2,1,0:T(8,128)(2,1)S(1)}, bf16[2,1024,256]{2,1,0:T(8,128)(2,1)S(1)}, u32[]{:S(2)}, u32[]{:S(2)}) collective-permute-start(bf16[2,1024,256]{2,1,0:T(8,128)(2,1)S(1)} %bitcast.99), channel_id=1, source_target_pairs={{0,12},{1,49},{2,14},{3,51},{4,0},{5,53},{6,2},{7,55},{8,4},{9,57}... | collective-permute-start | bytes 3145736 | tf_op jit(solution)/shard_map/ppermute | solution.py:36
  24.5 9.4 %collective-permute-start.12 = (bf16[2,256,256]{2,1,0:T(8,128)(2,1)S(1)}, bf16[2,256,256]{2,1,0:T(8,128)(2,1)S(1)}, u32[]{:S(2)}, u32[]{:S(2)}) collective-permute-start(bf16[2,256,256]{2,1,0:T(8,128)(2,1)S(1)} %collective-permute-done.11), channel_id=1, source_target_pairs={{0,16},{1,5},{2,18},{3,7},{4,20},{5,9},{6,22},{7,11},{8,24},{9,13}... | collective-permute-start | bytes 786440 | tf_op jit(solution)/shard_map/ppermute | solution.py:36
  25.9 9.2 %collective-permute-start.13 = (bf16[2,256,256]{2,1,0:T(8,128)(2,1)S(1)}, bf16[2,256,256]{2,1,0:T(8,128)(2,1)S(1)}, u32[]{:S(2)}, u32[]{:S(2)}) collective-permute-start(bf16[2,256,256]{2,1,0:T(8,128)(2,1)S(1)} %collective-permute-done.11), channel_id=1, source_target_pairs={{0,48},{1,13},{2,50},{3,15},{4,52},{5,1},{6,54},{7,3},{8,56},{9,5}... | collective-permute-start | bytes 786440 | tf_op jit(solution)/shard_map/ppermute | solution.py:36
  27.8 13.1 %collective-permute-start.14 = (bf16[2,256,256]{2,1,0:T(8,128)(2,1)S(1)}, bf16[2,256,256]{2,1,0:T(8,128)(2,1)S(1)}, u32[]{:S(2)}, u32[]{:S(2)}) collective-permute-start(bf16[2,256,256]{2,1,0:T(8,128)(2,1)S(1)} %collective-permute-done.11), channel_id=1, source_target_pairs={{0,32},{1,9},{2,34},{3,11},{4,36},{5,13},{6,38},{7,15},{8,40},{9,1... | collective-permute-start | bytes 786440 | tf_op jit(solution)/shard_map/ppermute | solution.py:36
  28.4 17.0 %collective-permute-start.6 = (bf16[2,1024,256]{2,1,0:T(8,128)(2,1)S(1)}, bf16[2,1024,256]{2,1,0:T(8,128)(2,1)S(1)}, u32[]{:S(2)}, u32[]{:S(2)}) collective-permute-start(bf16[2,1024,256]{2,1,0:T(8,128)(2,1)S(1)} %bitcast.100), channel_id=1, source_target_pairs={{0,4},{1,17},{2,6},{3,19},{4,8},{5,21},{6,10},{7,23},{8,12},{9,25}... | collective-permute-start | bytes 3145736 | tf_op jit(solution)/shard_map/ppermute | solution.py:36
  41.1 14.9 %collective-permute-start.17 = (bf16[2,1024,256]{2,1,0:T(8,128)(2,1)S(1)}, bf16[2,1024,256]{2,1,0:T(8,128)(2,1)S(1)}, u32[]{:S(2)}, u32[]{:S(2)}) collective-permute-start(bf16[2,1024,256]{2,1,0:T(8,128)(2,1)S(1)} %bitcast.102), channel_id=1, source_target_pairs={{0,12},{1,49},{2,14},{3,51},{4,0},{5,53},{6,2},{7,55},{8,4},{9,57}... | collective-permute-start | bytes 3145736 | tf_op jit(solution)/shard_map/ppermute | solution.py:36
  41.5 16.8 %collective-permute-start.15 = (bf16[2,1024,256]{2,1,0:T(8,128)(2,1)S(1)}, bf16[2,1024,256]{2,1,0:T(8,128)(2,1)S(1)}, u32[]{:S(2)}, u32[]{:S(2)}) collective-permute-start(bf16[2,1024,256]{2,1,0:T(8,128)(2,1)S(1)} %bitcast.103), channel_id=1, source_target_pairs={{0,4},{1,17},{2,6},{3,19},{4,8},{5,21},{6,10},{7,23},{8,12},{9,25}... | collective-permute-start | bytes 3145736 | tf_op jit(solution)/shard_map/ppermute | solution.py:36
  43.7 15.7 %collective-permute-start.24 = (bf16[1024,256]{1,0:T(8,128)(2,1)S(1)}, bf16[1024,256]{1,0:T(8,128)(2,1)S(1)}, u32[]{:S(2)}, u32[]{:S(2)}) collective-permute-start(bf16[1024,256]{1,0:T(8,128)(2,1)S(1)} %bitcast.114), channel_id=1, source_target_pairs={{0,1},{1,0},{2,3},{3,2},{4,5},{5,4},{6,7},{7,6},{8,9},{9,8},{10,11... | collective-permute-start | bytes 1572872 | tf_op jit(solution)/shard_map/ppermute | solution.py:36
  43.9 16.8 %collective-permute-start.25 = (bf16[1024,256]{1,0:T(8,128)(2,1)S(1)}, bf16[1024,256]{1,0:T(8,128)(2,1)S(1)}, u32[]{:S(2)}, u32[]{:S(2)}) collective-permute-start(bf16[1024,256]{1,0:T(8,128)(2,1)S(1)} %bitcast.113), channel_id=1, source_target_pairs={{0,1},{1,0},{2,3},{3,2},{4,5},{5,4},{6,7},{7,6},{8,9},{9,8},{10,11... | collective-permute-start | bytes 1572872 | tf_op jit(solution)/shard_map/ppermute | solution.py:36
  45.3 40.6 %collective-permute-start.23 = (bf16[1024,256]{1,0:T(8,128)(2,1)}, bf16[1024,256]{1,0:T(8,128)(2,1)}, u32[]{:S(2)}, u32[]{:S(2)}) collective-permute-start(bf16[1024,256]{1,0:T(8,128)(2,1)} %slice_bitcast_fusion.4), channel_id=1, source_target_pairs={{0,1},{1,0},{2,3},{3,2},{4,5},{5,4},{6,7},{7,6},{8,9},{9,8},{10,11... | collective-permute-start | bytes 1572872 | tf_op jit(solution)/shard_map/ppermute | solution.py:36
  56.0 30.1 %collective-permute-start.9 = (bf16[1024,256]{1,0:T(8,128)(2,1)}, bf16[1024,256]{1,0:T(8,128)(2,1)}, u32[]{:S(2)}, u32[]{:S(2)}) collective-permute-start(bf16[1024,256]{1,0:T(8,128)(2,1)} %slice_bitcast_fusion.4), channel_id=1, source_target_pairs={{0,12},{1,49},{2,14},{3,51},{4,0},{5,53},{6,2},{7,55},{8,4},{9,57}... | collective-permute-start | bytes 1572872 | tf_op jit(solution)/shard_map/ppermute | solution.py:36
  60.2 25.9 %collective-permute-start.20 = (bf16[1024,256]{1,0:T(8,128)(2,1)}, bf16[1024,256]{1,0:T(8,128)(2,1)}, u32[]{:S(2)}, u32[]{:S(2)}) collective-permute-start(bf16[1024,256]{1,0:T(8,128)(2,1)} %get-tuple-element.64), channel_id=1, source_target_pairs={{0,1},{1,0},{2,3},{3,2},{4,5},{5,4},{6,7},{7,6},{8,9},{9,8},{10,11... | collective-permute-start | bytes 1572872 | tf_op jit(solution)/shard_map/ppermute | solution.py:36
  61.5 25.0 %collective-permute-start.18 = (bf16[1024,256]{1,0:T(8,128)(2,1)}, bf16[1024,256]{1,0:T(8,128)(2,1)}, u32[]{:S(2)}, u32[]{:S(2)}) collective-permute-start(bf16[1024,256]{1,0:T(8,128)(2,1)} %slice_bitcast_fusion.2), channel_id=1, source_target_pairs={{0,12},{1,49},{2,14},{3,51},{4,0},{5,53},{6,2},{7,55},{8,4},{9,57}... | collective-permute-start | bytes 1572872 | tf_op jit(solution)/shard_map/ppermute | solution.py:36
  62.0 45.4 %collective-permute-start.21 = (bf16[1024,256]{1,0:T(8,128)(2,1)}, bf16[1024,256]{1,0:T(8,128)(2,1)S(1)}, u32[]{:S(2)}, u32[]{:S(2)}) collective-permute-start(bf16[1024,256]{1,0:T(8,128)(2,1)} %slice_bitcast_fusion.2), channel_id=1, source_target_pairs={{0,1},{1,0},{2,3},{3,2},{4,5},{5,4},{6,7},{7,6},{8,9},{9,8},{10,11... | collective-permute-start | bytes 1572872 | tf_op jit(solution)/shard_map/ppermute | solution.py:36
  86.0 28.6 %collective-permute-start.7 = (bf16[1024,256]{1,0:T(8,128)(2,1)S(1)}, bf16[1024,256]{1,0:T(8,128)(2,1)S(1)}, u32[]{:S(2)}, u32[]{:S(2)}) collective-permute-start(bf16[1024,256]{1,0:T(8,128)(2,1)S(1)} %copy-done.17), channel_id=1, source_target_pairs={{0,4},{1,17},{2,6},{3,19},{4,8},{5,21},{6,10},{7,23},{8,12},{9,25}... | collective-permute-start | bytes 1572872 | tf_op jit(solution)/shard_map/ppermute | solution.py:36
  86.0 28.6 %collective-permute-start.16 = (bf16[1024,256]{1,0:T(8,128)(2,1)S(1)}, bf16[1024,256]{1,0:T(8,128)(2,1)S(1)}, u32[]{:S(2)}, u32[]{:S(2)}) collective-permute-start(bf16[1024,256]{1,0:T(8,128)(2,1)S(1)} %copy-done.18), channel_id=1, source_target_pairs={{0,4},{1,17},{2,6},{3,19},{4,8},{5,21},{6,10},{7,23},{8,12},{9,25}... | collective-permute-start | bytes 1572872 | tf_op jit(solution)/shard_map/ppermute | solution.py:36
  86.1 28.5 %collective-permute-start.10 = (bf16[1024,256]{1,0:T(8,128)(2,1)}, bf16[1024,256]{1,0:T(8,128)(2,1)S(1)}, u32[]{:S(2)}, u32[]{:S(2)}) collective-permute-start(bf16[1024,256]{1,0:T(8,128)(2,1)} %collective-permute-done.9), channel_id=1, source_target_pairs={{0,1},{1,0},{2,3},{3,2},{4,5},{5,4},{6,7},{7,6},{8,9},{9,8},{10,11... | collective-permute-start | bytes 1572872 | tf_op jit(solution)/shard_map/ppermute | solution.py:36
  86.5 28.1 %collective-permute-start.19 = (bf16[1024,256]{1,0:T(8,128)(2,1)}, bf16[1024,256]{1,0:T(8,128)(2,1)S(1)}, u32[]{:S(2)}, u32[]{:S(2)}) collective-permute-start(bf16[1024,256]{1,0:T(8,128)(2,1)} %collective-permute-done.18), channel_id=1, source_target_pairs={{0,1},{1,0},{2,3},{3,2},{4,5},{5,4},{6,7},{7,6},{8,9},{9,8},{10,11... | collective-permute-start | bytes 1572872 | tf_op jit(solution)/shard_map/ppermute | solution.py:36
  123.6 11.0 %collective-permute-start.27 = (bf16[512,256]{1,0:T(8,128)(2,1)S(1)}, bf16[512,256]{1,0:T(8,128)(2,1)S(1)}, u32[]{:S(2)}, u32[]{:S(2)}) collective-permute-start(bf16[512,256]{1,0:T(8,128)(2,1)S(1)} %fusion.12), channel_id=1, source_target_pairs={{0,2},{1,3},{2,0},{3,1},{4,6},{5,7},{6,4},{7,5},{8,10},{9,11},{10,... | collective-permute-start | bytes 786440 | tf_op jit(solution)/shard_map/ppermute | solution.py:36
  136.3 9.5 %collective-permute-start.28 = (bf16[512,256]{1,0:T(8,128)(2,1)S(1)}, bf16[512,256]{1,0:T(8,128)(2,1)S(1)}, u32[]{:S(2)}, u32[]{:S(2)}) collective-permute-start(bf16[512,256]{1,0:T(8,128)(2,1)S(1)} %get-tuple-element.36.own), channel_id=1, source_target_pairs={{0,2},{1,3},{2,0},{3,1},{4,6},{5,7},{6,4},{7,5},{8,10},{9,11},{10,... | collective-permute-start | bytes 786440 | tf_op jit(solution)/shard_map/ppermute | solution.py:36
  158.1 17.3 %collective-permute-start.47 = (bf16[1024,256]{1,0:T(8,128)(2,1)S(1)}, bf16[1024,256]{1,0:T(8,128)(2,1)S(1)}, u32[]{:S(2)}, u32[]{:S(2)}) collective-permute-start(bf16[1024,256]{1,0:T(8,128)(2,1)S(1)} %get-tuple-element.52), channel_id=1, source_target_pairs={{0,1},{1,0},{2,3},{3,2},{4,5},{5,4},{6,7},{7,6},{8,9},{9,8},{10,11... | collective-permute-start | bytes 1572872 | tf_op jit(solution)/shard_map/ppermute | solution.py:36
  160.3 39.5 %collective-permute-start.36 = (bf16[1024,256]{1,0:T(8,128)(2,1)S(1)}, bf16[1024,256]{1,0:T(8,128)(2,1)S(1)}, u32[]{:S(2)}, u32[]{:S(2)}) collective-permute-start(bf16[1024,256]{1,0:T(8,128)(2,1)S(1)} %get-tuple-element.44), channel_id=1, source_target_pairs={{0,1},{1,0},{2,3},{3,2},{4,5},{5,4},{6,7},{7,6},{8,9},{9,8},{10,11... | collective-permute-start | bytes 1572872 | tf_op jit(solution)/shard_map/ppermute | solution.py:36
  160.4 35.0 %collective-permute-start.43 = (bf16[1024,256]{1,0:T(8,128)(2,1)S(1)}, bf16[1024,256]{1,0:T(8,128)(2,1)S(1)}, u32[]{:S(2)}, u32[]{:S(2)}) collective-permute-start(bf16[1024,256]{1,0:T(8,128)(2,1)S(1)} %get-tuple-element.48), channel_id=1, source_target_pairs={{0,4},{1,17},{2,6},{3,19},{4,8},{5,21},{6,10},{7,23},{8,12},{9,25}... | collective-permute-start | bytes 1572872 | tf_op jit(solution)/shard_map/ppermute | solution.py:36
  167.9 27.8 %collective-permute-start.44 = (bf16[1024,256]{1,0:T(8,128)(2,1)S(1)}, bf16[1024,256]{1,0:T(8,128)(2,1)S(1)}, u32[]{:S(2)}, u32[]{:S(2)}) collective-permute-start(bf16[1024,256]{1,0:T(8,128)(2,1)S(1)} %get-tuple-element.49), channel_id=1, source_target_pairs={{0,1},{1,0},{2,3},{3,2},{4,5},{5,4},{6,7},{7,6},{8,9},{9,8},{10,11... | collective-permute-start | bytes 1572872 | tf_op jit(solution)/shard_map/ppermute | solution.py:36
  168.6 31.3 %collective-permute-start.46 = (bf16[1024,256]{1,0:T(8,128)(2,1)S(1)}, bf16[1024,256]{1,0:T(8,128)(2,1)S(1)}, u32[]{:S(2)}, u32[]{:S(2)}) collective-permute-start(bf16[1024,256]{1,0:T(8,128)(2,1)S(1)} %get-tuple-element.51), channel_id=1, source_target_pairs={{0,1},{1,0},{2,3},{3,2},{4,5},{5,4},{6,7},{7,6},{8,9},{9,8},{10,11... | collective-permute-start | bytes 1572872 | tf_op jit(solution)/shard_map/ppermute | solution.py:36
  175.4 29.6 %collective-permute-start.48 = (bf16[1024,256]{1,0:T(8,128)(2,1)S(1)}, bf16[1024,256]{1,0:T(8,128)(2,1)S(1)}, u32[]{:S(2)}, u32[]{:S(2)}) collective-permute-start(bf16[1024,256]{1,0:T(8,128)(2,1)S(1)} %collective-permute-done.47), channel_id=1, source_target_pairs={{0,12},{1,49},{2,14},{3,51},{4,0},{5,53},{6,2},{7,55},{8,4},{9,57}... | collective-permute-start | bytes 1572872 | tf_op jit(solution)/shard_map/ppermute | solution.py:36
  195.4 10.8 %collective-permute-start.32 = (bf16[1024,256]{1,0:T(8,128)(2,1)S(1)}, bf16[1024,256]{1,0:T(8,128)(2,1)S(1)}, u32[]{:S(2)}, u32[]{:S(2)}) collective-permute-start(bf16[1024,256]{1,0:T(8,128)(2,1)S(1)} %get-tuple-element.40), channel_id=1, source_target_pairs={{0,4},{1,17},{2,6},{3,19},{4,8},{5,21},{6,10},{7,23},{8,12},{9,25}... | collective-permute-start | bytes 1572872 | tf_op jit(solution)/shard_map/ppermute | solution.py:36
  195.7 10.7 %collective-permute-start.33 = (bf16[1024,256]{1,0:T(8,128)(2,1)S(1)}, bf16[1024,256]{1,0:T(8,128)(2,1)S(1)}, u32[]{:S(2)}, u32[]{:S(2)}) collective-permute-start(bf16[1024,256]{1,0:T(8,128)(2,1)S(1)} %get-tuple-element.41), channel_id=1, source_target_pairs={{0,1},{1,0},{2,3},{3,2},{4,5},{5,4},{6,7},{7,6},{8,9},{9,8},{10,11... | collective-permute-start | bytes 1572872 | tf_op jit(solution)/shard_map/ppermute | solution.py:36
  199.8 14.3 %collective-permute-start.35 = (bf16[1024,256]{1,0:T(8,128)(2,1)S(1)}, bf16[1024,256]{1,0:T(8,128)(2,1)S(1)}, u32[]{:S(2)}, u32[]{:S(2)}) collective-permute-start(bf16[1024,256]{1,0:T(8,128)(2,1)S(1)} %get-tuple-element.43), channel_id=1, source_target_pairs={{0,1},{1,0},{2,3},{3,2},{4,5},{5,4},{6,7},{7,6},{8,9},{9,8},{10,11... | collective-permute-start | bytes 1572872 | tf_op jit(solution)/shard_map/ppermute | solution.py:36
  199.9 21.9 %collective-permute-start.45 = (bf16[2,1024,256]{2,1,0:T(8,128)(2,1)}, bf16[2,1024,256]{2,1,0:T(8,128)(2,1)}, u32[]{:S(2)}, u32[]{:S(2)}) collective-permute-start(bf16[2,1024,256]{2,1,0:T(8,128)(2,1)} %pad_maximum_fusion.4), channel_id=1, source_target_pairs={{0,4},{1,17},{2,6},{3,19},{4,8},{5,21},{6,10},{7,23},{8,12},{9,25}... | collective-permute-start | bytes 3145736 | tf_op jit(solution)/shard_map/ppermute | solution.py:36
  205.0 10.9 %collective-permute-start.37 = (bf16[1024,256]{1,0:T(8,128)(2,1)S(1)}, bf16[1024,256]{1,0:T(8,128)(2,1)S(1)}, u32[]{:S(2)}, u32[]{:S(2)}) collective-permute-start(bf16[1024,256]{1,0:T(8,128)(2,1)S(1)} %collective-permute-done.36), channel_id=1, source_target_pairs={{0,12},{1,49},{2,14},{3,51},{4,0},{5,53},{6,2},{7,55},{8,4},{9,57}... | collective-permute-start | bytes 1572872 | tf_op jit(solution)/shard_map/ppermute | solution.py:36
  206.2 19.3 %collective-permute-start.49 = (bf16[2,1024,256]{2,1,0:T(8,128)(2,1)}, bf16[2,1024,256]{2,1,0:T(8,128)(2,1)}, u32[]{:S(2)}, u32[]{:S(2)}) collective-permute-start(bf16[2,1024,256]{2,1,0:T(8,128)(2,1)} %pad_maximum_fusion.5), channel_id=1, source_target_pairs={{0,12},{1,49},{2,14},{3,51},{4,0},{5,53},{6,2},{7,55},{8,4},{9,57}... | collective-permute-start | bytes 3145736 | tf_op jit(solution)/shard_map/ppermute | solution.py:36
  206.4 12.3 %collective-permute-start.42 = (bf16[1024,256]{1,0:T(8,128)(2,1)S(1)}, bf16[1024,256]{1,0:T(8,128)(2,1)S(1)}, u32[]{:S(2)}, u32[]{:S(2)}) collective-permute-start(bf16[1024,256]{1,0:T(8,128)(2,1)S(1)} %get-tuple-element.46), channel_id=1, source_target_pairs={{0,1},{1,0},{2,3},{3,2},{4,5},{5,4},{6,7},{7,6},{8,9},{9,8},{10,11... | collective-permute-start | bytes 1572872 | tf_op jit(solution)/shard_map/ppermute | solution.py:36
  214.1 23.6 %collective-permute-start.34 = (bf16[2,1024,256]{2,1,0:T(8,128)(2,1)}, bf16[2,1024,256]{2,1,0:T(8,128)(2,1)}, u32[]{:S(2)}, u32[]{:S(2)}) collective-permute-start(bf16[2,1024,256]{2,1,0:T(8,128)(2,1)} %pad_maximum_fusion.2), channel_id=1, source_target_pairs={{0,4},{1,17},{2,6},{3,19},{4,8},{5,21},{6,10},{7,23},{8,12},{9,25}... | collective-permute-start | bytes 3145736 | tf_op jit(solution)/shard_map/ppermute | solution.py:36
  217.2 22.5 %collective-permute-start.38 = (bf16[2,1024,256]{2,1,0:T(8,128)(2,1)}, bf16[2,1024,256]{2,1,0:T(8,128)(2,1)}, u32[]{:S(2)}, u32[]{:S(2)}) collective-permute-start(bf16[2,1024,256]{2,1,0:T(8,128)(2,1)} %pad_maximum_fusion.3), channel_id=1, source_target_pairs={{0,12},{1,49},{2,14},{3,51},{4,0},{5,53},{6,2},{7,55},{8,4},{9,57}... | collective-permute-start | bytes 3145736 | tf_op jit(solution)/shard_map/ppermute | solution.py:36
  218.7 17.4 %collective-permute-start.31 = (bf16[1024,256]{1,0:T(8,128)(2,1)S(1)}, bf16[1024,256]{1,0:T(8,128)(2,1)S(1)}, u32[]{:S(2)}, u32[]{:S(2)}) collective-permute-start(bf16[1024,256]{1,0:T(8,128)(2,1)S(1)} %get-tuple-element.38), channel_id=1, source_target_pairs={{0,1},{1,0},{2,3},{3,2},{4,5},{5,4},{6,7},{7,6},{8,9},{9,8},{10,11... | collective-permute-start | bytes 1572872 | tf_op jit(solution)/shard_map/ppermute | solution.py:36
  227.5 26.9 %collective-permute-start.50 = (bf16[2,256,256]{2,1,0:T(8,128)(2,1)S(1)}, bf16[2,256,256]{2,1,0:T(8,128)(2,1)S(1)}, u32[]{:S(2)}, u32[]{:S(2)}) collective-permute-start(bf16[2,256,256]{2,1,0:T(8,128)(2,1)S(1)} %get-tuple-element.59), channel_id=1, source_target_pairs={{0,48},{1,13},{2,50},{3,15},{4,52},{5,1},{6,54},{7,3},{8,56},{9,5}... | collective-permute-start | bytes 786440 | tf_op jit(solution)/shard_map/ppermute | solution.py:36
  236.1 19.8 %collective-permute-start.51 = (bf16[2,256,256]{2,1,0:T(8,128)(2,1)S(1)}, bf16[2,256,256]{2,1,0:T(8,128)(2,1)S(1)}, u32[]{:S(2)}, u32[]{:S(2)}) collective-permute-start(bf16[2,256,256]{2,1,0:T(8,128)(2,1)S(1)} %get-tuple-element.60), channel_id=1, source_target_pairs={{0,16},{1,5},{2,18},{3,7},{4,20},{5,9},{6,22},{7,11},{8,24},{9,13}... | collective-permute-start | bytes 786440 | tf_op jit(solution)/shard_map/ppermute | solution.py:36
  236.1 19.8 %collective-permute-start.52 = (bf16[2,256,256]{2,1,0:T(8,128)(2,1)S(1)}, bf16[2,256,256]{2,1,0:T(8,128)(2,1)S(1)}, u32[]{:S(2)}, u32[]{:S(2)}) collective-permute-start(bf16[2,256,256]{2,1,0:T(8,128)(2,1)S(1)} %get-tuple-element.61), channel_id=1, source_target_pairs={{0,32},{1,9},{2,34},{3,11},{4,36},{5,13},{6,38},{7,15},{8,40},{9,1... | collective-permute-start | bytes 786440 | tf_op jit(solution)/shard_map/ppermute | solution.py:36
  242.5 134.6 %collective-permute-start.39 = (bf16[2,256,256]{2,1,0:T(8,128)(2,1)}, bf16[2,256,256]{2,1,0:T(8,128)(2,1)S(1)}, u32[]{:S(2)}, u32[]{:S(2)}) collective-permute-start(bf16[2,256,256]{2,1,0:T(8,128)(2,1)} %get-tuple-element.56), channel_id=1, source_target_pairs={{0,48},{1,13},{2,50},{3,15},{4,52},{5,1},{6,54},{7,3},{8,56},{9,5}... | collective-permute-start | bytes 786440 | tf_op jit(solution)/shard_map/ppermute | solution.py:36
  254.4 122.7 %collective-permute-start.40 = (bf16[2,256,256]{2,1,0:T(8,128)(2,1)}, bf16[2,256,256]{2,1,0:T(8,128)(2,1)S(1)}, u32[]{:S(2)}, u32[]{:S(2)}) collective-permute-start(bf16[2,256,256]{2,1,0:T(8,128)(2,1)} %get-tuple-element.57), channel_id=1, source_target_pairs={{0,16},{1,5},{2,18},{3,7},{4,20},{5,9},{6,22},{7,11},{8,24},{9,13}... | collective-permute-start | bytes 786440 | tf_op jit(solution)/shard_map/ppermute | solution.py:36
  254.4 122.7 %collective-permute-start.41 = (bf16[2,256,256]{2,1,0:T(8,128)(2,1)}, bf16[2,256,256]{2,1,0:T(8,128)(2,1)S(1)}, u32[]{:S(2)}, u32[]{:S(2)}) collective-permute-start(bf16[2,256,256]{2,1,0:T(8,128)(2,1)} %get-tuple-element.58), channel_id=1, source_target_pairs={{0,32},{1,9},{2,34},{3,11},{4,36},{5,13},{6,38},{7,15},{8,40},{9,1... | collective-permute-start | bytes 786440 | tf_op jit(solution)/shard_map/ppermute | solution.py:36
  256.0 121.1 %collective-permute-start.53 = (bf16[2,256,256]{2,1,0:T(8,128)(2,1)S(1)}, bf16[2,256,256]{2,1,0:T(8,128)(2,1)S(1)}, u32[]{:S(2)}, u32[]{:S(2)}) collective-permute-start(bf16[2,256,256]{2,1,0:T(8,128)(2,1)S(1)} %fusion.7), channel_id=1, source_target_pairs={{0,64},{1,65},{2,66},{3,67},{4,68},{5,69},{6,70},{7,71},{8,72},{9,... | collective-permute-start | bytes 786440 | tf_op jit(solution)/shard_map/ppermute | solution.py:36
  (28 other events, 271.0 us)
Sparse Core Ops, SparseCore 0:
  218.8 157.2 all-reduce.1

commit v2 on v1

--- a/solution.py
+++ b/solution.py
@@ -8,7 +8,8 @@
 from jax.sharding import PartitionSpec as P
 
 TILE = 128
-GROUP = 8
+GROUP = 16
+DEPTH = 4
 CLASSES = 4
 PIECES = 4
 PIECE_BLOCKS = 8
@@ -48,6 +49,22 @@
     return move(value, lambda z, x, y, h, c: (z + 1, x, y, h, c))
 
 
+def swap_x(value):
+    return move(value, lambda z, x, y, h, c: (z, x ^ 1, y, h, c))
+
+
+def swap_xx(value):
+    return move(value, lambda z, x, y, h, c: (z, x + 2, y, h, c))
+
+
+def swap_y(value):
+    return move(value, lambda z, x, y, h, c: (z, x, y ^ 1, h, c))
+
+
+def swap_yy(value):
+    return move(value, lambda z, x, y, h, c: (z, x, y + 2, h, c))
+
+
 def move_p(value, by):
     return move(value, lambda z, x, y, h, c: (z, x + by, y, h, c) if c == 0 else (z, x, y + by, h, c))
 
@@ -60,38 +77,46 @@
     return pltpu.CompilerParams(vmem_limit_bytes=mib * MIB)
 
 
-def prep_kernel(rows_ref, mask_ref, plain_ref, turned_ref, degree_ref):
+def degree_kernel(rows_ref, mask_ref, tiles_ref, degree_ref, sums):
     step = pl.program_id(0)
 
     @pl.when(step == 0)
     def _():
-        degree_ref[...] = jnp.zeros_like(degree_ref)
+        sums[...] = jnp.zeros_like(sums)
 
     for k in range(BLOCK_TILES):
-        wide = mask_ref[k].astype(jnp.float32)
-        plain_ref[k] = wide.astype(jnp.bfloat16)
-        turned = wide.T
-        turned_ref[k] = turned.astype(jnp.bfloat16)
+        mask = mask_ref[k].astype(jnp.float32)
         row = rows_ref[step * BLOCK_TILES + k]
-        degree_ref[pl.ds(row, 1), :] += jnp.sum(turned, axis=0, keepdims=True)
-
-
-def prep(tile_rows, tile_masks, block_count):
+        sums[row] += mask
+        tiles_ref[pl.ds(k, 1), :] = jnp.sum(mask, axis=0, keepdims=True)
+
+    @pl.when(step == pl.num_programs(0) - 1)
+    def _():
+        for r in range(degree_ref.shape[0]):
+            degree_ref[pl.ds(r, 1), :] = jnp.sum(sums[r].T, axis=0, keepdims=True)
+
+
+def degrees(tile_rows, tile_masks, block_count):
     slots = tile_masks.shape[0]
-    block = pl.BlockSpec((BLOCK_TILES, TILE, TILE), lambda i: (i, 0, 0))
     return pl.pallas_call(
-        prep_kernel,
+        degree_kernel,
         grid=(slots // BLOCK_TILES,),
-        in_specs=[pl.BlockSpec(memory_space=pltpu.SMEM), block],
-        out_specs=[block, block, pl.BlockSpec((block_count, TILE), lambda i: (0, 0))],
+        in_specs=[
+            pl.BlockSpec(memory_space=pltpu.SMEM),
+            pl.BlockSpec((BLOCK_TILES, TILE, TILE), lambda i: (i, 0, 0)),
+        ],
+        out_specs=[
+            pl.BlockSpec((BLOCK_TILES, TILE), lambda i: (i, 0)),
+            pl.BlockSpec((block_count, TILE), lambda i: (0, 0)),
+        ],
         out_shape=[
-            jax.ShapeDtypeStruct((slots, TILE, TILE), jnp.bfloat16),
-            jax.ShapeDtypeStruct((slots, TILE, TILE), jnp.bfloat16),
+            jax.ShapeDtypeStruct((slots, TILE), jnp.float32),
             jax.ShapeDtypeStruct((block_count, TILE), jnp.float32),
         ],
-        compiler_params=params(16),
-        cost_estimate=pl.CostEstimate(flops=0, bytes_accessed=slots * TILE * TILE * 8, transcendentals=0),
-        name="prep",
+        scratch_shapes=[pltpu.VMEM((block_count, TILE, TILE), jnp.float32)],
+        compiler_params=params(48),
+        cost_estimate=pl.CostEstimate(flops=0, bytes_accessed=slots * TILE * TILE * 4, transcendentals=0),
+        name="degrees",
     )(tile_rows, tile_masks)
 
 
@@ -99,25 +124,29 @@
     return meta & 1023, (meta >> 10) & 31, meta >> 15
 
 
+def as_bf16(mask):
+    return mask.astype(jnp.float32).astype(jnp.bfloat16)
+
+
 def each_group(first, last, meta_ref, masks_ref, buf, sems, body):
     def fetch(group):
-        slot = lax.rem(group, 3)
+        slot = lax.rem(group, DEPTH)
         for u in range(GROUP):
             tile = unpack(meta_ref[group * GROUP + u])[0]
             pltpu.make_async_copy(masks_ref.at[tile], buf.at[slot, u], sems.at[slot]).start()
 
-    for ahead in range(2):
+    for ahead in range(DEPTH - 1):
 
         @pl.when(first + ahead < last)
         def _():
             fetch(first + ahead)
 
     def turn(group, carry):
-        @pl.when(group + 2 < last)
+        @pl.when(group + DEPTH - 1 < last)
         def _():
-            fetch(group + 2)
-
-        slot = lax.rem(group, 3)
+            fetch(group + DEPTH - 1)
+
+        slot = lax.rem(group, DEPTH)
         pltpu.make_async_copy(masks_ref.at[pl.ds(0, GROUP)], buf.at[slot], sems.at[slot]).wait()
         body(group, slot)
         return carry
@@ -153,7 +182,7 @@
         for u in range(GROUP):
             _, row, block = unpack(meta_ref[group * GROUP + u])
             part = jnp.dot(
-                buf[slot, u],
+                as_bf16(buf[slot, u]),
                 feats[pl.ds(pl.multiple_of(block * TILE, TILE), TILE), :],
                 preferred_element_type=jnp.float32,
             )
@@ -178,8 +207,8 @@
     feat_rows = (CLASS_BLOCKS + 1) * TILE
     scratch = [
         pltpu.VMEM((feat_rows, width), jnp.bfloat16),
-        pltpu.VMEM((3, GROUP, TILE, TILE), jnp.bfloat16),
-        pltpu.SemaphoreType.DMA((3,)),
+        pltpu.VMEM((DEPTH, GROUP, TILE, TILE), jnp.int32),
+        pltpu.SemaphoreType.DMA((DEPTH,)),
         pltpu.SemaphoreType.DMA((PIECES + 1,)),
     ]
     vmem = pl.BlockSpec(memory_space=pltpu.VMEM)
@@ -191,15 +220,16 @@
         out_shape, out_specs = jax.ShapeDtypeStruct((total_rows, width), jnp.float32), vmem
     smem = pl.BlockSpec(memory_space=pltpu.SMEM)
     anywhere = pl.BlockSpec(memory_space=pl.ANY)
+    held = pl.BlockSpec(memory_space=pltpu.HBM)
     extra = [] if first_call else [before]
     tiles = masks.shape[0] // CLASSES
     return pl.pallas_call(
         functools.partial(forward_kernel, which, first_call, last_call),
-        in_specs=[smem, smem] + [anywhere] * (1 + len(pieces) + len(extra)),
+        in_specs=[smem, smem, held] + [anywhere] * (len(pieces) + len(extra)),
         out_specs=out_specs,
         out_shape=out_shape,
         scratch_shapes=scratch,
-        compiler_params=params(16),
+        compiler_params=params(48),
         cost_estimate=pl.CostEstimate(
             flops=tiles * TILE * TILE * width * 2 * 4, bytes_accessed=8 * MIB, transcendentals=0
         ),
@@ -226,9 +256,10 @@
     def body(group, slot):
         for u in range(GROUP):
             _, row, block = unpack(meta_ref[group * GROUP + u])
-            part = jnp.dot(
-                buf[slot, u],
+            part = lax.dot_general(
+                as_bf16(buf[slot, u]),
                 grads[pl.ds(pl.multiple_of(row * TILE, TILE), TILE), :],
+                (((0,), (0,)), ((), ())),
                 preferred_element_type=jnp.float32,
             )
             total[pl.ds(pl.multiple_of(block * TILE, TILE), TILE), :] += part
@@ -244,21 +275,22 @@
     vmem = pl.BlockSpec(memory_space=pltpu.VMEM)
     smem = pl.BlockSpec(memory_space=pltpu.SMEM)
     anywhere = pl.BlockSpec(memory_space=pl.ANY)
+    held = pl.BlockSpec(memory_space=pltpu.HBM)
     piece = jax.ShapeDtypeStruct((PIECE_BLOCKS * TILE, width), jnp.bfloat16)
     tiles = masks.shape[0] // CLASSES
     return pl.pallas_call(
         functools.partial(backward_kernel, which),
-        in_specs=[smem, smem] + [anywhere] * 5,
+        in_specs=[smem, smem, held] + [anywhere] * 4,
         out_specs=[vmem] * PIECES,
         out_shape=[piece] * PIECES,
         scratch_shapes=[
             pltpu.VMEM((4 * quarter + TILE, width), jnp.bfloat16),
-            pltpu.VMEM((3, GROUP, TILE, TILE), jnp.bfloat16),
-            pltpu.SemaphoreType.DMA((3,)),
+            pltpu.VMEM((DEPTH, GROUP, TILE, TILE), jnp.int32),
+            pltpu.SemaphoreType.DMA((DEPTH,)),
             pltpu.SemaphoreType.DMA((4,)),
             pltpu.VMEM(((CLASS_BLOCKS + 1) * TILE, width), jnp.float32),
         ],
-        compiler_params=params(16),
+        compiler_params=params(48),
         cost_estimate=pl.CostEstimate(
             flops=tiles * TILE * TILE * width * 2 * 4, bytes_accessed=8 * MIB, transcendentals=0
         ),
@@ -312,7 +344,7 @@
     )(features, self_weight, neigh_weight, cotangent, scale, keep, near, far)
 
 
-def plan_tiles(tile_rows, tile_cols, row_blocks):
+def plan_tiles(tile_rows, tile_cols, tile_sums, row_blocks):
     slots = tile_rows.shape[0]
     row_index, rep_index = lax.axis_index("row"), lax.axis_index("rep")
     z, x, y = row_index // 16, row_index // 4 % 4, row_index % 4
@@ -323,6 +355,7 @@
     dx, dy = (section // 4 % 4 - x) % 4, (section % 4 - y) % 4
     dp, dq = jnp.where(stream == 0, dx, dy), jnp.where(stream == 0, dy, dx)
     kind = jnp.where(dq == 0, 0, jnp.where(dq == 2, 3, 1 + far_z))
+    kind = jnp.where(jnp.max(tile_sums, axis=1) > 0, kind, CLASSES)
     pair = jnp.where(dq % 2 == 0, far_z, (dq == 1).astype(jnp.int32))
     piece = pair * 2 + (stream != core).astype(jnp.int32)
     place = jnp.where(dp == 0, 0, jnp.where(dp == 3, 1, jnp.where(dp == 1, 2, 3)))
@@ -338,102 +371,123 @@
     same_before = (kind[:, None] == kind[None, :]) & (slot[None, :] < slot[:, None])
     rank = jnp.sum(same_before.astype(jnp.int32), axis=1)
     start = jnp.sum(jnp.where(kind[:, None] == classes[None, :], starts[None, :CLASSES], 0), axis=1)
-    position = start * GROUP + rank
+    position = jnp.where(kind < CLASSES, start * GROUP + rank, -1)
     places = -(-(slots + CLASSES * (GROUP - 1)) // GROUP) * GROUP
     hit = jnp.arange(places, dtype=jnp.int32)[:, None] == position[None, :]
     pad = row_blocks * 1024 + CLASS_BLOCKS * 32768
     meta = pad + jnp.sum(jnp.where(hit, code[None, :] - pad, 0), axis=1)
     bounds = jnp.concatenate([starts, core[None], high[None]]).astype(jnp.int32)
-    return meta.astype(jnp.int32), bounds, core, high
-
-
-def gather(features, core):
+    return meta.astype(jnp.int32), bounds
+
+
+def tie(*values):
+    return lax.optimization_barrier(values)
+
+
+def add(*values):
+    return sum(value.astype(jnp.float32) for value in values).astype(jnp.bfloat16)
+
+
+def local(features, self_weight, neigh_weight, tile_rows, tile_cols, tile_masks, cotangent):
     rows, width = features.shape
     half = rows // 2
+    row_blocks = rows * 4 // TILE
+    core, high = lax.axis_index("rep") % 2, lax.axis_index("rep") // 2
+
     mine = lax.dynamic_slice_in_dim(features, core * half, half, 0)
     theirs = lax.dynamic_slice_in_dim(features, (1 - core) * half, half, 0)
     own = jnp.stack([mine, swap_core(theirs)])
-    sides = []
-    for start in (own, swap_low(own)):
-        near = [start, move_p(start, 1), move_p(start, -1), move_p(start, 2)]
-        block = jnp.stack(near, axis=1).reshape(2, 4 * half, width)
-        below, above = move_q(block, 1), move_q(block, -1)
-        sides.append((block, below, above, move_q(below[0], 1), move_q(above[1], -1)))
-    classes = [[], [], [], []]
-    for s, (block, below, above, far0, far1) in enumerate(sides):
-        classes[0] += [block, swap_core(block[1])]
-        classes[1 + s] += [below, swap_core(below[1]), above, swap_core(above[1])]
-        classes[3] += [far0, swap_core(far1)]
-    return classes
-
-
-def add(*values):
-    return sum(value.astype(jnp.float32) for value in values).astype(jnp.bfloat16)
-
-
-def scatter(run_class, core):
-    far = run_class(3)
-    sides = [None, None]
-    for s in (1, 0):
-        from_below = move_q(far[2 * s], 1)
-        from_above = move_q(swap_core(far[2 * s + 1]), -1)
-        down, down_other, up, up_other = run_class(1 + s)
-        to_above = jnp.stack([add(up, from_below), swap_core(up_other)])
-        to_below = jnp.stack([down, add(swap_core(down_other), from_above)])
-        sides[s] = (move_q(to_above, 1), move_q(to_below, -1))
-    here = run_class(0)
-    ends = [None, None]
-    for s in (1, 0):
-        total = add(jnp.stack([here[2 * s], swap_core(here[2 * s + 1])]), *sides[s])
-        parts = total.reshape(2, 4, -1, total.shape[-1])
-        ends[s] = sum(
-            value.astype(jnp.float32)
-            for value in (
-                parts[:, 0],
-                move_p(parts[:, 1], -1),
-                move_p(parts[:, 2], 1),
-                move_p(parts[:, 3], 2),
-            )
-        )
-    end = ends[0] + swap_low(ends[1].astype(jnp.bfloat16)).astype(jnp.float32)
-    mine = end[0]
-    other = swap_core(end[1].astype(jnp.bfloat16)).astype(jnp.float32)
-    first = jnp.where(core == 0, mine, other)
-    second = jnp.where(core == 0, other, mine)
-    return jnp.concatenate([first, second], axis=0)
-
-
-def local(features, self_weight, neigh_weight, tile_rows, tile_cols, tile_masks, cotangent):
-    rows, width = features.shape
-    row_blocks = rows * 4 // TILE
-    meta, bounds, core, high = plan_tiles(tile_rows, tile_cols, row_blocks)
-    classes = gather(features, core)
-    plain, turned, degree = prep(tile_rows, tile_masks, row_blocks)
+    low = swap_low(own)
+    near = [move_p(own, 1), move_p(own, -1), move_p(own, 2)]
+    tile_sums, degree = degrees(tile_rows, tile_masks, row_blocks)
+    *near, low, tile_sums, degree = tie(*near, low, tile_sums, degree)
+    block0 = jnp.stack([own, *near], axis=1).reshape(2, 4 * half, width)
+    below0, above0 = move_q(block0, 1), move_q(block0, -1)
+    meta, bounds = plan_tiles(tile_rows, tile_cols, tile_sums, row_blocks)
+    low, meta = tie(low, meta)
+    near = [move_p(low, 1), move_p(low, -1), move_p(low, 2)]
     degree = degree + swap_core(degree)
     degree = degree + swap_high(degree)
+    *near, degree = tie(*near, degree)
+    block1 = jnp.stack([low, *near], axis=1).reshape(2, 4 * half, width)
+    below1, above1 = move_q(block1, 1), move_q(block1, -1)
+
+    def forward(which, before, *pieces):
+        return forward_class(which, meta, bounds, tile_masks, pieces, before, row_blocks)
+
     own_degree = lax.dynamic_slice_in_dim(
         degree, (high * 2 + core) * (row_blocks // 4), row_blocks // 4, 0
     )
     scale = jnp.broadcast_to(
         lax.rsqrt(jnp.maximum(own_degree, 1.0)).reshape(rows, 1), (rows, width)
     )
-    total = None
-    for which in range(CLASSES):
-        total = forward_class(which, meta, bounds, plain, classes[which], total, row_blocks)
-    keep, give = total
+    total = forward(0, None, block0, swap_core(block0[1]), block1, swap_core(block1[1]))
+    below0, above0, total, scale = tie(below0, above0, total, scale)
+    far00, far01 = move_q(below0[0], 1), move_q(above0[1], -1)
+    total = forward(1, total, below0, swap_core(below0[1]), above0, swap_core(above0[1]))
+    below1, above1, total = tie(below1, above1, total)
+    far10, far11 = move_q(below1[0], 1), move_q(above1[1], -1)
+    total = forward(2, total, below1, swap_core(below1[1]), above1, swap_core(above1[1]))
+    keep, give = forward(3, total, far00, swap_core(far01), far10, swap_core(far11))
+
     near = swap_core(give)
     far = swap_high(add(keep[1], near[1]))
     output, back, mean, weight = dense(
         features, self_weight, neigh_weight, cotangent, scale, keep, near, far
     )
-    weight = lax.psum(weight, BOTH) * ((rows * lax.axis_size(BOTH)) ** (-0.5))
     mean_far = swap_high(mean)
     grads = (mean, mean_far, swap_core(mean), swap_core(mean_far))
-    incoming = scatter(
-        lambda which: backward_class(which, meta, bounds, turned, grads), core
+    weight_mine = lax.dynamic_slice_in_dim(weight, core * width, width, 0)
+    weight_theirs = lax.dynamic_slice_in_dim(weight, (1 - core) * width, width, 0)
+    weight = weight_mine + swap_core(weight_theirs)
+
+    def fold(weight, exchange):
+        sent = weight.astype(jnp.bfloat16)
+        return sent.astype(jnp.float32) + exchange(sent).astype(jnp.float32)
+
+    def backward(which):
+        return backward_class(which, meta, bounds, tile_masks, grads)
+
+    far = backward(3)
+    weight = fold(weight, swap_high)
+    passed = {}
+    for s in (1, 0):
+        passed[s] = (move_q(far[2 * s], 1), move_q(swap_core(far[2 * s + 1]), -1))
+    sides = {}
+    for s, exchange in ((1, swap_low), (0, swap_x)):
+        down, down_other, up, up_other = backward(1 + s)
+        from_below, from_above = passed[s]
+        down, down_other, up, up_other, from_below, from_above, weight = tie(
+            down, down_other, up, up_other, from_below, from_above, weight
+        )
+        to_above = jnp.stack([add(up, from_below), swap_core(up_other)])
+        to_below = jnp.stack([down, add(swap_core(down_other), from_above)])
+        sides[s] = (move_q(to_above, 1), move_q(to_below, -1))
+        weight = fold(weight, exchange)
+    here = backward(0)
+    *here, weight = tie(*here, weight)
+    ends = {}
+    for s, exchange in ((1, swap_xx), (0, swap_y)):
+        from_below, from_above = sides[s]
+        from_below, from_above, weight = tie(from_below, from_above, weight)
+        total = add(jnp.stack([here[2 * s], swap_core(here[2 * s + 1])]), from_below, from_above)
+        parts = total.reshape(2, 4, half, width)
+        moved = (move_p(parts[:, 1], -1), move_p(parts[:, 2], 1), move_p(parts[:, 3], 2))
+        weight = fold(weight, exchange)
+        ends[s] = (parts[:, 0], *moved)
+    passed = swap_low(add(*ends[1]))
+    weight = fold(weight, swap_yy)
+    end = sum(value.astype(jnp.float32) for value in (*ends[0], passed))
+    other = swap_core(end[1].astype(jnp.bfloat16)).astype(jnp.float32)
+    incoming = jnp.concatenate(
+        [jnp.where(core == 0, end[0], other), jnp.where(core == 0, other, end[0])], axis=0
     )
     grad_feat = (back + incoming).astype(jnp.bfloat16)
-    return (output, grad_feat, weight[:width], weight[width:])
+    weight = weight * ((rows * lax.axis_size(BOTH)) ** (-0.5))
+    weight_other = swap_core(weight)
+    self_total = jnp.where(core == 0, weight, weight_other)
+    neigh_total = jnp.where(core == 0, weight_other, weight)
+    return (output, grad_feat, self_total, neigh_total)
 
 
 def solution(mesh):

time: 388 us -> 205 us (0.53)
  waiting for transfers between devices: 167 us -> 51.9 us
  Pallas kernels: 87 us -> 57.1 us
  between operations: 14.7 us -> 1.31 us
  starting transfers between devices: 88.1 us -> 78 us
  local copies, waits for them, and re-layouts: 16.6 us -> 8.31 us
  other arithmetic: 12.9 us -> 6.29 us
    psum x1 -> x0, waiting for transfers between devices: 119 us -> none  [local(): weight = lax.psum(weight, BOTH) * (rows * lax.axis_size(BOTH)) ** (-0.5)]
    pallas_call x4, Pallas kernels: 33.7 us -> 18.9 us  [backward_class(): pl.pallas_call(functools.partial(backward_kernel, which), in_specs=[smem,...]
    pallas_call x4, Pallas kernels: 34.7 us -> 21.3 us  [forward_class(): pl.pallas_call(functools.partial(forward_kernel, which, first_call, last_...]
    ppermute x55 -> x63, starting transfers between devices: 88.1 us -> 78 us  [move(): return lax.ppermute(value, BOTH, pairs(step))]
    unnamed x40 -> x20, local copies, waits for them, and re-layouts: 9.65 us -> 3.11 us
    another operation x11, other arithmetic: 5.21 us -> 1.25 us  [the longest x4 0.48 us: local(): to_below = jnp.stack([down, add(swap_core(down_other), from_above)])]
    ppermute x55 -> x63, waiting for transfers between devices: 48.5 us -> 51.9 us  [move(): return lax.ppermute(value, BOTH, pairs(step))]
  transfers between devices with their start and end apart: 56 -> 63, of which waited for: 16 -> 20; matrix products, arithmetic and copies ran while one was open for 5% -> 4% of each run, Pallas kernels for 19% -> 25%
where the time goes in v2:
time: 205 us; the launch traced here: 203 us
  starting transfers between devices  78 us (38%)
  Pallas kernels  57.1 us (28%)
  waiting for transfers between devices  51.9 us (25%)
  local copies, waits for them, and re-layouts  8.31 us (4%)
  other arithmetic  6.29 us (3%)
    ppermute x63, starting transfers between devices, move(): return lax.ppermute(value, BOTH, pairs(step))  78 us
    ppermute x63, waiting for transfers between devices, move(): return lax.ppermute(value, BOTH, pairs(step))  51.9 us
    pallas_call x4, Pallas kernels, forward_class(): pl.pallas_call(functools.partial(forward_kernel, which, first_call, last_...  21.3 us
    pallas_call x4, Pallas kernels, backward_class(): pl.pallas_call(functools.partial(backward_kernel, which), in_specs=[smem,...  18.9 us
    pallas_call x1, Pallas kernels, degrees(): pl.pallas_call(degree_kernel, grid=(slots // BLOCK_TILES,), in_specs=[pl....  15.5 us
  transfers between devices with their start and end apart: 63, of which 20 were waited for; matrix products, arithmetic and copies ran while one was open for 4% of the time, Pallas kernels for 25%

profile of v2, /device:TPU:0, one launch (start us, length us, event | category | flops | bytes accessed | tf_op | source)
XLA Modules:
  0.0 202.9 jit_solution(13332211794775132560)
XLA Ops:
  1.7 1.3 collective-permute-done
  3.1 1.6 collective-permute-start.1
  4.8 1.7 collective-permute-start.2
  6.4 1.9 collective-permute-start.3
  8.3 1.9 collective-permute-start.4
  10.9 15.5 %degrees.1 = (f32[320,128]{1,0:T(8,128)S(1)}, f32[16,128]{1,0:T(8,128)S(1)}) custom-call(s32[320]{0:T(512)S(1)} %copy-done.6, s32[320,128,128]{2,1,0:T(8,128)} %masks_ref.15), custom_call_target="tpu_custom_call" | custom-call | bytes 20971520 | tf_op jit(solution)/shard_map/degrees/pallas_call | solution.py:101
  27.6 2.3 %collective-permute-start.10 = (bf16[2,256,256]{2,1,0:T(8,128)(2,1)S(1)}, bf16[2,256,256]{2,1,0:T(8,128)(2,1)S(1)}, u32[]{:S(2)}, u32[]{:S(2)}) collective-permute-start(bf16[2,256,256]{2,1,0:T(8,128)(2,1)S(1)} %collective-permute-done.4), channel_id=1, source_target_pairs={{0,32},{1,9},{2,34},{3,11},{4,36},{5,13},{6,38},{7,15},{8,40},{9,1... | collective-permute-start | bytes 786440 | tf_op jit(solution)/shard_map/ppermute | solution.py:37
  30.4 2.6 %collective-permute-start.9 = (bf16[2,256,256]{2,1,0:T(8,128)(2,1)S(1)}, bf16[2,256,256]{2,1,0:T(8,128)(2,1)S(1)}, u32[]{:S(2)}, u32[]{:S(2)}) collective-permute-start(bf16[2,256,256]{2,1,0:T(8,128)(2,1)S(1)} %collective-permute-done.4), channel_id=1, source_target_pairs={{0,48},{1,13},{2,50},{3,15},{4,52},{5,1},{6,54},{7,3},{8,56},{9,5}... | collective-permute-start | bytes 786440 | tf_op jit(solution)/shard_map/ppermute | solution.py:37
  33.1 3.6 %collective-permute-start.12 = (f32[16,128]{1,0:T(8,128)S(1)}, f32[16,128]{1,0:T(8,128)S(1)}, u32[]{:S(2)}, u32[]{:S(2)}) collective-permute-start(f32[16,128]{1,0:T(8,128)S(1)} %add.205), channel_id=1, source_target_pairs={{0,2},{1,3},{2,0},{3,1},{4,6},{5,7},{6,4},{7,5},{8,10},{9,11},{10,... | collective-permute-start | bytes 24584 | tf_op jit(solution)/shard_map/ppermute | solution.py:37
  38.3 2.5 %collective-permute-start.6 = (bf16[2,1024,256]{2,1,0:T(8,128)(2,1)S(1)}, bf16[2,1024,256]{2,1,0:T(8,128)(2,1)S(1)}, u32[]{:S(2)}, u32[]{:S(2)}) collective-permute-start(bf16[2,1024,256]{2,1,0:T(8,128)(2,1)S(1)} %bitcast.100), channel_id=1, source_target_pairs={{0,12},{1,49},{2,14},{3,51},{4,0},{5,53},{6,2},{7,55},{8,4},{9,57}... | collective-permute-start | bytes 3145736 | tf_op jit(solution)/shard_map/ppermute | solution.py:37
  45.7 3.3 %collective-permute-start.18 = (bf16[2,1024,256]{2,1,0:T(8,128)(2,1)S(1)}, bf16[2,1024,256]{2,1,0:T(8,128)(2,1)S(1)}, u32[]{:S(2)}, u32[]{:S(2)}) collective-permute-start(bf16[2,1024,256]{2,1,0:T(8,128)(2,1)S(1)} %bitcast.103), channel_id=1, source_target_pairs={{0,12},{1,49},{2,14},{3,51},{4,0},{5,53},{6,2},{7,55},{8,4},{9,57}... | collective-permute-start | bytes 3145736 | tf_op jit(solution)/shard_map/ppermute | solution.py:37
  48.9 5.1 %forward_class0.1.refs_4_ = f32[2176,256]{1,0:T(8,128)S(1)} custom-call(s32[384]{0:T(512)S(1)} %broadcast_add_fusion.meta_ref, s32[7]{0:T(128)S(1)} %pad_add_fusion.bounds_ref, s32[320,128,128]{2,1,0:T(8,128)} %masks_ref.15, bf16[2,1024,256]{2,1,0:T(8,128)(2,1)S(1)} %bitcast.101, bf16[1024,256]{1,0:T(8,128)(2,1)} %collective-permute-done.7.refs_1_, ...), custom_call_target="tpu_custom_call" | custom-call | flops 2684354560 | bytes 8388608 | tf_op jit(solution)/shard_map/forward_class0/pallas_call | solution.py:226
  54.1 1.4 copy-done
  56.4 1.4 collective-permute-start.15
  58.4 6.0 %forward_class1.1.refs_4_ = f32[2176,256]{1,0:T(8,128)S(1)} custom-call(s32[384]{0:T(512)S(1)} %broadcast_add_fusion.meta_ref, s32[7]{0:T(128)S(1)} %pad_add_fusion.bounds_ref, s32[320,128,128]{2,1,0:T(8,128)} %masks_ref.15, bf16[2,1024,256]{2,1,0:T(8,128)(2,1)S(1)} %collective-permute-done.5.refs_0_, bf16[1024,256]{1,0:T(8,128)(2,1)S(1)} %collective-permute-done.19.refs_1_, ...), custom_call_target="tpu_custom_call" | custom-call | flops 2684354560 | bytes 8388608 | tf_op jit(solution)/shard_map/forward_class1/pallas_call | solution.py:226
  64.6 3.7 %collective-permute-start.22 = (bf16[1024,256]{1,0:T(8,128)(2,1)S(1)}, bf16[1024,256]{1,0:T(8,128)(2,1)S(1)}, u32[]{:S(2)}, u32[]{:S(2)}) collective-permute-start(bf16[1024,256]{1,0:T(8,128)(2,1)S(1)} %slice_bitcast_fusion.1), channel_id=1, source_target_pairs={{0,12},{1,49},{2,14},{3,51},{4,0},{5,53},{6,2},{7,55},{8,4},{9,57}... | collective-permute-start | bytes 1572872 | tf_op jit(solution)/shard_map/ppermute | solution.py:37
  68.4 1.6 collective-permute-done.15
  71.3 4.3 %collective-permute-done.22 = bf16[1024,256]{1,0:T(8,128)(2,1)S(1)} collective-permute-done((bf16[1024,256]{1,0:T(8,128)(2,1)S(1)}, bf16[1024,256]{1,0:T(8,128)(2,1)S(1)}, u32[]{:S(2)}, u32[]{:S(2)}) %collective-permute-start.22) | collective-permute-done | bytes 524320 | tf_op jit(solution)/shard_map/ppermute | solution.py:37
  75.6 6.1 %forward_class2.1.refs_4_ = f32[2176,256]{1,0:T(8,128)S(1)} custom-call(s32[384]{0:T(512)S(1)} %broadcast_add_fusion.meta_ref, s32[7]{0:T(128)S(1)} %pad_add_fusion.bounds_ref, s32[320,128,128]{2,1,0:T(8,128)} %masks_ref.15, bf16[2,1024,256]{2,1,0:T(8,128)(2,1)S(1)} %collective-permute-done.17.refs_0_, ...), custom_call_target="tpu_custom_call" | custom-call | flops 2684354560 | bytes 8388608 | tf_op jit(solution)/shard_map/forward_class2/pallas_call | solution.py:226
  81.8 2.6 %collective-permute-done.21.refs_2_ = bf16[1024,256]{1,0:T(8,128)(2,1)S(1)} collective-permute-done((bf16[1024,256]{1,0:T(8,128)(2,1)S(1)}, bf16[1024,256]{1,0:T(8,128)(2,1)S(1)}, u32[]{:S(2)}, u32[]{:S(2)}) %collective-permute-start.21) | collective-permute-done | bytes 524320 | tf_op jit(solution)/shard_map/ppermute | solution.py:37
  84.4 4.2 %forward_class3.1 = (bf16[2,512,256]{2,1,0:T(8,128)(2,1)S(1)}, bf16[2,512,256]{2,1,0:T(8,128)(2,1)S(1)}) custom-call(s32[384]{0:T(512)S(1)} %broadcast_add_fusion.meta_ref, s32[7]{0:T(128)S(1)} %pad_add_fusion.bounds_ref, s32[320,128,128]{2,1,0:T(8,128)} %masks_ref.15, bf16[1024,256]{1,0:T(8,128)(2,1)S(1)} %collective-permute-done.14.refs_0_, ...), custom_call_target="tpu_custom_call" | custom-call | flops 2684354560 | bytes 8388608 | tf_op jit(solution)/shard_map/forward_class3/pallas_call | solution.py:226
  88.7 1.9 collective-permute-done.26.near_ref
  90.7 3.2 %collective-permute-start.27 = (bf16[512,256]{1,0:T(8,128)(2,1)S(1)}, bf16[512,256]{1,0:T(8,128)(2,1)S(1)}, u32[]{:S(2)}, u32[]{:S(2)}) collective-permute-start(bf16[512,256]{1,0:T(8,128)(2,1)S(1)} %fusion.12), channel_id=1, source_target_pairs={{0,2},{1,3},{2,0},{3,1},{4,6},{5,7},{6,4},{7,5},{8,10},{9,11},{10,... | collective-permute-start | bytes 786440 | tf_op jit(solution)/shard_map/ppermute | solution.py:37
  93.9 6.7 %collective-permute-done.27.far_ref = bf16[512,256]{1,0:T(8,128)(2,1)S(1)} collective-permute-done((bf16[512,256]{1,0:T(8,128)(2,1)S(1)}, bf16[512,256]{1,0:T(8,128)(2,1)S(1)}, u32[]{:S(2)}, u32[]{:S(2)}) %collective-permute-start.27) | collective-permute-done | bytes 262176 | tf_op jit(solution)/shard_map/ppermute | solution.py:37
  100.6 1.3 dense.1
  101.9 3.1 %collective-permute-start.28 = (bf16[512,256]{1,0:T(8,128)(2,1)S(1)}, bf16[512,256]{1,0:T(8,128)(2,1)S(1)}, u32[]{:S(2)}, u32[]{:S(2)}) collective-permute-start(bf16[512,256]{1,0:T(8,128)(2,1)S(1)} %get-tuple-element.97.own), channel_id=1, source_target_pairs={{0,2},{1,3},{2,0},{3,1},{4,6},{5,7},{6,4},{7,5},{8,10},{9,11},{10,... | collective-permute-start | bytes 786440 | tf_op jit(solution)/shard_map/ppermute | solution.py:37
  105.1 5.9 %collective-permute-done.28.far = bf16[512,256]{1,0:T(8,128)(2,1)S(1)} collective-permute-done((bf16[512,256]{1,0:T(8,128)(2,1)S(1)}, bf16[512,256]{1,0:T(8,128)(2,1)S(1)}, u32[]{:S(2)}, u32[]{:S(2)}) %collective-permute-start.28) | collective-permute-done | bytes 262176 | tf_op jit(solution)/shard_map/ppermute | solution.py:37
  112.5 4.4 %backward_class3.1 = (bf16[1024,256]{1,0:T(8,128)(2,1)S(1)}, bf16[1024,256]{1,0:T(8,128)(2,1)S(1)}, bf16[1024,256]{1,0:T(8,128)(2,1)S(1)}, bf16[1024,256]{1,0:T(8,128)(2,1)S(1)}) custom-call(s32[384]{0:T(512)S(1)} %broadcast_add_fusion.meta_ref, s32[7]{0:T(128)S(1)} %pad_add_fusion.bounds_ref, s32[320,128,128]{2,1,0:T(8,128)} %masks_ref.15, ...), custom_call_target="tpu_custom_call" | custom-call | flops 2684354560 | bytes 8388608 | tf_op jit(solution)/shard_map/backward_class3/pallas_call | solution.py:281
  117.1 3.3 %collective-permute-start.38 = (bf16[256,256]{1,0:T(8,128)(2,1)S(1)}, bf16[256,256]{1,0:T(8,128)(2,1)S(1)}, u32[]{:S(2)}, u32[]{:S(2)}) collective-permute-start(bf16[256,256]{1,0:T(8,128)(2,1)S(1)} %add_convert_fusion.8), channel_id=1, source_target_pairs={{0,2},{1,3},{2,0},{3,1},{4,6},{5,7},{6,4},{7,5},{8,10},{9,11},{10,... | collective-permute-start | bytes 393224 | tf_op jit(solution)/shard_map/ppermute | solution.py:37
  121.3 2.3 %collective-permute-start.36 = (bf16[1024,256]{1,0:T(8,128)(2,1)S(1)}, bf16[1024,256]{1,0:T(8,128)(2,1)S(1)}, u32[]{:S(2)}, u32[]{:S(2)}) collective-permute-start(bf16[1024,256]{1,0:T(8,128)(2,1)S(1)} %collective-permute-done.35), channel_id=1, source_target_pairs={{0,12},{1,49},{2,14},{3,51},{4,0},{5,53},{6,2},{7,55},{8,4},{9,57}... | collective-permute-start | bytes 1572872 | tf_op jit(solution)/shard_map/ppermute | solution.py:37
  125.1 4.9 %backward_class2.1 = (bf16[1024,256]{1,0:T(8,128)(2,1)S(1)}, bf16[1024,256]{1,0:T(8,128)(2,1)S(1)}, bf16[1024,256]{1,0:T(8,128)(2,1)S(1)}, bf16[1024,256]{1,0:T(8,128)(2,1)S(1)}) custom-call(s32[384]{0:T(512)S(1)} %broadcast_add_fusion.meta_ref, s32[7]{0:T(128)S(1)} %pad_add_fusion.bounds_ref, s32[320,128,128]{2,1,0:T(8,128)} %masks_ref.15, ...), custom_call_target="tpu_custom_call" | custom-call | flops 2684354560 | bytes 8388608 | tf_op jit(solution)/shard_map/backward_class2/pallas_call | solution.py:281
  130.0 4.9 %backward_class1.1 = (bf16[1024,256]{1,0:T(8,128)(2,1)S(1)}, bf16[1024,256]{1,0:T(8,128)(2,1)S(1)}, bf16[1024,256]{1,0:T(8,128)(2,1)S(1)}, bf16[1024,256]{1,0:T(8,128)(2,1)S(1)}) custom-call(s32[384]{0:T(512)S(1)} %broadcast_add_fusion.meta_ref, s32[7]{0:T(128)S(1)} %pad_add_fusion.bounds_ref, s32[320,128,128]{2,1,0:T(8,128)} %masks_ref.15, ...), custom_call_target="tpu_custom_call" | custom-call | flops 2684354560 | bytes 8388608 | tf_op jit(solution)/shard_map/backward_class1/pallas_call | solution.py:281
  136.5 4.6 %backward_class0.1 = (bf16[1024,256]{1,0:T(8,128)(2,1)S(1)}, bf16[1024,256]{1,0:T(8,128)(2,1)S(1)}, bf16[1024,256]{1,0:T(8,128)(2,1)S(1)}, bf16[1024,256]{1,0:T(8,128)(2,1)S(1)}) custom-call(s32[384]{0:T(512)S(1)} %broadcast_add_fusion.meta_ref, s32[7]{0:T(128)S(1)} %pad_add_fusion.bounds_ref, s32[320,128,128]{2,1,0:T(8,128)} %masks_ref.15, ...), custom_call_target="tpu_custom_call" | custom-call | flops 2684354560 | bytes 8388608 | tf_op jit(solution)/shard_map/backward_class0/pallas_call | solution.py:281
  141.5 4.7 %collective-permute-done.39 = bf16[256,256]{1,0:T(8,128)(2,1)S(1)} collective-permute-done((bf16[256,256]{1,0:T(8,128)(2,1)S(1)}, bf16[256,256]{1,0:T(8,128)(2,1)S(1)}, u32[]{:S(2)}, u32[]{:S(2)}) %collective-permute-start.39) | collective-permute-done | bytes 131104 | tf_op jit(solution)/shard_map/ppermute | solution.py:37
  146.2 1.8 collective-permute-start.40
  148.8 1.6 collective-permute-start.49
  151.8 4.5 %collective-permute-start.45 = (bf16[2,1024,256]{2,1,0:T(8,128)(2,1)S(1)}, bf16[2,1024,256]{2,1,0:T(8,128)(2,1)S(1)}, u32[]{:S(2)}, u32[]{:S(2)}) collective-permute-start(bf16[2,1024,256]{2,1,0:T(8,128)(2,1)S(1)} %pad_maximum_fusion.3), channel_id=1, source_target_pairs={{0,12},{1,49},{2,14},{3,51},{4,0},{5,53},{6,2},{7,55},{8,4},{9,57}... | collective-permute-start | bytes 3145736 | tf_op jit(solution)/shard_map/ppermute | solution.py:37
  156.4 7.2 %collective-permute-done.49 = bf16[2,1024,256]{2,1,0:T(8,128)(2,1)S(1)} collective-permute-done((bf16[2,1024,256]{2,1,0:T(8,128)(2,1)S(1)}, bf16[2,1024,256]{2,1,0:T(8,128)(2,1)S(1)}, u32[]{:S(2)}, u32[]{:S(2)}) %collective-permute-start.49) | collective-permute-done | bytes 1048608 | tf_op jit(solution)/shard_map/ppermute | solution.py:37
  163.7 2.9 %collective-permute-done.47 = bf16[2,1024,256]{2,1,0:T(8,128)(2,1)S(1)} collective-permute-done((bf16[2,1024,256]{2,1,0:T(8,128)(2,1)S(1)}, bf16[2,1024,256]{2,1,0:T(8,128)(2,1)S(1)}, u32[]{:S(2)}, u32[]{:S(2)}) %collective-permute-start.47) | collective-permute-done | bytes 1048608 | tf_op jit(solution)/shard_map/ppermute | solution.py:37
  167.7 4.0 %collective-permute-start.55 = (bf16[2,256,256]{2,1,0:T(8,128)(2,1)S(1)}, bf16[2,256,256]{2,1,0:T(8,128)(2,1)S(1)}, u32[]{:S(2)}, u32[]{:S(2)}) collective-permute-start(bf16[2,256,256]{2,1,0:T(8,128)(2,1)S(1)} %get-tuple-element.145), channel_id=1, source_target_pairs={{0,48},{1,13},{2,50},{3,15},{4,52},{5,1},{6,54},{7,3},{8,56},{9,5}... | collective-permute-start | bytes 786440 | tf_op jit(solution)/shard_map/ppermute | solution.py:37
  171.8 2.7 %collective-permute-done.50 = bf16[256,256]{1,0:T(8,128)(2,1)S(1)} collective-permute-done((bf16[256,256]{1,0:T(8,128)(2,1)S(1)}, bf16[256,256]{1,0:T(8,128)(2,1)S(1)}, u32[]{:S(2)}, u32[]{:S(2)}) %collective-permute-start.50) | collective-permute-done | bytes 131104 | tf_op jit(solution)/shard_map/ppermute | solution.py:37
  174.5 1.9 collective-permute-start.56
  177.7 2.1 %collective-permute-start.57 = (bf16[2,256,256]{2,1,0:T(8,128)(2,1)S(1)}, bf16[2,256,256]{2,1,0:T(8,128)(2,1)S(1)}, u32[]{:S(2)}, u32[]{:S(2)}) collective-permute-start(bf16[2,256,256]{2,1,0:T(8,128)(2,1)S(1)} %get-tuple-element.147), channel_id=1, source_target_pairs={{0,32},{1,9},{2,34},{3,11},{4,36},{5,13},{6,38},{7,15},{8,40},{9,1... | collective-permute-start | bytes 786440 | tf_op jit(solution)/shard_map/ppermute | solution.py:37
  181.6 2.9 %collective-permute-start.51 = (bf16[2,256,256]{2,1,0:T(8,128)(2,1)}, bf16[2,256,256]{2,1,0:T(8,128)(2,1)S(1)}, u32[]{:S(2)}, u32[]{:S(2)}) collective-permute-start(bf16[2,256,256]{2,1,0:T(8,128)(2,1)} %get-tuple-element.142), channel_id=1, source_target_pairs={{0,48},{1,13},{2,50},{3,15},{4,52},{5,1},{6,54},{7,3},{8,56},{9,5}... | collective-permute-start | bytes 786440 | tf_op jit(solution)/shard_map/ppermute | solution.py:37
  186.1 1.6 collective-permute-start.58
  188.6 2.2 %collective-permute-start.61 = (bf16[256,256]{1,0:T(8,128)(2,1)S(1)}, bf16[256,256]{1,0:T(8,128)(2,1)S(1)}, u32[]{:S(2)}, u32[]{:S(2)}) collective-permute-start(bf16[256,256]{1,0:T(8,128)(2,1)S(1)} %add_convert_fusion.7), channel_id=1, source_target_pairs={{0,8},{1,9},{2,10},{3,11},{4,12},{5,13},{6,14},{7,15},{8,0},{9,1},... | collective-permute-start | bytes 393224 | tf_op jit(solution)/shard_map/ppermute | solution.py:37
  190.8 4.1 %collective-permute-done.52 = bf16[2,256,256]{2,1,0:T(8,128)(2,1)S(1)} collective-permute-done((bf16[2,256,256]{2,1,0:T(8,128)(2,1)S(1)}, bf16[2,256,256]{2,1,0:T(8,128)(2,1)S(1)}, u32[]{:S(2)}, u32[]{:S(2)}) %collective-permute-start.52) | collective-permute-done | bytes 262176 | tf_op jit(solution)/shard_map/ppermute | solution.py:37
  195.1 4.5 %collective-permute-start.59 = (bf16[256,256]{1,0:T(8,128)(2,1)S(1)}, bf16[256,256]{1,0:T(8,128)(2,1)S(1)}, u32[]{:S(2)}, u32[]{:S(2)}) collective-permute-start(bf16[256,256]{1,0:T(8,128)(2,1)S(1)} %fusion.13), channel_id=1, source_target_pairs={{0,1},{1,0},{2,3},{3,2},{4,5},{5,4},{6,7},{7,6},{8,9},{9,8},{10,11... | collective-permute-start | bytes 393224 | tf_op jit(solution)/shard_map/ppermute | solution.py:37
  (162 shorter events, 31.4 us)
Async XLA Ops:
  3.1 23.4 %collective-permute-start.1 = (bf16[2,256,256]{2,1,0:T(8,128)(2,1)S(1)}, bf16[2,256,256]{2,1,0:T(8,128)(2,1)S(1)}, u32[]{:S(2)}, u32[]{:S(2)}) collective-permute-start(bf16[2,256,256]{2,1,0:T(8,128)(2,1)S(1)} %get-tuple-element.157), channel_id=1, source_target_pairs={{0,16},{1,5},{2,18},{3,7},{4,20},{5,9},{6,22},{7,11},{8,24},{9,13}... | collective-permute-start | bytes 786440 | tf_op jit(solution)/shard_map/ppermute | solution.py:37
  4.8 21.7 %collective-permute-start.2 = (bf16[2,256,256]{2,1,0:T(8,128)(2,1)S(1)}, bf16[2,256,256]{2,1,0:T(8,128)(2,1)S(1)}, u32[]{:S(2)}, u32[]{:S(2)}) collective-permute-start(bf16[2,256,256]{2,1,0:T(8,128)(2,1)S(1)} %get-tuple-element.157), channel_id=1, source_target_pairs={{0,48},{1,13},{2,50},{3,15},{4,52},{5,1},{6,54},{7,3},{8,56},{9,5}... | collective-permute-start | bytes 786440 | tf_op jit(solution)/shard_map/ppermute | solution.py:37
  6.4 20.1 %collective-permute-start.3 = (bf16[2,256,256]{2,1,0:T(8,128)(2,1)S(1)}, bf16[2,256,256]{2,1,0:T(8,128)(2,1)S(1)}, u32[]{:S(2)}, u32[]{:S(2)}) collective-permute-start(bf16[2,256,256]{2,1,0:T(8,128)(2,1)S(1)} %get-tuple-element.157), channel_id=1, source_target_pairs={{0,32},{1,9},{2,34},{3,11},{4,36},{5,13},{6,38},{7,15},{8,40},{9,1... | collective-permute-start | bytes 786440 | tf_op jit(solution)/shard_map/ppermute | solution.py:37
  8.3 18.2 %collective-permute-start.4 = (bf16[2,256,256]{2,1,0:T(8,128)(2,1)S(1)}, bf16[2,256,256]{2,1,0:T(8,128)(2,1)S(1)}, u32[]{:S(2)}, u32[]{:S(2)}) collective-permute-start(bf16[2,256,256]{2,1,0:T(8,128)(2,1)S(1)} %get-tuple-element.157), channel_id=1, source_target_pairs={{0,64},{1,65},{2,66},{3,67},{4,68},{5,69},{6,70},{7,71},{8,72},{9,... | collective-permute-start | bytes 786440 | tf_op jit(solution)/shard_map/ppermute | solution.py:37
  27.1 6.0 %collective-permute-start.11 = (f32[16,128]{1,0:T(8,128)S(1)}, f32[16,128]{1,0:T(8,128)S(1)}, u32[]{:S(2)}, u32[]{:S(2)}) collective-permute-start(f32[16,128]{1,0:T(8,128)S(1)} %get-tuple-element.81), channel_id=1, source_target_pairs={{0,1},{1,0},{2,3},{3,2},{4,5},{5,4},{6,7},{7,6},{8,9},{9,8},{10,11... | collective-permute-start | bytes 24584 | tf_op jit(solution)/shard_map/ppermute | solution.py:37
  27.6 14.1 %collective-permute-start.10 = (bf16[2,256,256]{2,1,0:T(8,128)(2,1)S(1)}, bf16[2,256,256]{2,1,0:T(8,128)(2,1)S(1)}, u32[]{:S(2)}, u32[]{:S(2)}) collective-permute-start(bf16[2,256,256]{2,1,0:T(8,128)(2,1)S(1)} %collective-permute-done.4), channel_id=1, source_target_pairs={{0,32},{1,9},{2,34},{3,11},{4,36},{5,13},{6,38},{7,15},{8,40},{9,1... | collective-permute-start | bytes 786440 | tf_op jit(solution)/shard_map/ppermute | solution.py:37
  29.8 11.8 %collective-permute-start.8 = (bf16[2,256,256]{2,1,0:T(8,128)(2,1)S(1)}, bf16[2,256,256]{2,1,0:T(8,128)(2,1)S(1)}, u32[]{:S(2)}, u32[]{:S(2)}) collective-permute-start(bf16[2,256,256]{2,1,0:T(8,128)(2,1)S(1)} %collective-permute-done.4), channel_id=1, source_target_pairs={{0,16},{1,5},{2,18},{3,7},{4,20},{5,9},{6,22},{7,11},{8,24},{9,13}... | collective-permute-start | bytes 786440 | tf_op jit(solution)/shard_map/ppermute | solution.py:37
  30.4 11.3 %collective-permute-start.9 = (bf16[2,256,256]{2,1,0:T(8,128)(2,1)S(1)}, bf16[2,256,256]{2,1,0:T(8,128)(2,1)S(1)}, u32[]{:S(2)}, u32[]{:S(2)}) collective-permute-start(bf16[2,256,256]{2,1,0:T(8,128)(2,1)S(1)} %collective-permute-done.4), channel_id=1, source_target_pairs={{0,48},{1,13},{2,50},{3,15},{4,52},{5,1},{6,54},{7,3},{8,56},{9,5}... | collective-permute-start | bytes 786440 | tf_op jit(solution)/shard_map/ppermute | solution.py:37
  36.9 18.5 %collective-permute-start.5 = (bf16[2,1024,256]{2,1,0:T(8,128)(2,1)S(1)}, bf16[2,1024,256]{2,1,0:T(8,128)(2,1)S(1)}, u32[]{:S(2)}, u32[]{:S(2)}) collective-permute-start(bf16[2,1024,256]{2,1,0:T(8,128)(2,1)S(1)} %bitcast.99), channel_id=1, source_target_pairs={{0,4},{1,17},{2,6},{3,19},{4,8},{5,21},{6,10},{7,23},{8,12},{9,25}... | collective-permute-start | bytes 3145736 | tf_op jit(solution)/shard_map/ppermute | solution.py:37
  38.3 17.1 %collective-permute-start.6 = (bf16[2,1024,256]{2,1,0:T(8,128)(2,1)S(1)}, bf16[2,1024,256]{2,1,0:T(8,128)(2,1)S(1)}, u32[]{:S(2)}, u32[]{:S(2)}) collective-permute-start(bf16[2,1024,256]{2,1,0:T(8,128)(2,1)S(1)} %bitcast.100), channel_id=1, source_target_pairs={{0,12},{1,49},{2,14},{3,51},{4,0},{5,53},{6,2},{7,55},{8,4},{9,57}... | collective-permute-start | bytes 3145736 | tf_op jit(solution)/shard_map/ppermute | solution.py:37
  45.6 18.8 %collective-permute-start.17 = (bf16[2,1024,256]{2,1,0:T(8,128)(2,1)S(1)}, bf16[2,1024,256]{2,1,0:T(8,128)(2,1)S(1)}, u32[]{:S(2)}, u32[]{:S(2)}) collective-permute-start(bf16[2,1024,256]{2,1,0:T(8,128)(2,1)S(1)} %bitcast.102), channel_id=1, source_target_pairs={{0,4},{1,17},{2,6},{3,19},{4,8},{5,21},{6,10},{7,23},{8,12},{9,25}... | collective-permute-start | bytes 3145736 | tf_op jit(solution)/shard_map/ppermute | solution.py:37
  45.7 18.7 %collective-permute-start.18 = (bf16[2,1024,256]{2,1,0:T(8,128)(2,1)S(1)}, bf16[2,1024,256]{2,1,0:T(8,128)(2,1)S(1)}, u32[]{:S(2)}, u32[]{:S(2)}) collective-permute-start(bf16[2,1024,256]{2,1,0:T(8,128)(2,1)S(1)} %bitcast.103), channel_id=1, source_target_pairs={{0,12},{1,49},{2,14},{3,51},{4,0},{5,53},{6,2},{7,55},{8,4},{9,57}... | collective-permute-start | bytes 3145736 | tf_op jit(solution)/shard_map/ppermute | solution.py:37
  56.4 13.6 %collective-permute-start.15 = (bf16[1024,256]{1,0:T(8,128)(2,1)S(1)}, bf16[1024,256]{1,0:T(8,128)(2,1)S(1)}, u32[]{:S(2)}, u32[]{:S(2)}) collective-permute-start(bf16[1024,256]{1,0:T(8,128)(2,1)S(1)} %slice_bitcast_fusion.4), channel_id=1, source_target_pairs={{0,12},{1,49},{2,14},{3,51},{4,0},{5,53},{6,2},{7,55},{8,4},{9,57}... | collective-permute-start | bytes 1572872 | tf_op jit(solution)/shard_map/ppermute | solution.py:37
  64.5 6.8 %collective-permute-start.24 = (bf16[1024,256]{1,0:T(8,128)(2,1)S(1)}, bf16[1024,256]{1,0:T(8,128)(2,1)S(1)}, u32[]{:S(2)}, u32[]{:S(2)}) collective-permute-start(bf16[1024,256]{1,0:T(8,128)(2,1)S(1)} %get-tuple-element.148), channel_id=1, source_target_pairs={{0,1},{1,0},{2,3},{3,2},{4,5},{5,4},{6,7},{7,6},{8,9},{9,8},{10,11... | collective-permute-start | bytes 1572872 | tf_op jit(solution)/shard_map/ppermute | solution.py:37
  64.6 11.0 %collective-permute-start.22 = (bf16[1024,256]{1,0:T(8,128)(2,1)S(1)}, bf16[1024,256]{1,0:T(8,128)(2,1)S(1)}, u32[]{:S(2)}, u32[]{:S(2)}) collective-permute-start(bf16[1024,256]{1,0:T(8,128)(2,1)S(1)} %slice_bitcast_fusion.1), channel_id=1, source_target_pairs={{0,12},{1,49},{2,14},{3,51},{4,0},{5,53},{6,2},{7,55},{8,4},{9,57}... | collective-permute-start | bytes 1572872 | tf_op jit(solution)/shard_map/ppermute | solution.py:37
  68.4 7.3 %collective-permute-start.25 = (bf16[1024,256]{1,0:T(8,128)(2,1)S(1)}, bf16[1024,256]{1,0:T(8,128)(2,1)S(1)}, u32[]{:S(2)}, u32[]{:S(2)}) collective-permute-start(bf16[1024,256]{1,0:T(8,128)(2,1)S(1)} %slice_bitcast_fusion.1), channel_id=1, source_target_pairs={{0,1},{1,0},{2,3},{3,2},{4,5},{5,4},{6,7},{7,6},{8,9},{9,8},{10,11... | collective-permute-start | bytes 1572872 | tf_op jit(solution)/shard_map/ppermute | solution.py:37
  68.4 13.4 %collective-permute-start.14 = (bf16[1024,256]{1,0:T(8,128)(2,1)S(1)}, bf16[1024,256]{1,0:T(8,128)(2,1)S(1)}, u32[]{:S(2)}, u32[]{:S(2)}) collective-permute-start(bf16[1024,256]{1,0:T(8,128)(2,1)S(1)} %get-tuple-element.151), channel_id=1, source_target_pairs={{0,4},{1,17},{2,6},{3,19},{4,8},{5,21},{6,10},{7,23},{8,12},{9,25}... | collective-permute-start | bytes 1572872 | tf_op jit(solution)/shard_map/ppermute | solution.py:37
  70.0 14.4 %collective-permute-start.21 = (bf16[1024,256]{1,0:T(8,128)(2,1)S(1)}, bf16[1024,256]{1,0:T(8,128)(2,1)S(1)}, u32[]{:S(2)}, u32[]{:S(2)}) collective-permute-start(bf16[1024,256]{1,0:T(8,128)(2,1)S(1)} %get-tuple-element.149), channel_id=1, source_target_pairs={{0,4},{1,17},{2,6},{3,19},{4,8},{5,21},{6,10},{7,23},{8,12},{9,25}... | collective-permute-start | bytes 1572872 | tf_op jit(solution)/shard_map/ppermute | solution.py:37
  71.3 13.1 %collective-permute-start.16 = (bf16[1024,256]{1,0:T(8,128)(2,1)S(1)}, bf16[1024,256]{1,0:T(8,128)(2,1)S(1)}, u32[]{:S(2)}, u32[]{:S(2)}) collective-permute-start(bf16[1024,256]{1,0:T(8,128)(2,1)S(1)} %collective-permute-done.15), channel_id=1, source_target_pairs={{0,1},{1,0},{2,3},{3,2},{4,5},{5,4},{6,7},{7,6},{8,9},{9,8},{10,11... | collective-permute-start | bytes 1572872 | tf_op jit(solution)/shard_map/ppermute | solution.py:37
  75.6 8.8 %collective-permute-start.23 = (bf16[1024,256]{1,0:T(8,128)(2,1)S(1)}, bf16[1024,256]{1,0:T(8,128)(2,1)S(1)}, u32[]{:S(2)}, u32[]{:S(2)}) collective-permute-start(bf16[1024,256]{1,0:T(8,128)(2,1)S(1)} %collective-permute-done.22), channel_id=1, source_target_pairs={{0,1},{1,0},{2,3},{3,2},{4,5},{5,4},{6,7},{7,6},{8,9},{9,8},{10,11... | collective-permute-start | bytes 1572872 | tf_op jit(solution)/shard_map/ppermute | solution.py:37
  90.7 9.9 %collective-permute-start.27 = (bf16[512,256]{1,0:T(8,128)(2,1)S(1)}, bf16[512,256]{1,0:T(8,128)(2,1)S(1)}, u32[]{:S(2)}, u32[]{:S(2)}) collective-permute-start(bf16[512,256]{1,0:T(8,128)(2,1)S(1)} %fusion.12), channel_id=1, source_target_pairs={{0,2},{1,3},{2,0},{3,1},{4,6},{5,7},{6,4},{7,5},{8,10},{9,11},{10,... | collective-permute-start | bytes 786440 | tf_op jit(solution)/shard_map/ppermute | solution.py:37
  101.9 9.0 %collective-permute-start.28 = (bf16[512,256]{1,0:T(8,128)(2,1)S(1)}, bf16[512,256]{1,0:T(8,128)(2,1)S(1)}, u32[]{:S(2)}, u32[]{:S(2)}) collective-permute-start(bf16[512,256]{1,0:T(8,128)(2,1)S(1)} %get-tuple-element.97.own), channel_id=1, source_target_pairs={{0,2},{1,3},{2,0},{3,1},{4,6},{5,7},{6,4},{7,5},{8,10},{9,11},{10,... | collective-permute-start | bytes 786440 | tf_op jit(solution)/shard_map/ppermute | solution.py:37
  105.1 6.5 %collective-permute-start.29 = (bf16[512,256]{1,0:T(8,128)(2,1)S(1)}, bf16[512,256]{1,0:T(8,128)(2,1)S(1)}, u32[]{:S(2)}, u32[]{:S(2)}) collective-permute-start(bf16[512,256]{1,0:T(8,128)(2,1)S(1)} %get-tuple-element.97.own), channel_id=1, source_target_pairs={{0,1},{1,0},{2,3},{3,2},{4,5},{5,4},{6,7},{7,6},{8,9},{9,8},{10,11... | collective-permute-start | bytes 786440 | tf_op jit(solution)/shard_map/ppermute | solution.py:37
  117.1 7.5 %collective-permute-start.38 = (bf16[256,256]{1,0:T(8,128)(2,1)S(1)}, bf16[256,256]{1,0:T(8,128)(2,1)S(1)}, u32[]{:S(2)}, u32[]{:S(2)}) collective-permute-start(bf16[256,256]{1,0:T(8,128)(2,1)S(1)} %add_convert_fusion.8), channel_id=1, source_target_pairs={{0,2},{1,3},{2,0},{3,1},{4,6},{5,7},{6,4},{7,5},{8,10},{9,11},{10,... | collective-permute-start | bytes 393224 | tf_op jit(solution)/shard_map/ppermute | solution.py:37
  120.4 15.7 %collective-permute-start.34 = (bf16[1024,256]{1,0:T(8,128)(2,1)S(1)}, bf16[1024,256]{1,0:T(8,128)(2,1)S(1)}, u32[]{:S(2)}, u32[]{:S(2)}) collective-permute-start(bf16[1024,256]{1,0:T(8,128)(2,1)S(1)} %get-tuple-element.112), channel_id=1, source_target_pairs={{0,4},{1,17},{2,6},{3,19},{4,8},{5,21},{6,10},{7,23},{8,12},{9,25}... | collective-permute-start | bytes 1572872 | tf_op jit(solution)/shard_map/ppermute | solution.py:37
  120.8 14.2 %collective-permute-start.32 = (bf16[1024,256]{1,0:T(8,128)(2,1)S(1)}, bf16[1024,256]{1,0:T(8,128)(2,1)S(1)}, u32[]{:S(2)}, u32[]{:S(2)}) collective-permute-start(bf16[1024,256]{1,0:T(8,128)(2,1)S(1)} %get-tuple-element.107), channel_id=1, source_target_pairs={{0,1},{1,0},{2,3},{3,2},{4,5},{5,4},{6,7},{7,6},{8,9},{9,8},{10,11... | collective-permute-start | bytes 1572872 | tf_op jit(solution)/shard_map/ppermute | solution.py:37
  121.3 14.8 %collective-permute-start.36 = (bf16[1024,256]{1,0:T(8,128)(2,1)S(1)}, bf16[1024,256]{1,0:T(8,128)(2,1)S(1)}, u32[]{:S(2)}, u32[]{:S(2)}) collective-permute-start(bf16[1024,256]{1,0:T(8,128)(2,1)S(1)} %collective-permute-done.35), channel_id=1, source_target_pairs={{0,12},{1,49},{2,14},{3,51},{4,0},{5,53},{6,2},{7,55},{8,4},{9,57}... | collective-permute-start | bytes 1572872 | tf_op jit(solution)/shard_map/ppermute | solution.py:37
  124.6 21.6 %collective-permute-start.31 = (bf16[1024,256]{1,0:T(8,128)(2,1)S(1)}, bf16[1024,256]{1,0:T(8,128)(2,1)S(1)}, u32[]{:S(2)}, u32[]{:S(2)}) collective-permute-start(bf16[1024,256]{1,0:T(8,128)(2,1)S(1)} %get-tuple-element.106), channel_id=1, source_target_pairs={{0,4},{1,17},{2,6},{3,19},{4,8},{5,21},{6,10},{7,23},{8,12},{9,25}... | collective-permute-start | bytes 1572872 | tf_op jit(solution)/shard_map/ppermute | solution.py:37
  135.0 11.2 %collective-permute-start.33 = (bf16[1024,256]{1,0:T(8,128)(2,1)S(1)}, bf16[1024,256]{1,0:T(8,128)(2,1)S(1)}, u32[]{:S(2)}, u32[]{:S(2)}) collective-permute-start(bf16[1024,256]{1,0:T(8,128)(2,1)S(1)} %collective-permute-done.32), channel_id=1, source_target_pairs={{0,12},{1,49},{2,14},{3,51},{4,0},{5,53},{6,2},{7,55},{8,4},{9,57}... | collective-permute-start | bytes 1572872 | tf_op jit(solution)/shard_map/ppermute | solution.py:37
  136.1 12.5 %collective-permute-start.48 = (bf16[1024,256]{1,0:T(8,128)(2,1)S(1)}, bf16[1024,256]{1,0:T(8,128)(2,1)S(1)}, u32[]{:S(2)}, u32[]{:S(2)}) collective-permute-start(bf16[1024,256]{1,0:T(8,128)(2,1)S(1)} %get-tuple-element.129), channel_id=1, source_target_pairs={{0,1},{1,0},{2,3},{3,2},{4,5},{5,4},{6,7},{7,6},{8,9},{9,8},{10,11... | collective-permute-start | bytes 1572872 | tf_op jit(solution)/shard_map/ppermute | solution.py:37
  141.2 9.2 %collective-permute-start.46 = (bf16[1024,256]{1,0:T(8,128)(2,1)S(1)}, bf16[1024,256]{1,0:T(8,128)(2,1)S(1)}, u32[]{:S(2)}, u32[]{:S(2)}) collective-permute-start(bf16[1024,256]{1,0:T(8,128)(2,1)S(1)} %get-tuple-element.127), channel_id=1, source_target_pairs={{0,1},{1,0},{2,3},{3,2},{4,5},{5,4},{6,7},{7,6},{8,9},{9,8},{10,11... | collective-permute-start | bytes 1572872 | tf_op jit(solution)/shard_map/ppermute | solution.py:37
  148.0 8.2 %collective-permute-start.42 = (bf16[1024,256]{1,0:T(8,128)(2,1)S(1)}, bf16[1024,256]{1,0:T(8,128)(2,1)S(1)}, u32[]{:S(2)}, u32[]{:S(2)}) collective-permute-start(bf16[1024,256]{1,0:T(8,128)(2,1)S(1)} %get-tuple-element.121), channel_id=1, source_target_pairs={{0,1},{1,0},{2,3},{3,2},{4,5},{5,4},{6,7},{7,6},{8,9},{9,8},{10,11... | collective-permute-start | bytes 1572872 | tf_op jit(solution)/shard_map/ppermute | solution.py:37
  148.8 14.9 %collective-permute-start.49 = (bf16[2,1024,256]{2,1,0:T(8,128)(2,1)S(1)}, bf16[2,1024,256]{2,1,0:T(8,128)(2,1)S(1)}, u32[]{:S(2)}, u32[]{:S(2)}) collective-permute-start(bf16[2,1024,256]{2,1,0:T(8,128)(2,1)S(1)} %pad_maximum_fusion.5), channel_id=1, source_target_pairs={{0,12},{1,49},{2,14},{3,51},{4,0},{5,53},{6,2},{7,55},{8,4},{9,57}... | collective-permute-start | bytes 3145736 | tf_op jit(solution)/shard_map/ppermute | solution.py:37
  150.5 16.1 %collective-permute-start.47 = (bf16[2,1024,256]{2,1,0:T(8,128)(2,1)S(1)}, bf16[2,1024,256]{2,1,0:T(8,128)(2,1)S(1)}, u32[]{:S(2)}, u32[]{:S(2)}) collective-permute-start(bf16[2,1024,256]{2,1,0:T(8,128)(2,1)S(1)} %pad_maximum_fusion.4), channel_id=1, source_target_pairs={{0,4},{1,17},{2,6},{3,19},{4,8},{5,21},{6,10},{7,23},{8,12},{9,25}... | collective-permute-start | bytes 3145736 | tf_op jit(solution)/shard_map/ppermute | solution.py:37
  151.4 15.8 %collective-permute-start.54 = (bf16[1024,256]{1,0:T(8,128)(2,1)S(1)}, bf16[1024,256]{1,0:T(8,128)(2,1)S(1)}, u32[]{:S(2)}, u32[]{:S(2)}) collective-permute-start(bf16[1024,256]{1,0:T(8,128)(2,1)S(1)} %get-tuple-element.136), channel_id=1, source_target_pairs={{0,1},{1,0},{2,3},{3,2},{4,5},{5,4},{6,7},{7,6},{8,9},{9,8},{10,11... | collective-permute-start | bytes 1572872 | tf_op jit(solution)/shard_map/ppermute | solution.py:37
  151.8 25.9 %collective-permute-start.45 = (bf16[2,1024,256]{2,1,0:T(8,128)(2,1)S(1)}, bf16[2,1024,256]{2,1,0:T(8,128)(2,1)S(1)}, u32[]{:S(2)}, u32[]{:S(2)}) collective-permute-start(bf16[2,1024,256]{2,1,0:T(8,128)(2,1)S(1)} %pad_maximum_fusion.3), channel_id=1, source_target_pairs={{0,12},{1,49},{2,14},{3,51},{4,0},{5,53},{6,2},{7,55},{8,4},{9,57}... | collective-permute-start | bytes 3145736 | tf_op jit(solution)/shard_map/ppermute | solution.py:37
  156.4 23.5 %collective-permute-start.43 = (bf16[2,1024,256]{2,1,0:T(8,128)(2,1)S(1)}, bf16[2,1024,256]{2,1,0:T(8,128)(2,1)S(1)}, u32[]{:S(2)}, u32[]{:S(2)}) collective-permute-start(bf16[2,1024,256]{2,1,0:T(8,128)(2,1)S(1)} %pad_maximum_fusion.2), channel_id=1, source_target_pairs={{0,4},{1,17},{2,6},{3,19},{4,8},{5,21},{6,10},{7,23},{8,12},{9,25}... | collective-permute-start | bytes 3145736 | tf_op jit(solution)/shard_map/ppermute | solution.py:37
  163.7 16.7 %collective-permute-start.41 = (bf16[1024,256]{1,0:T(8,128)(2,1)S(1)}, bf16[1024,256]{1,0:T(8,128)(2,1)S(1)}, u32[]{:S(2)}, u32[]{:S(2)}) collective-permute-start(bf16[1024,256]{1,0:T(8,128)(2,1)S(1)} %get-tuple-element.118), channel_id=1, source_target_pairs={{0,1},{1,0},{2,3},{3,2},{4,5},{5,4},{6,7},{7,6},{8,9},{9,8},{10,11... | collective-permute-start | bytes 1572872 | tf_op jit(solution)/shard_map/ppermute | solution.py:37
  166.6 7.9 %collective-permute-start.50 = (bf16[256,256]{1,0:T(8,128)(2,1)S(1)}, bf16[256,256]{1,0:T(8,128)(2,1)S(1)}, u32[]{:S(2)}, u32[]{:S(2)}) collective-permute-start(bf16[256,256]{1,0:T(8,128)(2,1)S(1)} %convert_add_fusion.3), channel_id=1, source_target_pairs={{0,32},{1,33},{2,34},{3,35},{4,36},{5,37},{6,38},{7,39},{8,40},{9,... | collective-permute-start | bytes 393224 | tf_op jit(solution)/shard_map/ppermute | solution.py:37
  167.7 16.8 %collective-permute-start.55 = (bf16[2,256,256]{2,1,0:T(8,128)(2,1)S(1)}, bf16[2,256,256]{2,1,0:T(8,128)(2,1)S(1)}, u32[]{:S(2)}, u32[]{:S(2)}) collective-permute-start(bf16[2,256,256]{2,1,0:T(8,128)(2,1)S(1)} %get-tuple-element.145), channel_id=1, source_target_pairs={{0,48},{1,13},{2,50},{3,15},{4,52},{5,1},{6,54},{7,3},{8,56},{9,5}... | collective-permute-start | bytes 786440 | tf_op jit(solution)/shard_map/ppermute | solution.py:37
  174.5 11.2 %collective-permute-start.56 = (bf16[2,256,256]{2,1,0:T(8,128)(2,1)S(1)}, bf16[2,256,256]{2,1,0:T(8,128)(2,1)S(1)}, u32[]{:S(2)}, u32[]{:S(2)}) collective-permute-start(bf16[2,256,256]{2,1,0:T(8,128)(2,1)S(1)} %get-tuple-element.146), channel_id=1, source_target_pairs={{0,16},{1,5},{2,18},{3,7},{4,20},{5,9},{6,22},{7,11},{8,24},{9,13}... | collective-permute-start | bytes 786440 | tf_op jit(solution)/shard_map/ppermute | solution.py:37
  177.7 8.2 %collective-permute-start.57 = (bf16[2,256,256]{2,1,0:T(8,128)(2,1)S(1)}, bf16[2,256,256]{2,1,0:T(8,128)(2,1)S(1)}, u32[]{:S(2)}, u32[]{:S(2)}) collective-permute-start(bf16[2,256,256]{2,1,0:T(8,128)(2,1)S(1)} %get-tuple-element.147), channel_id=1, source_target_pairs={{0,32},{1,9},{2,34},{3,11},{4,36},{5,13},{6,38},{7,15},{8,40},{9,1... | collective-permute-start | bytes 786440 | tf_op jit(solution)/shard_map/ppermute | solution.py:37
  179.8 7.9 %collective-permute-start.60 = (bf16[256,256]{1,0:T(8,128)(2,1)S(1)}, bf16[256,256]{1,0:T(8,128)(2,1)}, u32[]{:S(2)}, u32[]{:S(2)}) collective-permute-start(bf16[256,256]{1,0:T(8,128)(2,1)S(1)} %convert_add_fusion.2), channel_id=1, source_target_pairs={{0,4},{1,5},{2,6},{3,7},{4,0},{5,1},{6,2},{7,3},{8,12},{9,13},{10,... | collective-permute-start | bytes 393224 | tf_op jit(solution)/shard_map/ppermute | solution.py:37
  181.6 9.3 %collective-permute-start.51 = (bf16[2,256,256]{2,1,0:T(8,128)(2,1)}, bf16[2,256,256]{2,1,0:T(8,128)(2,1)S(1)}, u32[]{:S(2)}, u32[]{:S(2)}) collective-permute-start(bf16[2,256,256]{2,1,0:T(8,128)(2,1)} %get-tuple-element.142), channel_id=1, source_target_pairs={{0,48},{1,13},{2,50},{3,15},{4,52},{5,1},{6,54},{7,3},{8,56},{9,5}... | collective-permute-start | bytes 786440 | tf_op jit(solution)/shard_map/ppermute | solution.py:37
  184.5 10.4 %collective-permute-start.52 = (bf16[2,256,256]{2,1,0:T(8,128)(2,1)S(1)}, bf16[2,256,256]{2,1,0:T(8,128)(2,1)S(1)}, u32[]{:S(2)}, u32[]{:S(2)}) collective-permute-start(bf16[2,256,256]{2,1,0:T(8,128)(2,1)S(1)} %get-tuple-element.143), channel_id=1, source_target_pairs={{0,16},{1,5},{2,18},{3,7},{4,20},{5,9},{6,22},{7,11},{8,24},{9,13}... | collective-permute-start | bytes 786440 | tf_op jit(solution)/shard_map/ppermute | solution.py:37
  185.7 9.2 %collective-permute-start.53 = (bf16[2,256,256]{2,1,0:T(8,128)(2,1)S(1)}, bf16[2,256,256]{2,1,0:T(8,128)(2,1)S(1)}, u32[]{:S(2)}, u32[]{:S(2)}) collective-permute-start(bf16[2,256,256]{2,1,0:T(8,128)(2,1)S(1)} %get-tuple-element.144), channel_id=1, source_target_pairs={{0,32},{1,9},{2,34},{3,11},{4,36},{5,13},{6,38},{7,15},{8,40},{9,1... | collective-permute-start | bytes 786440 | tf_op jit(solution)/shard_map/ppermute | solution.py:37
  186.1 8.8 %collective-permute-start.58 = (bf16[2,256,256]{2,1,0:T(8,128)(2,1)S(1)}, bf16[2,256,256]{2,1,0:T(8,128)(2,1)S(1)}, u32[]{:S(2)}, u32[]{:S(2)}) collective-permute-start(bf16[2,256,256]{2,1,0:T(8,128)(2,1)S(1)} %fusion.7), channel_id=1, source_target_pairs={{0,64},{1,65},{2,66},{3,67},{4,68},{5,69},{6,70},{7,71},{8,72},{9,... | collective-permute-start | bytes 786440 | tf_op jit(solution)/shard_map/ppermute | solution.py:37
  188.6 11.0 %collective-permute-start.61 = (bf16[256,256]{1,0:T(8,128)(2,1)S(1)}, bf16[256,256]{1,0:T(8,128)(2,1)S(1)}, u32[]{:S(2)}, u32[]{:S(2)}) collective-permute-start(bf16[256,256]{1,0:T(8,128)(2,1)S(1)} %add_convert_fusion.7), channel_id=1, source_target_pairs={{0,8},{1,9},{2,10},{3,11},{4,12},{5,13},{6,14},{7,15},{8,0},{9,1},... | collective-permute-start | bytes 393224 | tf_op jit(solution)/shard_map/ppermute | solution.py:37
  (25 other events, 178.5 us)

commit v3 on v2

v3 whole, which is shorter than its diff:
```python
import functools

import jax
import jax.numpy as jnp
from jax import lax
from jax.experimental import pallas as pl
from jax.experimental.pallas import tpu as pltpu
from jax.sharding import PartitionSpec as P

TILE = 128
GROUP = 16
DEPTH = 4
CLASSES = 5
CLASS_BLOCKS = 32
BLOCK_TILES = 16
BOTH = ("row", "rep")
MIB = 1024 * 1024


def pairs(step):
    out = []
    for z in range(2):
        for x in range(4):
            for y in range(4):
                for h in range(2):
                    for c in range(2):
                        src = (z * 16 + x * 4 + y) * 4 + h * 2 + c
                        z2, x2, y2, h2, c2 = step(z, x, y, h, c)
                        dst = ((z2 % 2) * 16 + (x2 % 4) * 4 + y2 % 4) * 4 + (h2 % 2) * 2 + c2 % 2
                        out.append((src, dst))
    return out


def move(value, step):
    return lax.ppermute(value, BOTH, pairs(step))


def swap_core(value):
    return move(value, lambda z, x, y, h, c: (z, x, y, h, c + 1))


def swap_high(value):
    return move(value, lambda z, x, y, h, c: (z, x, y, h + 1, c))


def swap_low(value):
    return move(value, lambda z, x, y, h, c: (z + 1, x, y, h, c))


def swap_x(value):
    return move(value, lambda z, x, y, h, c: (z, x ^ 1, y, h, c))


def swap_xx(value):
    return move(value, lambda z, x, y, h, c: (z, x + 2, y, h, c))


def swap_y(value):
    return move(value, lambda z, x, y, h, c: (z, x, y ^ 1, h, c))


def swap_yy(value):
    return move(value, lambda z, x, y, h, c: (z, x, y + 2, h, c))


def move_p(value, by):
    return move(value, lambda z, x, y, h, c: (z, x + by, y, h, c) if c == 0 else (z, x, y + by, h, c))


def move_q(value, by):
    return move(value, lambda z, x, y, h, c: (z, x, y + by, h, c) if c == 0 else (z, x + by, y, h, c))


def params(mib):
    return pltpu.CompilerParams(vmem_limit_bytes=mib * MIB)


def degree_kernel(first, rows_ref, masks_ref, tiles_ref, degree_ref, sums, buf, sems):
    count = tiles_ref.shape[0] // BLOCK_TILES

    def fetch(group):
        source = masks_ref.at[pl.ds(first + group * BLOCK_TILES, BLOCK_TILES)]
        slot = lax.rem(group, DEPTH)
        return pltpu.make_async_copy(source, buf.at[slot], sems.at[slot])

    for group in range(DEPTH - 1):
        fetch(group).start()
    sums[...] = jnp.zeros_like(sums)

    def turn(group, carry):
        @pl.when(group + DEPTH - 1 < count)
        def _():
            fetch(group + DEPTH - 1).start()

        fetch(group).wait()
        slot = lax.rem(group, DEPTH)
        for k in range(BLOCK_TILES):
            mask = buf[slot, k].astype(jnp.float32)
            row = rows_ref[first + group * BLOCK_TILES + k]
            sums[row] += mask
            tiles_ref[pl.ds(group * BLOCK_TILES + k, 1), :] = jnp.sum(mask, axis=0, keepdims=True)
        return carry

    lax.fori_loop(0, count, turn, 0)
    for r in range(degree_ref.shape[0]):
        degree_ref[pl.ds(r, 1), :] = jnp.sum(sums[r].T, axis=0, keepdims=True)


def degrees(part, parts, tile_rows, tile_masks, block_count):
    slots = tile_masks.shape[0] // parts
    vmem = pl.BlockSpec(memory_space=pltpu.VMEM)
    return pl.pallas_call(
        functools.partial(degree_kernel, part * slots),
        in_specs=[pl.BlockSpec(memory_space=pltpu.SMEM), pl.BlockSpec(memory_space=pltpu.HBM)],
        out_specs=[vmem, vmem],
        out_shape=[
            jax.ShapeDtypeStruct((slots, TILE), jnp.float32),
            jax.ShapeDtypeStruct((block_count, TILE), jnp.float32),
        ],
        scratch_shapes=[
            pltpu.VMEM((block_count, TILE, TILE), jnp.float32),
            pltpu.VMEM((DEPTH, BLOCK_TILES, TILE, TILE), jnp.int32),
            pltpu.SemaphoreType.DMA((DEPTH,)),
        ],
        compiler_params=params(41),
        cost_estimate=pl.CostEstimate(flops=0, bytes_accessed=20 * MIB, transcendentals=0),
        name=f"degrees{part}",
    )(tile_rows, tile_masks)


def unpack(meta):
    return meta & 1023, (meta >> 10) & 31, meta >> 15


def as_bf16(mask):
    return mask.astype(jnp.float32).astype(jnp.bfloat16)


def each_group(first, last, meta_ref, masks_ref, buf, sems, body):
    def fetch(group):
        slot = lax.rem(group, DEPTH)
        for u in range(GROUP):
            tile = unpack(meta_ref[group * GROUP + u])[0]
            pltpu.make_async_copy(masks_ref.at[tile], buf.at[slot, u], sems.at[slot]).start()

    for ahead in range(DEPTH - 1):

        @pl.when(first + ahead < last)
        def _():
            fetch(first + ahead)

    def turn(group, carry):
        @pl.when(group + DEPTH - 1 < last)
        def _():
            fetch(group + DEPTH - 1)

        slot = lax.rem(group, DEPTH)
        pltpu.make_async_copy(masks_ref.at[pl.ds(0, GROUP)], buf.at[slot], sems.at[slot]).wait()
        body(group, slot)
        return carry

    lax.fori_loop(first, last, turn, 0)


def forward_kernel(begin, end, count, first_call, last_call, meta_ref, bounds_ref, masks_ref, *refs):
    pieces = refs[:count]
    refs = refs[count:]
    before = None
    if not first_call:
        before, refs = refs[0], refs[1:]
    if last_call:
        keep_ref, give_ref, feats, buf, sems, total = refs
    else:
        total, feats, buf, sems = refs
    start = 0
    for piece in pieces:
        feats[start : start + piece.shape[0], :] = piece[...]
        start += piece.shape[0]
    total[...] = jnp.zeros_like(total) if first_call else before[...]

    def body(group, slot):
        for u in range(GROUP):
            _, row, block = unpack(meta_ref[group * GROUP + u])
            part = jnp.dot(
                as_bf16(buf[slot, u]),
                feats[pl.ds(pl.multiple_of(block * TILE, TILE), TILE), :],
                preferred_element_type=jnp.float32,
            )
            total[pl.ds(pl.multiple_of(row * TILE, TILE), TILE), :] += part

    each_group(bounds_ref[begin], bounds_ref[end], meta_ref, masks_ref, buf, sems, body)
    if last_call:
        quarter = keep_ref.shape[1]
        core, high = bounds_ref[CLASSES + 1], bounds_ref[CLASSES + 2]
        for h in range(2):
            side = (high + h) % 2
            kept = pl.multiple_of((side * 2 + core) * quarter, quarter)
            given = pl.multiple_of((side * 2 + 1 - core) * quarter, quarter)
            keep_ref[h] = total[pl.ds(kept, quarter), :].astype(jnp.bfloat16)
            give_ref[h] = total[pl.ds(given, quarter), :].astype(jnp.bfloat16)


def forward_class(begin, end, meta, bounds, masks, pieces, before, row_blocks):
    width = pieces[0].shape[-1]
    first_call, last_call = before is None, end == CLASSES

    total_rows = (row_blocks + 1) * TILE
    feat_rows = (CLASS_BLOCKS + 1) * TILE
    scratch = [
        pltpu.VMEM((feat_rows, width), jnp.bfloat16),
        pltpu.VMEM((DEPTH, GROUP, TILE, TILE), jnp.int32),
        pltpu.SemaphoreType.DMA((DEPTH,)),
    ]
    vmem = pl.BlockSpec(memory_space=pltpu.VMEM)
    if last_call:
        half = jax.ShapeDtypeStruct((2, row_blocks * TILE // 4, width), jnp.bfloat16)
        out_shape, out_specs = [half, half], [vmem, vmem]
        scratch.append(pltpu.VMEM((total_rows, width), jnp.float32))
    else:
        out_shape, out_specs = jax.ShapeDtypeStruct((total_rows, width), jnp.float32), vmem
    smem = pl.BlockSpec(memory_space=pltpu.SMEM)
    held = pl.BlockSpec(memory_space=pltpu.HBM)
    extra = [] if first_call else [before]
    aliases = {} if first_call or last_call else {3 + len(pieces): 0}
    return pl.pallas_call(
        functools.partial(forward_kernel, begin, end, len(pieces), first_call, last_call),
        in_specs=[smem, smem, held] + [vmem] * (len(pieces) + len(extra)),
        out_specs=out_specs,
        out_shape=out_shape,
        scratch_shapes=scratch,
        input_output_aliases=aliases,
        compiler_params=params(41),
        cost_estimate=pl.CostEstimate(flops=0, bytes_accessed=16 * MIB, transcendentals=0),
        name=f"forward_class{begin}",
    )(meta, bounds, masks, *pieces, *extra)


def backward_kernel(which, count, meta_ref, bounds_ref, masks_ref, own, far, near, cross, *refs):
    extra, refs = (refs[0], refs[1:]) if which == 2 else (None, refs)
    outs = refs[:count]
    grads, buf, sems, total = refs[count:]
    quarter = own.shape[0]
    core, high = bounds_ref[CLASSES + 1], bounds_ref[CLASSES + 2]
    for piece, h, c in ((own, 0, 0), (far, 1, 0), (near, 0, 1), (cross, 1, 1)):
        place = ((high + h) % 2) * 2 + (core + c) % 2
        grads[pl.ds(pl.multiple_of(place * quarter, quarter), quarter), :] = piece[...]
    total[...] = jnp.zeros_like(total)

    def body(group, slot):
        for u in range(GROUP):
            _, row, block = unpack(meta_ref[group * GROUP + u])
            part = lax.dot_general(
                as_bf16(buf[slot, u]),
                grads[pl.ds(pl.multiple_of(row * TILE, TILE), TILE), :],
                (((0,), (0,)), ((), ())),
                preferred_element_type=jnp.float32,
            )
            total[pl.ds(pl.multiple_of(block * TILE, TILE), TILE), :] += part

    each_group(bounds_ref[which], bounds_ref[which + 1], meta_ref, masks_ref, buf, sems, body)
    start = 0
    for out in outs:
        size = out.shape[0] if extra is None else out.shape[0] - extra.shape[0]
        out[:size, :] = total[start : start + size, :].astype(jnp.bfloat16)
        start += size
        if extra is not None:
            out[size:, :] = extra[...]


def backward_class(which, meta, bounds, masks, grads, *extra):
    quarter, width = grads[0].shape
    vmem = pl.BlockSpec(memory_space=pltpu.VMEM)
    smem = pl.BlockSpec(memory_space=pltpu.SMEM)
    held = pl.BlockSpec(memory_space=pltpu.HBM)
    count = 2
    blocks = CLASS_BLOCKS // 2 if which in (2, 4) else CLASS_BLOCKS
    behind = sum(value.shape[0] for value in extra)
    piece = jax.ShapeDtypeStruct((blocks * TILE // count + behind, width), jnp.bfloat16)
    return pl.pallas_call(
        functools.partial(backward_kernel, which, count),
        in_specs=[smem, smem, held] + [vmem] * (4 + len(extra)),
        out_specs=[vmem] * count,
        out_shape=[piece] * count,
        scratch_shapes=[
            pltpu.VMEM((4 * quarter + TILE, width), jnp.bfloat16),
            pltpu.VMEM((DEPTH, GROUP, TILE, TILE), jnp.int32),
            pltpu.SemaphoreType.DMA((DEPTH,)),
            pltpu.VMEM(((CLASS_BLOCKS + 1) * TILE, width), jnp.float32),
        ],
        compiler_params=params(41),
        cost_estimate=pl.CostEstimate(flops=0, bytes_accessed=16 * MIB, transcendentals=0),
        name=f"backward_class{which}",
    )(meta, bounds, masks, *grads, *extra)


def dense_kernel(
    feat_hbm, self_hbm, neigh_hbm, cot_hbm, scale_ref, keep_ref, near_ref, far_ref,
    out_ref, back_ref, mean_ref, weight_ref,
    feat_ref, self_ref, neigh_ref, cot_ref, sems,
):
    rows_first = (((0,), (0,)), ((), ()))
    cols_both = (((1,), (1,)), ((), ()))
    f32 = jnp.float32
    pairs_in = (
        (feat_hbm, feat_ref), (self_hbm, self_ref), (neigh_hbm, neigh_ref), (cot_hbm, cot_ref)
    )
    copies = [pltpu.make_async_copy(a, b, sems.at[k]) for k, (a, b) in enumerate(pairs_in)]
    for copy in copies:
        copy.start()
    summed = keep_ref[0].astype(f32) + near_ref[0].astype(f32) + far_ref[...].astype(f32)
    scale = jnp.concatenate([scale_ref[...]] * (self_hbm.shape[1] // TILE), axis=1)
    agg = (summed * scale).astype(jnp.bfloat16)
    for copy in copies:
        copy.wait()
    feats = feat_ref[...]
    pre = jnp.dot(feats, self_ref[...], preferred_element_type=f32) + jnp.dot(
        agg, neigh_ref[...], preferred_element_type=f32
    )
    sig = jax.nn.sigmoid(pre)
    out_ref[...] = (pre * sig).astype(jnp.bfloat16)
    grad = (cot_ref[...].astype(f32) * sig * (1.0 + pre * (1.0 - sig))).astype(jnp.bfloat16)
    mean = lax.dot_general(grad, neigh_ref[...], cols_both, preferred_element_type=f32) * scale
    mean_ref[...] = mean.astype(jnp.bfloat16)
    width = feats.shape[1]
    weight_ref[:width, :] = lax.dot_general(feats, grad, rows_first, preferred_element_type=f32)
    weight_ref[width:, :] = lax.dot_general(agg, grad, rows_first, preferred_element_type=f32)
    back_ref[...] = lax.dot_general(grad, self_ref[...], cols_both, preferred_element_type=f32)


def dense(features, self_weight, neigh_weight, cotangent, scale, keep, near, far):
    rows, width = features.shape
    vmem = pl.BlockSpec(memory_space=pltpu.VMEM)
    return pl.pallas_call(
        dense_kernel,
        in_specs=[pl.BlockSpec(memory_space=pl.ANY)] * 4 + [vmem] * 4,
        out_specs=[vmem] * 4,
        scratch_shapes=[
            pltpu.VMEM((rows, width), jnp.bfloat16),
            pltpu.VMEM((width, width), jnp.bfloat16),
            pltpu.VMEM((width, width), jnp.bfloat16),
            pltpu.VMEM((rows, width), jnp.bfloat16),
            pltpu.SemaphoreType.DMA((4,)),
        ],
        out_shape=[
            jax.ShapeDtypeStruct((rows, width), jnp.bfloat16),
            jax.ShapeDtypeStruct((rows, width), jnp.float32),
            jax.ShapeDtypeStruct((rows, width), jnp.bfloat16),
            jax.ShapeDtypeStruct((2 * width, width), jnp.float32),
        ],
        compiler_params=params(56),
        cost_estimate=pl.CostEstimate(
            flops=6 * 2 * rows * width * width, bytes_accessed=4 * MIB, transcendentals=rows * width
        ),
        name="dense",
    )(features, self_weight, neigh_weight, cotangent, scale, keep, near, far)


def plan_tiles(tile_rows, tile_cols, tile_sums, row_blocks):
    slots = tile_rows.shape[0]
    row_index, rep_index = lax.axis_index("row"), lax.axis_index("rep")
    z, x, y = row_index // 16, row_index // 4 % 4, row_index % 4
    core, high = rep_index % 2, rep_index // 2
    section, t = tile_cols // 16, tile_cols % 4
    far_z = (section // 16 != z).astype(jnp.int32)
    dx, dy = (section // 4 % 4 - x) % 4, (section % 4 - y) % 4
    dp, dq = jnp.where(core == 0, dx, dy), jnp.where(core == 0, dy, dx)
    kind = jnp.where(dq == 0, 0, 2 * far_z + jnp.where(dq == 2, 2, 1))
    kind = jnp.where(jnp.max(tile_sums, axis=1) > 0, kind, CLASSES)
    piece = jnp.where(dq == 0, far_z, (dq == 1).astype(jnp.int32))
    place = jnp.where(dp == 0, 0, jnp.where(dp == 3, 1, jnp.where(dp == 1, 2, 3)))
    block = piece * 16 + place * 4 + t
    slot = jnp.arange(slots, dtype=jnp.int32)
    code = slot + tile_rows * 1024 + block * 32768
    classes = jnp.arange(CLASSES, dtype=jnp.int32)
    counts = jnp.sum((kind[:, None] == classes[None, :]).astype(jnp.int32), axis=0)
    groups = (counts + GROUP - 1) // GROUP
    starts = jnp.sum(
        jnp.where(jnp.arange(CLASSES + 1)[:, None] > classes[None, :], groups[None, :], 0), axis=1
    )
    same_before = (kind[:, None] == kind[None, :]) & (slot[None, :] < slot[:, None])
    rank = jnp.sum(same_before.astype(jnp.int32), axis=1)
    start = jnp.sum(jnp.where(kind[:, None] == classes[None, :], starts[None, :CLASSES], 0), axis=1)
    position = jnp.where(kind < CLASSES, start * GROUP + rank, -1)
    places = -(-(slots + CLASSES * (GROUP - 1)) // GROUP) * GROUP
    hit = jnp.arange(places, dtype=jnp.int32)[:, None] == position[None, :]
    pad = row_blocks * 1024 + CLASS_BLOCKS * 32768
    meta = pad + jnp.sum(jnp.where(hit, code[None, :] - pad, 0), axis=1)
    bounds = jnp.concatenate([starts, core[None], high[None]]).astype(jnp.int32)
    return meta.astype(jnp.int32), bounds


def tie(*values):
    return lax.optimization_barrier(values)


def add(*values):
    return sum(value.astype(jnp.float32) for value in values).astype(jnp.bfloat16)


def local(features, self_weight, neigh_weight, tile_rows, tile_cols, tile_masks, cotangent):
    rows, width = features.shape
    row_blocks = rows * 4 // TILE
    core, high = lax.axis_index("rep") % 2, lax.axis_index("rep") // 2

    low = swap_low(features)
    near = [move_p(features, 1), move_p(features, -1), move_p(features, 2)]
    sums0, degree0 = degrees(0, 2, tile_rows, tile_masks, row_blocks)
    *near, low, sums0, degree0 = tie(*near, low, sums0, degree0)
    block0 = jnp.concatenate([features, *near])
    block0, far, low, rows_after = tie(block0, near[2], low, tile_rows)
    below0, above0 = move_q(block0, 1), move_q(block0, -1)
    near = [move_p(low, 1), move_p(low, -1), swap_low(far)]
    sums1, degree1 = degrees(1, 2, rows_after, tile_masks, row_blocks)
    *near, sums1, degree1 = tie(*near, sums1, degree1)
    block1 = jnp.concatenate([low, *near])
    block1, sums1 = tie(block1, sums1)
    below1, above1 = move_q(block1, 1), move_q(block1, -1)
    meta, bounds = plan_tiles(
        tile_rows, tile_cols, jnp.concatenate([sums0, sums1]), row_blocks
    )
    degree = degree0 + degree1
    degree = degree + swap_core(degree)

    def forward(begin, end, before, *pieces):
        return forward_class(begin, end, meta, bounds, tile_masks, pieces, before, row_blocks)

    total = forward(0, 1, None, block0, block1)
    below0, above0, total = tie(below0, above0, total)
    edge = block0.shape[0] // 2
    start0, start1 = below0[:edge], above0[edge:]
    start0, start1, total = tie(start0, start1, total)
    far00, far01 = move_q(start0, 1), move_q(start1, -1)
    total = forward(1, 2, total, below0, above0)
    below1, above1, total = tie(below1, above1, total)
    start0, start1 = below1[:edge], above1[edge:]
    start0, start1, total = tie(start0, start1, total)
    far10, far11 = move_q(start0, 1), move_q(start1, -1)
    total = forward(3, 4, total, below1, above1)
    far00, far01, total = tie(far00, far01, total)
    total = forward(2, 3, total, far00, far01)
    far10, far11, total = tie(far10, far11, total)
    keep, give = forward(4, 5, total, far10, far11)
    degree = degree + swap_high(degree)
    own_degree = lax.dynamic_slice_in_dim(
        degree, (high * 2 + core) * (row_blocks // 4), row_blocks // 4, 0
    )
    scale = jnp.broadcast_to(
        lax.rsqrt(jnp.maximum(own_degree, 1.0)).reshape(rows, 1), (rows, TILE)
    )

    near = swap_core(give)
    far = swap_high(add(keep[1], near[1]))
    output, back, mean, weight = dense(
        features, self_weight, neigh_weight, cotangent, scale, keep, near, far
    )
    def fold(weight, exchange):
        sent = weight.astype(jnp.bfloat16)
        return sent.astype(jnp.float32) + exchange(sent).astype(jnp.float32)

    def ring_sum(own, below, above, across, odd):
        own, below, above, across = (v.astype(jnp.float32) for v in (own, below, above, across))
        beside, beyond = jnp.where(odd, below, above), jnp.where(odd, above, below)
        return ((own + beside) + (beyond + across)).astype(jnp.bfloat16)

    mean_far = swap_high(mean)
    mean_near = swap_core(mean)
    grads = (mean, mean_far, mean_near, swap_core(mean_far))
    weight_mine = lax.dynamic_slice_in_dim(weight, core * width, width, 0)
    weight_theirs = lax.dynamic_slice_in_dim(weight, (1 - core) * width, width, 0)
    weight = fold(fold(weight_mine + swap_core(weight_theirs), swap_low), swap_high)
    weight = weight.astype(jnp.bfloat16)
    row_index = lax.axis_index("row")
    odd_x, odd_y = row_index // 4 % 2 == 1, row_index % 2 == 1
    odd_p, odd_q = jnp.where(core == 0, odd_x, odd_y), jnp.where(core == 0, odd_y, odd_x)

    def backward(which, grads, *extra):
        return backward_class(which, meta, bounds, tile_masks, grads, *extra)

    far10, far11 = backward(4, grads)
    far10, far11, *grads = tie(far10, far11, *grads)
    below1, above1 = move_q(far10, 1), move_q(far11, -1)
    far00, far01 = backward(2, grads, weight)
    far00, far01, *grads = tie(far00, far01, *grads)
    below0, above0 = move_q(far00, 1), move_q(far01, -1)
    down, up = backward(3, grads)
    down, up, below1, above1 = tie(down, up, below1, above1)
    to_above = jnp.concatenate([add(up[:edge], below1), up[edge:]])
    to_below = jnp.concatenate([down[:edge], add(down[edge:], above1)])
    to_above, to_below, *grads = tie(to_above, to_below, *grads)
    from_below1, from_above1 = move_q(to_above, 1), move_q(to_below, -1)
    down, up = backward(1, grads)
    down, up, below0, above0 = tie(down, up, below0, above0)
    to_above = jnp.concatenate([add(up[:edge], below0[:edge]), up[edge:], below0[edge:]])
    to_below = jnp.concatenate([down[:edge], add(down[edge:], above0[:edge])])
    to_above, to_below, *grads = tie(to_above, to_below, *grads)
    from_below0, from_above0 = move_q(to_above, 1), move_q(to_below, -1)
    here0, here1 = backward(0, grads)
    here0, here1, from_below1, from_above1 = tie(here0, here1, from_below1, from_above1)
    total = add(here1, from_below1, from_above1)
    parts = [total[k * rows : (k + 1) * rows] for k in range(4)]
    moved = (move_p(parts[1], -1), move_p(parts[2], 1))
    low_far = swap_low(parts[3])
    own_part, *moved, low_far = tie(parts[0], *moved, low_far)
    low_own = swap_low(add(own_part, *moved))
    low_far, from_below0, from_above0 = tie(low_far, from_below0, from_above0)
    weight = ring_sum(weight, below0[edge:], above0[edge:], from_below0[2 * edge :], odd_q)
    total = add(here0[rows:], from_below0[rows : 2 * edge], from_above0[rows:])
    down = jnp.concatenate([total[:rows], weight])
    up = jnp.concatenate([total[rows : 2 * rows], weight])
    across = jnp.concatenate([add(total[2 * rows :], low_far), weight])
    from_above, from_below, from_across = move_p(down, -1), move_p(up, 1), move_p(across, 2)
    weight = ring_sum(weight, from_below[rows:], from_above[rows:], from_across[rows:], odd_p)
    weight = weight.astype(jnp.float32)
    incoming = sum(
        value[:rows].astype(jnp.float32)
        for value in (here0, from_below0, from_above0, low_own, from_above, from_below, from_across)
    )
    grad_feat = (back + incoming).astype(jnp.bfloat16)
    weight = weight * ((rows * lax.axis_size(BOTH)) ** (-0.5))
    weight_other = swap_core(weight)
    self_total = jnp.where(core == 0, weight, weight_other)
    neigh_total = jnp.where(core == 0, weight_other, weight)
    return (output, grad_feat, self_total, neigh_total)


def solution(mesh):
    in_specs = (
        P(BOTH, None),
        P(),
        P(),
        P(BOTH),
        P(BOTH),
        P(BOTH, None, None),
        P(BOTH, None),
    )
    out_specs = (P(BOTH, None), P(BOTH, None), P(), P())
    return jax.shard_map(local, mesh=mesh, in_specs=in_specs, out_specs=out_specs, check_vma=False)
```

time: 205 us -> 173 us (0.84)
  starting transfers between devices: 78 us -> 62.4 us
  Pallas kernels: 57.1 us -> 46.6 us
  waiting for transfers between devices: 51.9 us -> 42.5 us
  other arithmetic: 6.29 us -> 13.5 us
  local copies, waits for them, and re-layouts: 8.31 us -> 4.7 us
    ppermute x63 -> x41, starting transfers between devices: 78 us -> 62.4 us  [move(): return lax.ppermute(value, BOTH, pairs(step))]
    pallas_call x10 -> x13, Pallas kernels: 57.1 us -> 46.6 us  [the longest x5 16 us: backward_class(): pl.pallas_call(functools.partial(backward_kernel, which, count), in_specs...]
    ppermute x63 -> x41, waiting for transfers between devices: 51.9 us -> 42.5 us  [move(): return lax.ppermute(value, BOTH, pairs(step))]
    convert_element_type x4 -> x8, other arithmetic: 1.08 us -> 3.98 us  [add(): sum((value.astype(jnp.float32) for value in values)).astype(jnp.bfloat16)]
    concatenate x0 -> x7, other arithmetic: none -> 2.38 us  [the longest x1 1.06 us: local(): to_below = jnp.concatenate([down[:edge], add(down[edge:], above0[:edge])])]
    another operation x3 -> x0, local copies, waits for them, and re-layouts: 2.36 us -> none  [the longest x1 1.29 us: local(): block1 = jnp.stack([low, *near], axis=1).reshape(2, 4 * half, width)]
  transfers between devices with their start and end apart: 63 -> 41, of which waited for: 20 -> 14; matrix products, arithmetic and copies ran while one was open for 4% -> 6% of each run, Pallas kernels for 25% -> 23%
where the time goes in v3:
time: 173 us; the launch traced here: 171 us
  starting transfers between devices  62.4 us (36%)
  Pallas kernels  46.6 us (27%)
  waiting for transfers between devices  42.5 us (25%)
  other arithmetic  13.5 us (8%)
  local copies, waits for them, and re-layouts  4.7 us (3%)
    ppermute x41, starting transfers between devices, move(): return lax.ppermute(value, BOTH, pairs(step))  62.4 us
    ppermute x41, waiting for transfers between devices, move(): return lax.ppermute(value, BOTH, pairs(step))  42.5 us
    pallas_call x5, Pallas kernels, backward_class(): pl.pallas_call(functools.partial(backward_kernel, which, count), in_specs...  16 us
    pallas_call x5, Pallas kernels, forward_class(): pl.pallas_call(functools.partial(forward_kernel, begin, end, len(pieces),...  14.8 us
    pallas_call x2, Pallas kernels, degrees(): pl.pallas_call(functools.partial(degree_kernel, part * slots), in_specs=[...  11.4 us
    pallas_call x1, Pallas kernels, dense(): pl.pallas_call(dense_kernel, in_specs=[pl.BlockSpec(memory_space=pl.ANY)]...  4.31 us
    convert_element_type x8, other arithmetic, add(): sum((value.astype(jnp.float32) for value in values)).astype(jnp.bfloat16)  3.98 us
  transfers between devices with their start and end apart: 41, of which 14 were waited for; matrix products, arithmetic and copies ran while one was open for 6% of the time, Pallas kernels for 23%

profile of v3, /device:TPU:0, one launch (start us, length us, event | category | flops | bytes accessed | tf_op | source)
XLA Modules:
  0.0 170.9 jit_solution(11172269504866352516)
XLA Ops:
  0.6 1.6 collective-permute-start
  2.3 1.7 collective-permute-start.1
  3.9 1.9 %collective-permute-start.2 = (bf16[512,256]{1,0:T(8,128)(2,1)}, bf16[512,256]{1,0:T(8,128)(2,1)S(1)}, u32[]{:S(2)}, u32[]{:S(2)}) collective-permute-start(bf16[512,256]{1,0:T(8,128)(2,1)} %feat_hbm.1), channel_id=1, source_target_pairs={{0,32},{1,9},{2,34},{3,11},{4,36},{5,13},{6,38},{7,15},{8,40},{9,1... | collective-permute-start | bytes 786440 | tf_op jit(solution)/shard_map/ppermute | solution.py:35
  5.8 1.9 %collective-permute-start.3 = (bf16[512,256]{1,0:T(8,128)(2,1)}, bf16[512,256]{1,0:T(8,128)(2,1)S(1)}, u32[]{:S(2)}, u32[]{:S(2)}) collective-permute-start(bf16[512,256]{1,0:T(8,128)(2,1)} %feat_hbm.1), channel_id=1, source_target_pairs={{0,64},{1,65},{2,66},{3,67},{4,68},{5,69},{6,70},{7,71},{8,72},{9,... | collective-permute-start | bytes 786440 | tf_op jit(solution)/shard_map/ppermute | solution.py:35
  8.4 5.7 %degrees0.1 = (f32[160,128]{1,0:T(8,128)S(1)}, f32[16,128]{1,0:T(8,128)S(1)}) custom-call(s32[320]{0:T(512)S(1)} %copy-done.2, s32[320,128,128]{2,1,0:T(8,128)} %masks_ref.23), custom_call_target="tpu_custom_call" | custom-call | bytes 20971520 | tf_op jit(solution)/shard_map/degrees0/pallas_call | solution.py:112
  15.3 2.4 %collective-permute-start.5 = (bf16[512,256]{1,0:T(8,128)(2,1)S(1)}, bf16[512,256]{1,0:T(8,128)(2,1)S(1)}, u32[]{:S(2)}, u32[]{:S(2)}) collective-permute-start(bf16[512,256]{1,0:T(8,128)(2,1)S(1)} %collective-permute-done.3), channel_id=1, source_target_pairs={{0,48},{1,13},{2,50},{3,15},{4,52},{5,1},{6,54},{7,3},{8,56},{9,5}... | collective-permute-start | bytes 786440 | tf_op jit(solution)/shard_map/ppermute | solution.py:35
  19.4 2.6 %collective-permute-start.12 = (bf16[2048,256]{1,0:T(8,128)(2,1)S(1)}, bf16[2048,256]{1,0:T(8,128)(2,1)S(1)}, u32[]{:S(2)}, u32[]{:S(2)}) collective-permute-start(bf16[2048,256]{1,0:T(8,128)(2,1)S(1)} %pad_maximum_fusion.1.refs_0_), channel_id=1, source_target_pairs={{0,12},{1,49},{2,14},{3,51},{4,0},{5,53},{6,2},{7,55},{8,4},{9,57}... | collective-permute-start | bytes 3145736 | tf_op jit(solution)/shard_map/ppermute | solution.py:35
  22.0 5.7 %degrees1.1 = (f32[160,128]{1,0:T(8,128)S(1)}, f32[16,128]{1,0:T(8,128)S(1)}) custom-call(s32[320]{0:T(512)S(1)} %copy-done.3, s32[320,128,128]{2,1,0:T(8,128)} %masks_ref.23), custom_call_target="tpu_custom_call" | custom-call | bytes 20971520 | tf_op jit(solution)/shard_map/degrees1/pallas_call | solution.py:112
  28.7 1.2 collective-permute-start.9
  31.0 3.0 %forward_class0.1.refs_2_ = f32[2176,256]{1,0:T(8,128)S(1)} custom-call(s32[400]{0:T(512)S(1)} %broadcast_add_fusion.meta_ref, s32[8]{0:T(128)S(1)} %pad_add_fusion.bounds_ref, s32[320,128,128]{2,1,0:T(8,128)} %masks_ref.23, bf16[2048,256]{1,0:T(8,128)(2,1)S(1)} %pad_maximum_fusion.1.refs_0_, bf16[2048,256]{1,0:T(8,128)(2,1)S(1)} %pad_maximum_fusion.2.refs_1_), custom_call_target="tpu_custom_call" | custom-call | bytes 16777216 | tf_op jit(solution)/shard_map/forward_class0/pallas_call | solution.py:225
  34.8 3.2 %forward_class1.1.refs_2_ = f32[2176,256]{1,0:T(8,128)S(1)} custom-call(s32[400]{0:T(512)S(1)} %broadcast_add_fusion.meta_ref, s32[8]{0:T(128)S(1)} %pad_add_fusion.bounds_ref, s32[320,128,128]{2,1,0:T(8,128)} %masks_ref.23, bf16[2048,256]{1,0:T(8,128)(2,1)S(1)} %collective-permute-done.11.refs_0_, ...), custom_call_target="tpu_custom_call", output_to_operand_aliasing={{}: (5, {})} | custom-call | bytes 16777216 | tf_op jit(solution)/shard_map/forward_class1/pallas_call | solution.py:225
  38.0 1.9 %collective-permute-start.15 = (bf16[1024,256]{1,0:T(8,128)(2,1)S(1)}, bf16[1024,256]{1,0:T(8,128)(2,1)S(1)}, u32[]{:S(2)}, u32[]{:S(2)}) collective-permute-start(bf16[1024,256]{1,0:T(8,128)(2,1)S(1)} %slice.119), channel_id=1, source_target_pairs={{0,4},{1,17},{2,6},{3,19},{4,8},{5,21},{6,10},{7,23},{8,12},{9,25}... | collective-permute-start | bytes 1572872 | tf_op jit(solution)/shard_map/ppermute | solution.py:35
  40.0 3.6 %collective-permute-start.16 = (bf16[1024,256]{1,0:T(8,128)(2,1)S(1)}, bf16[1024,256]{1,0:T(8,128)(2,1)S(1)}, u32[]{:S(2)}, u32[]{:S(2)}) collective-permute-start(bf16[1024,256]{1,0:T(8,128)(2,1)S(1)} %slice.120), channel_id=1, source_target_pairs={{0,12},{1,49},{2,14},{3,51},{4,0},{5,53},{6,2},{7,55},{8,4},{9,57}... | collective-permute-start | bytes 1572872 | tf_op jit(solution)/shard_map/ppermute | solution.py:35
  43.5 2.0 %collective-permute-done.10.refs_1_ = bf16[2048,256]{1,0:T(8,128)(2,1)S(1)} collective-permute-done((bf16[2048,256]{1,0:T(8,128)(2,1)S(1)}, bf16[2048,256]{1,0:T(8,128)(2,1)S(1)}, u32[]{:S(2)}, u32[]{:S(2)}) %collective-permute-start.10) | collective-permute-done | bytes 1048608 | tf_op jit(solution)/shard_map/ppermute | solution.py:35
  47.1 2.4 %collective-permute-start.14 = (bf16[1024,256]{1,0:T(8,128)(2,1)S(1)}, bf16[1024,256]{1,0:T(8,128)(2,1)S(1)}, u32[]{:S(2)}, u32[]{:S(2)}) collective-permute-start(bf16[1024,256]{1,0:T(8,128)(2,1)S(1)} %slice.122), channel_id=1, source_target_pairs={{0,12},{1,49},{2,14},{3,51},{4,0},{5,53},{6,2},{7,55},{8,4},{9,57}... | collective-permute-start | bytes 1572872 | tf_op jit(solution)/shard_map/ppermute | solution.py:35
  49.4 3.2 %forward_class3.1.refs_2_ = f32[2176,256]{1,0:T(8,128)S(1)} custom-call(s32[400]{0:T(512)S(1)} %broadcast_add_fusion.meta_ref, s32[8]{0:T(128)S(1)} %pad_add_fusion.bounds_ref, s32[320,128,128]{2,1,0:T(8,128)} %masks_ref.23, bf16[2048,256]{1,0:T(8,128)(2,1)S(1)} %collective-permute-done.9.refs_0_, ...), custom_call_target="tpu_custom_call", output_to_operand_aliasing={{}: (5, {})} | custom-call | bytes 16777216 | tf_op jit(solution)/shard_map/forward_class3/pallas_call | solution.py:225
  52.7 2.8 %forward_class2.1.refs_2_ = f32[2176,256]{1,0:T(8,128)S(1)} custom-call(s32[400]{0:T(512)S(1)} %broadcast_add_fusion.meta_ref, s32[8]{0:T(128)S(1)} %pad_add_fusion.bounds_ref, s32[320,128,128]{2,1,0:T(8,128)} %masks_ref.23, bf16[1024,256]{1,0:T(8,128)(2,1)S(1)} %collective-permute-done.15.refs_0_, ...), custom_call_target="tpu_custom_call", output_to_operand_aliasing={{}: (5, {})} | custom-call | bytes 16777216 | tf_op jit(solution)/shard_map/forward_class2/pallas_call | solution.py:225
  55.4 1.8 %collective-permute-done.13.refs_0_ = bf16[1024,256]{1,0:T(8,128)(2,1)S(1)} collective-permute-done((bf16[1024,256]{1,0:T(8,128)(2,1)S(1)}, bf16[1024,256]{1,0:T(8,128)(2,1)S(1)}, u32[]{:S(2)}, u32[]{:S(2)}) %collective-permute-start.13) | collective-permute-done | bytes 524320 | tf_op jit(solution)/shard_map/ppermute | solution.py:35
  57.2 2.6 %forward_class4.1 = (bf16[2,512,256]{2,1,0:T(8,128)(2,1)S(1)}, bf16[2,512,256]{2,1,0:T(8,128)(2,1)S(1)}) custom-call(s32[400]{0:T(512)S(1)} %broadcast_add_fusion.meta_ref, s32[8]{0:T(128)S(1)} %pad_add_fusion.bounds_ref, s32[320,128,128]{2,1,0:T(8,128)} %masks_ref.23, bf16[1024,256]{1,0:T(8,128)(2,1)S(1)} %collective-permute-done.13.refs_0_, ...), custom_call_target="tpu_custom_call" | custom-call | bytes 16777216 | tf_op jit(solution)/shard_map/forward_class4/pallas_call | solution.py:225
  59.9 1.9 %collective-permute-done.17.near_ref = bf16[2,512,256]{2,1,0:T(8,128)(2,1)S(1)} collective-permute-done((bf16[2,512,256]{2,1,0:T(8,128)(2,1)S(1)}, bf16[2,512,256]{2,1,0:T(8,128)(2,1)S(1)}, u32[]{:S(2)}, u32[]{:S(2)}) %collective-permute-start.17) | collective-permute-done | bytes 524320 | tf_op jit(solution)/shard_map/ppermute | solution.py:35
  61.9 3.7 %collective-permute-start.18 = (bf16[512,256]{1,0:T(8,128)(2,1)S(1)}, bf16[512,256]{1,0:T(8,128)(2,1)S(1)}, u32[]{:S(2)}, u32[]{:S(2)}) collective-permute-start(bf16[512,256]{1,0:T(8,128)(2,1)S(1)} %fusion.9), channel_id=1, source_target_pairs={{0,2},{1,3},{2,0},{3,1},{4,6},{5,7},{6,4},{7,5},{8,10},{9,11},{10,... | collective-permute-start | bytes 786440 | tf_op jit(solution)/shard_map/ppermute | solution.py:35
  65.6 1.2 collective-permute-done.7
  66.8 5.5 %collective-permute-done.8 = f32[16,128]{1,0:T(8,128)S(1)} collective-permute-done((f32[16,128]{1,0:T(8,128)S(1)}, f32[16,128]{1,0:T(8,128)S(1)}, u32[]{:S(2)}, u32[]{:S(2)}) %collective-permute-start.8) | collective-permute-done | bytes 8224 | tf_op jit(solution)/shard_map/ppermute | solution.py:35
  73.2 4.3 %dense.1 = (bf16[512,256]{1,0:T(8,128)(2,1)}, f32[512,256]{1,0:T(8,128)}, bf16[512,256]{1,0:T(8,128)(2,1)}, f32[512,256]{1,0:T(8,128)}) custom-call(bf16[512,256]{1,0:T(8,128)(2,1)} %feat_hbm.1, bf16[256,256]{1,0:T(8,128)(2,1)} %self_hbm.1, bf16[256,256]{1,0:T(8,128)(2,1)} %neigh_hbm.1, bf16[512,256]{1,0:T(8,128)(2,1)} %cot_hbm.1, ...), custom_call_target="tpu_custom_call" | custom-call | flops 402653184 | bytes 4194304 | tf_op jit(solution)/shard_map/dense/pallas_call | solution.py:333
  77.5 3.3 %collective-permute-start.19 = (bf16[512,256]{1,0:T(8,128)(2,1)}, bf16[512,256]{1,0:T(8,128)(2,1)S(1)}, u32[]{:S(2)}, u32[]{:S(2)}) collective-permute-start(bf16[512,256]{1,0:T(8,128)(2,1)} %get-tuple-element.179.own), channel_id=1, source_target_pairs={{0,2},{1,3},{2,0},{3,1},{4,6},{5,7},{6,4},{7,5},{8,10},{9,11},{10,... | collective-permute-start | bytes 786440 | tf_op jit(solution)/shard_map/ppermute | solution.py:35
  82.4 4.7 %collective-permute-done.19.far = bf16[512,256]{1,0:T(8,128)(2,1)S(1)} collective-permute-done((bf16[512,256]{1,0:T(8,128)(2,1)}, bf16[512,256]{1,0:T(8,128)(2,1)S(1)}, u32[]{:S(2)}, u32[]{:S(2)}) %collective-permute-start.19) | collective-permute-done | bytes 262176 | tf_op jit(solution)/shard_map/ppermute | solution.py:35
  88.2 2.1 %collective-permute-start.23 = (bf16[256,256]{1,0:T(8,128)(2,1)S(1)}, bf16[256,256]{1,0:T(8,128)(2,1)S(1)}, u32[]{:S(2)}, u32[]{:S(2)}) collective-permute-start(bf16[256,256]{1,0:T(8,128)(2,1)S(1)} %add_convert_fusion.12), channel_id=1, source_target_pairs={{0,64},{1,65},{2,66},{3,67},{4,68},{5,69},{6,70},{7,71},{8,72},{9,... | collective-permute-start | bytes 393224 | tf_op jit(solution)/shard_map/ppermute | solution.py:35
  91.2 2.8 %backward_class4.1 = (bf16[1024,256]{1,0:T(8,128)(2,1)S(1)}, bf16[1024,256]{1,0:T(8,128)(2,1)S(1)}) custom-call(s32[400]{0:T(512)S(1)} %broadcast_add_fusion.meta_ref, s32[8]{0:T(128)S(1)} %pad_add_fusion.bounds_ref, s32[320,128,128]{2,1,0:T(8,128)} %masks_ref.23, bf16[512,256]{1,0:T(8,128)(2,1)S(1)} %copy-done, ...), custom_call_target="tpu_custom_call" | custom-call | bytes 16777216 | tf_op jit(solution)/shard_map/backward_class4/pallas_call | solution.py:279
  94.0 2.2 %collective-permute-start.25 = (bf16[1024,256]{1,0:T(8,128)(2,1)S(1)}, bf16[1024,256]{1,0:T(8,128)(2,1)S(1)}, u32[]{:S(2)}, u32[]{:S(2)}) collective-permute-start(bf16[1024,256]{1,0:T(8,128)(2,1)S(1)} %get-tuple-element.161), channel_id=1, source_target_pairs={{0,4},{1,17},{2,6},{3,19},{4,8},{5,21},{6,10},{7,23},{8,12},{9,25}... | collective-permute-start | bytes 1572872 | tf_op jit(solution)/shard_map/ppermute | solution.py:35
  97.3 3.7 %collective-permute-start.24 = (bf16[256,256]{1,0:T(8,128)(2,1)S(1)}, bf16[256,256]{1,0:T(8,128)(2,1)S(1)}, u32[]{:S(2)}, u32[]{:S(2)}) collective-permute-start(bf16[256,256]{1,0:T(8,128)(2,1)S(1)} %add_convert_fusion.11), channel_id=1, source_target_pairs={{0,2},{1,3},{2,0},{3,1},{4,6},{5,7},{6,4},{7,5},{8,10},{9,11},{10,... | collective-permute-start | bytes 393224 | tf_op jit(solution)/shard_map/ppermute | solution.py:35
  101.1 4.3 %collective-permute-done.24 = bf16[256,256]{1,0:T(8,128)(2,1)S(1)} collective-permute-done((bf16[256,256]{1,0:T(8,128)(2,1)S(1)}, bf16[256,256]{1,0:T(8,128)(2,1)S(1)}, u32[]{:S(2)}, u32[]{:S(2)}) %collective-permute-start.24) | collective-permute-done | bytes 131104 | tf_op jit(solution)/shard_map/ppermute | solution.py:35
  105.4 2.9 %backward_class2.1 = (bf16[1280,256]{1,0:T(8,128)(2,1)S(1)}, bf16[1280,256]{1,0:T(8,128)(2,1)S(1)}) custom-call(s32[400]{0:T(512)S(1)} %broadcast_add_fusion.meta_ref, s32[8]{0:T(128)S(1)} %pad_add_fusion.bounds_ref, s32[320,128,128]{2,1,0:T(8,128)} %masks_ref.23, bf16[512,256]{1,0:T(8,128)(2,1)S(1)} %copy-done, ...), custom_call_target="tpu_custom_call" | custom-call | bytes 16777216 | tf_op jit(solution)/shard_map/backward_class2/pallas_call | solution.py:279
  108.8 2.8 %collective-permute-start.28 = (bf16[1280,256]{1,0:T(8,128)(2,1)S(1)}, bf16[1280,256]{1,0:T(8,128)(2,1)S(1)}, u32[]{:S(2)}, u32[]{:S(2)}) collective-permute-start(bf16[1280,256]{1,0:T(8,128)(2,1)S(1)} %get-tuple-element.174), channel_id=1, source_target_pairs={{0,12},{1,49},{2,14},{3,51},{4,0},{5,53},{6,2},{7,55},{8,4},{9,57}... | collective-permute-start | bytes 1966088 | tf_op jit(solution)/shard_map/ppermute | solution.py:35
  111.7 3.4 %backward_class3.1 = (bf16[2048,256]{1,0:T(8,128)(2,1)S(1)}, bf16[2048,256]{1,0:T(8,128)(2,1)S(1)}) custom-call(s32[400]{0:T(512)S(1)} %broadcast_add_fusion.meta_ref, s32[8]{0:T(128)S(1)} %pad_add_fusion.bounds_ref, s32[320,128,128]{2,1,0:T(8,128)} %masks_ref.23, bf16[512,256]{1,0:T(8,128)(2,1)S(1)} %copy-done, ...), custom_call_target="tpu_custom_call" | custom-call | bytes 16777216 | tf_op jit(solution)/shard_map/backward_class3/pallas_call | solution.py:279
  116.4 2.5 %collective-permute-start.30 = (bf16[2048,256]{1,0:T(8,128)(2,1)S(1)}, bf16[2048,256]{1,0:T(8,128)(2,1)S(1)}, u32[]{:S(2)}, u32[]{:S(2)}) collective-permute-start(bf16[2048,256]{1,0:T(8,128)(2,1)S(1)} %pad_maximum_fusion.4), channel_id=1, source_target_pairs={{0,12},{1,49},{2,14},{3,51},{4,0},{5,53},{6,2},{7,55},{8,4},{9,57}... | collective-permute-start | bytes 3145736 | tf_op jit(solution)/shard_map/ppermute | solution.py:35
  118.9 3.6 %backward_class1.1 = (bf16[2048,256]{1,0:T(8,128)(2,1)S(1)}, bf16[2048,256]{1,0:T(8,128)(2,1)S(1)}) custom-call(s32[400]{0:T(512)S(1)} %broadcast_add_fusion.meta_ref, s32[8]{0:T(128)S(1)} %pad_add_fusion.bounds_ref, s32[320,128,128]{2,1,0:T(8,128)} %masks_ref.23, bf16[512,256]{1,0:T(8,128)(2,1)S(1)} %copy-done, ...), custom_call_target="tpu_custom_call" | custom-call | bytes 16777216 | tf_op jit(solution)/shard_map/backward_class1/pallas_call | solution.py:279
  124.6 3.6 %collective-permute-start.35 = (bf16[2048,256]{1,0:T(8,128)(2,1)}, bf16[2048,256]{1,0:T(8,128)(2,1)}, u32[]{:S(2)}, u32[]{:S(2)}) collective-permute-start(bf16[2048,256]{1,0:T(8,128)(2,1)} %pad_maximum_fusion.5), channel_id=1, source_target_pairs={{0,12},{1,49},{2,14},{3,51},{4,0},{5,53},{6,2},{7,55},{8,4},{9,57}... | collective-permute-start | bytes 3145736 | tf_op jit(solution)/shard_map/ppermute | solution.py:35
  128.2 3.4 %backward_class0.1 = (bf16[2048,256]{1,0:T(8,128)(2,1)S(1)}, bf16[2048,256]{1,0:T(8,128)(2,1)S(1)}) custom-call(s32[400]{0:T(512)S(1)} %broadcast_add_fusion.meta_ref, s32[8]{0:T(128)S(1)} %pad_add_fusion.bounds_ref, s32[320,128,128]{2,1,0:T(8,128)} %masks_ref.23, bf16[512,256]{1,0:T(8,128)(2,1)S(1)} %copy-done, ...), custom_call_target="tpu_custom_call" | custom-call | bytes 16777216 | tf_op jit(solution)/shard_map/backward_class0/pallas_call | solution.py:279
  133.0 3.2 %collective-permute-start.31 = (bf16[512,256]{1,0:T(8,128)(2,1)}, bf16[512,256]{1,0:T(8,128)(2,1)}, u32[]{:S(2)}, u32[]{:S(2)}) collective-permute-start(bf16[512,256]{1,0:T(8,128)(2,1)} %get-tuple-element.204), channel_id=1, source_target_pairs={{0,48},{1,13},{2,50},{3,15},{4,52},{5,1},{6,54},{7,3},{8,56},{9,5}... | collective-permute-start | bytes 786440 | tf_op jit(solution)/shard_map/ppermute | solution.py:35
  136.2 1.2 collective-permute-start.33
  137.4 5.9 %collective-permute-done.31 = bf16[512,256]{1,0:T(8,128)(2,1)} collective-permute-done((bf16[512,256]{1,0:T(8,128)(2,1)}, bf16[512,256]{1,0:T(8,128)(2,1)}, u32[]{:S(2)}, u32[]{:S(2)}) %collective-permute-start.31) | collective-permute-done | bytes 262176 | tf_op jit(solution)/shard_map/ppermute | solution.py:35
  143.3 3.7 %collective-permute-done.32 = bf16[512,256]{1,0:T(8,128)(2,1)} collective-permute-done((bf16[512,256]{1,0:T(8,128)(2,1)}, bf16[512,256]{1,0:T(8,128)(2,1)}, u32[]{:S(2)}, u32[]{:S(2)}) %collective-permute-start.32) | collective-permute-done | bytes 262176 | tf_op jit(solution)/shard_map/ppermute | solution.py:35
  147.0 1.7 add_convert_fusion.1
  150.8 2.4 %collective-permute-start.37 = (bf16[768,256]{1,0:T(8,128)(2,1)}, bf16[768,256]{1,0:T(8,128)(2,1)S(1)}, u32[]{:S(2)}, u32[]{:S(2)}) collective-permute-start(bf16[768,256]{1,0:T(8,128)(2,1)} %get-tuple-element.210), channel_id=1, source_target_pairs={{0,48},{1,13},{2,50},{3,15},{4,52},{5,1},{6,54},{7,3},{8,56},{9,5}... | collective-permute-start | bytes 1179656 | tf_op jit(solution)/shard_map/ppermute | solution.py:35
  153.2 2.1 %collective-permute-start.39 = (bf16[768,256]{1,0:T(8,128)(2,1)S(1)}, bf16[768,256]{1,0:T(8,128)(2,1)}, u32[]{:S(2)}, u32[]{:S(2)}) collective-permute-start(bf16[768,256]{1,0:T(8,128)(2,1)S(1)} %get-tuple-element.212), channel_id=1, source_target_pairs={{0,32},{1,9},{2,34},{3,11},{4,36},{5,13},{6,38},{7,15},{8,40},{9,1... | collective-permute-start | bytes 1179656 | tf_op jit(solution)/shard_map/ppermute | solution.py:35
  156.6 6.5 %collective-permute-done.37 = bf16[768,256]{1,0:T(8,128)(2,1)S(1)} collective-permute-done((bf16[768,256]{1,0:T(8,128)(2,1)}, bf16[768,256]{1,0:T(8,128)(2,1)S(1)}, u32[]{:S(2)}, u32[]{:S(2)}) %collective-permute-start.37) | collective-permute-done | bytes 393248 | tf_op jit(solution)/shard_map/ppermute | solution.py:35
  163.0 3.7 %collective-permute-done.38 = bf16[768,256]{1,0:T(8,128)(2,1)} collective-permute-done((bf16[768,256]{1,0:T(8,128)(2,1)}, bf16[768,256]{1,0:T(8,128)(2,1)}, u32[]{:S(2)}, u32[]{:S(2)}) %collective-permute-start.38) | collective-permute-done | bytes 393248 | tf_op jit(solution)/shard_map/ppermute | solution.py:35
  167.9 2.1 %add_convert_fusion.6 = bf16[512,256]{1,0:T(8,128)(2,1)} fusion(f32[512,256]{1,0:T(8,128)S(1)} %copy-done.7, bf16[512,256]{1,0:T(8,128)(2,1)S(1)} %collective-permute-done.36, bf16[768,256]{1,0:T(8,128)(2,1)} %collective-permute-done.39, bf16[768,256]{1,0:T(8,128)(2,1)} %collective-permute-done.38, bf16[768,256]{1,0:T(8,128)(2,1)S(1)} %collective-permute-done.37, ...), kind=kLoop, calls=%fused_computation.17 | loop fusion | flops 1966080 | bytes 2621440 | tf_op jit(solution)/shard_map/convert_element_type | solution.py:518
  (117 shorter events, 24.4 us)
Async XLA Ops:
  0.6 13.5 %collective-permute-start = (bf16[512,256]{1,0:T(8,128)(2,1)}, bf16[512,256]{1,0:T(8,128)(2,1)S(1)}, u32[]{:S(2)}, u32[]{:S(2)}) collective-permute-start(bf16[512,256]{1,0:T(8,128)(2,1)} %feat_hbm.1), channel_id=1, source_target_pairs={{0,16},{1,5},{2,18},{3,7},{4,20},{5,9},{6,22},{7,11},{8,24},{9,13}... | collective-permute-start | bytes 786440 | tf_op jit(solution)/shard_map/ppermute | solution.py:35
  2.3 11.9 %collective-permute-start.1 = (bf16[512,256]{1,0:T(8,128)(2,1)}, bf16[512,256]{1,0:T(8,128)(2,1)S(1)}, u32[]{:S(2)}, u32[]{:S(2)}) collective-permute-start(bf16[512,256]{1,0:T(8,128)(2,1)} %feat_hbm.1), channel_id=1, source_target_pairs={{0,48},{1,13},{2,50},{3,15},{4,52},{5,1},{6,54},{7,3},{8,56},{9,5}... | collective-permute-start | bytes 786440 | tf_op jit(solution)/shard_map/ppermute | solution.py:35
  3.9 10.3 %collective-permute-start.2 = (bf16[512,256]{1,0:T(8,128)(2,1)}, bf16[512,256]{1,0:T(8,128)(2,1)S(1)}, u32[]{:S(2)}, u32[]{:S(2)}) collective-permute-start(bf16[512,256]{1,0:T(8,128)(2,1)} %feat_hbm.1), channel_id=1, source_target_pairs={{0,32},{1,9},{2,34},{3,11},{4,36},{5,13},{6,38},{7,15},{8,40},{9,1... | collective-permute-start | bytes 786440 | tf_op jit(solution)/shard_map/ppermute | solution.py:35
  5.8 8.4 %collective-permute-start.3 = (bf16[512,256]{1,0:T(8,128)(2,1)}, bf16[512,256]{1,0:T(8,128)(2,1)S(1)}, u32[]{:S(2)}, u32[]{:S(2)}) collective-permute-start(bf16[512,256]{1,0:T(8,128)(2,1)} %feat_hbm.1), channel_id=1, source_target_pairs={{0,64},{1,65},{2,66},{3,67},{4,68},{5,69},{6,70},{7,71},{8,72},{9,... | collective-permute-start | bytes 786440 | tf_op jit(solution)/shard_map/ppermute | solution.py:35
  8.4 5.8 %copy-start.5 = (bf16[512,256]{1,0:T(8,128)(2,1)S(1)}, bf16[512,256]{1,0:T(8,128)(2,1)}, u32[]{:S(2)}) copy-start(bf16[512,256]{1,0:T(8,128)(2,1)} %feat_hbm.1) | copy-start | bytes 786436
  14.2 7.8 %copy-start.3 = (s32[320]{0:T(512)S(1)}, s32[320]{0:T(512)}, u32[]{:S(2)}) copy-start(s32[320]{0:T(512)} %rows_ref.2) | copy-start | bytes 3844
  14.3 13.4 %collective-permute-start.4 = (bf16[512,256]{1,0:T(8,128)(2,1)S(1)}, bf16[512,256]{1,0:T(8,128)(2,1)S(1)}, u32[]{:S(2)}, u32[]{:S(2)}) collective-permute-start(bf16[512,256]{1,0:T(8,128)(2,1)S(1)} %collective-permute-done.3), channel_id=1, source_target_pairs={{0,16},{1,5},{2,18},{3,7},{4,20},{5,9},{6,22},{7,11},{8,24},{9,13}... | collective-permute-start | bytes 786440 | tf_op jit(solution)/shard_map/ppermute | solution.py:35
  15.3 12.5 %collective-permute-start.5 = (bf16[512,256]{1,0:T(8,128)(2,1)S(1)}, bf16[512,256]{1,0:T(8,128)(2,1)S(1)}, u32[]{:S(2)}, u32[]{:S(2)}) collective-permute-start(bf16[512,256]{1,0:T(8,128)(2,1)S(1)} %collective-permute-done.3), channel_id=1, source_target_pairs={{0,48},{1,13},{2,50},{3,15},{4,52},{5,1},{6,54},{7,3},{8,56},{9,5}... | collective-permute-start | bytes 786440 | tf_op jit(solution)/shard_map/ppermute | solution.py:35
  17.6 10.1 %collective-permute-start.6 = (bf16[512,256]{1,0:T(8,128)(2,1)S(1)}, bf16[512,256]{1,0:T(8,128)(2,1)S(1)}, u32[]{:S(2)}, u32[]{:S(2)}) collective-permute-start(bf16[512,256]{1,0:T(8,128)(2,1)S(1)} %collective-permute-done.2), channel_id=1, source_target_pairs={{0,64},{1,65},{2,66},{3,67},{4,68},{5,69},{6,70},{7,71},{8,72},{9,... | collective-permute-start | bytes 786440 | tf_op jit(solution)/shard_map/ppermute | solution.py:35
  18.7 16.0 %collective-permute-start.11 = (bf16[2048,256]{1,0:T(8,128)(2,1)S(1)}, bf16[2048,256]{1,0:T(8,128)(2,1)S(1)}, u32[]{:S(2)}, u32[]{:S(2)}) collective-permute-start(bf16[2048,256]{1,0:T(8,128)(2,1)S(1)} %pad_maximum_fusion.1.refs_0_), channel_id=1, source_target_pairs={{0,4},{1,17},{2,6},{3,19},{4,8},{5,21},{6,10},{7,23},{8,12},{9,25}... | collective-permute-start | bytes 3145736 | tf_op jit(solution)/shard_map/ppermute | solution.py:35
  19.4 15.3 %collective-permute-start.12 = (bf16[2048,256]{1,0:T(8,128)(2,1)S(1)}, bf16[2048,256]{1,0:T(8,128)(2,1)S(1)}, u32[]{:S(2)}, u32[]{:S(2)}) collective-permute-start(bf16[2048,256]{1,0:T(8,128)(2,1)S(1)} %pad_maximum_fusion.1.refs_0_), channel_id=1, source_target_pairs={{0,12},{1,49},{2,14},{3,51},{4,0},{5,53},{6,2},{7,55},{8,4},{9,57}... | collective-permute-start | bytes 3145736 | tf_op jit(solution)/shard_map/ppermute | solution.py:35
  27.7 2.4 %copy-start.9 = (s32[320]{0:T(512)S(1)}, s32[320]{0:T(512)}, u32[]{:S(2)}) copy-start(s32[320]{0:T(512)} %param.11) | copy-start | bytes 3844
  27.8 17.7 %collective-permute-start.10 = (bf16[2048,256]{1,0:T(8,128)(2,1)S(1)}, bf16[2048,256]{1,0:T(8,128)(2,1)S(1)}, u32[]{:S(2)}, u32[]{:S(2)}) collective-permute-start(bf16[2048,256]{1,0:T(8,128)(2,1)S(1)} %pad_maximum_fusion.2.refs_1_), channel_id=1, source_target_pairs={{0,12},{1,49},{2,14},{3,51},{4,0},{5,53},{6,2},{7,55},{8,4},{9,57}... | collective-permute-start | bytes 3145736 | tf_op jit(solution)/shard_map/ppermute | solution.py:35
  28.7 17.3 %collective-permute-start.9 = (bf16[2048,256]{1,0:T(8,128)(2,1)S(1)}, bf16[2048,256]{1,0:T(8,128)(2,1)S(1)}, u32[]{:S(2)}, u32[]{:S(2)}) collective-permute-start(bf16[2048,256]{1,0:T(8,128)(2,1)S(1)} %pad_maximum_fusion.2.refs_1_), channel_id=1, source_target_pairs={{0,4},{1,17},{2,6},{3,19},{4,8},{5,21},{6,10},{7,23},{8,12},{9,25}... | collective-permute-start | bytes 3145736 | tf_op jit(solution)/shard_map/ppermute | solution.py:35
  38.0 14.6 %collective-permute-start.15 = (bf16[1024,256]{1,0:T(8,128)(2,1)S(1)}, bf16[1024,256]{1,0:T(8,128)(2,1)S(1)}, u32[]{:S(2)}, u32[]{:S(2)}) collective-permute-start(bf16[1024,256]{1,0:T(8,128)(2,1)S(1)} %slice.119), channel_id=1, source_target_pairs={{0,4},{1,17},{2,6},{3,19},{4,8},{5,21},{6,10},{7,23},{8,12},{9,25}... | collective-permute-start | bytes 1572872 | tf_op jit(solution)/shard_map/ppermute | solution.py:35
  40.0 12.7 %collective-permute-start.16 = (bf16[1024,256]{1,0:T(8,128)(2,1)S(1)}, bf16[1024,256]{1,0:T(8,128)(2,1)S(1)}, u32[]{:S(2)}, u32[]{:S(2)}) collective-permute-start(bf16[1024,256]{1,0:T(8,128)(2,1)S(1)} %slice.120), channel_id=1, source_target_pairs={{0,12},{1,49},{2,14},{3,51},{4,0},{5,53},{6,2},{7,55},{8,4},{9,57}... | collective-permute-start | bytes 1572872 | tf_op jit(solution)/shard_map/ppermute | solution.py:35
  46.0 11.2 %collective-permute-start.13 = (bf16[1024,256]{1,0:T(8,128)(2,1)S(1)}, bf16[1024,256]{1,0:T(8,128)(2,1)S(1)}, u32[]{:S(2)}, u32[]{:S(2)}) collective-permute-start(bf16[1024,256]{1,0:T(8,128)(2,1)S(1)} %slice.121), channel_id=1, source_target_pairs={{0,4},{1,17},{2,6},{3,19},{4,8},{5,21},{6,10},{7,23},{8,12},{9,25}... | collective-permute-start | bytes 1572872 | tf_op jit(solution)/shard_map/ppermute | solution.py:35
  47.1 10.1 %collective-permute-start.14 = (bf16[1024,256]{1,0:T(8,128)(2,1)S(1)}, bf16[1024,256]{1,0:T(8,128)(2,1)S(1)}, u32[]{:S(2)}, u32[]{:S(2)}) collective-permute-start(bf16[1024,256]{1,0:T(8,128)(2,1)S(1)} %slice.122), channel_id=1, source_target_pairs={{0,12},{1,49},{2,14},{3,51},{4,0},{5,53},{6,2},{7,55},{8,4},{9,57}... | collective-permute-start | bytes 1572872 | tf_op jit(solution)/shard_map/ppermute | solution.py:35
  59.8 13.4 %copy-start.1 = (bf16[2,512,256]{2,1,0:T(8,128)(2,1)}, bf16[2,512,256]{2,1,0:T(8,128)(2,1)S(1)}, u32[]{:S(2)}) copy-start(bf16[2,512,256]{2,1,0:T(8,128)(2,1)S(1)} %get-tuple-element.141.keep_ref) | copy-start | bytes 1572868
  59.8 2.0 %collective-permute-start.17 = (bf16[2,512,256]{2,1,0:T(8,128)(2,1)S(1)}, bf16[2,512,256]{2,1,0:T(8,128)(2,1)S(1)}, u32[]{:S(2)}, u32[]{:S(2)}) collective-permute-start(bf16[2,512,256]{2,1,0:T(8,128)(2,1)S(1)} %get-tuple-element.142), channel_id=1, source_target_pairs={{0,1},{1,0},{2,3},{3,2},{4,5},{5,4},{6,7},{7,6},{8,9},{9,8},{10,11... | collective-permute-start | bytes 1572872 | tf_op jit(solution)/shard_map/ppermute | solution.py:35
  61.8 11.4 %copy-start.4 = (bf16[2,512,256]{2,1,0:T(8,128)(2,1)}, bf16[2,512,256]{2,1,0:T(8,128)(2,1)S(1)}, u32[]{:S(2)}) copy-start(bf16[2,512,256]{2,1,0:T(8,128)(2,1)S(1)} %collective-permute-done.17.near_ref) | copy-start | bytes 1572868
  61.9 10.5 %collective-permute-start.18 = (bf16[512,256]{1,0:T(8,128)(2,1)S(1)}, bf16[512,256]{1,0:T(8,128)(2,1)S(1)}, u32[]{:S(2)}, u32[]{:S(2)}) collective-permute-start(bf16[512,256]{1,0:T(8,128)(2,1)S(1)} %fusion.9), channel_id=1, source_target_pairs={{0,2},{1,3},{2,0},{3,1},{4,6},{5,7},{6,4},{7,5},{8,10},{9,11},{10,... | collective-permute-start | bytes 786440 | tf_op jit(solution)/shard_map/ppermute | solution.py:35
  65.6 1.2 collective-permute-start.7
  66.7 5.6 %collective-permute-start.8 = (f32[16,128]{1,0:T(8,128)S(1)}, f32[16,128]{1,0:T(8,128)S(1)}, u32[]{:S(2)}, u32[]{:S(2)}) collective-permute-start(f32[16,128]{1,0:T(8,128)S(1)} %add.192), channel_id=1, source_target_pairs={{0,2},{1,3},{2,0},{3,1},{4,6},{5,7},{6,4},{7,5},{8,10},{9,11},{10,... | collective-permute-start | bytes 24584 | tf_op jit(solution)/shard_map/ppermute | solution.py:35
  77.5 9.6 %collective-permute-start.19 = (bf16[512,256]{1,0:T(8,128)(2,1)}, bf16[512,256]{1,0:T(8,128)(2,1)S(1)}, u32[]{:S(2)}, u32[]{:S(2)}) collective-permute-start(bf16[512,256]{1,0:T(8,128)(2,1)} %get-tuple-element.179.own), channel_id=1, source_target_pairs={{0,2},{1,3},{2,0},{3,1},{4,6},{5,7},{6,4},{7,5},{8,10},{9,11},{10,... | collective-permute-start | bytes 786440 | tf_op jit(solution)/shard_map/ppermute | solution.py:35
  81.8 5.3 %collective-permute-start.22 = (f32[256,256]{1,0:T(8,128)S(1)}, f32[256,256]{1,0:T(8,128)S(1)}, u32[]{:S(2)}, u32[]{:S(2)}) collective-permute-start(f32[256,256]{1,0:T(8,128)S(1)} %constant_dynamic-slice_fusion), channel_id=1, source_target_pairs={{0,1},{1,0},{2,3},{3,2},{4,5},{5,4},{6,7},{7,6},{8,9},{9,8},{10,11... | collective-permute-start | bytes 786440 | tf_op jit(solution)/shard_map/ppermute | solution.py:35
  81.9 8.3 %collective-permute-start.20 = (bf16[512,256]{1,0:T(8,128)(2,1)}, bf16[512,256]{1,0:T(8,128)(2,1)S(1)}, u32[]{:S(2)}, u32[]{:S(2)}) collective-permute-start(bf16[512,256]{1,0:T(8,128)(2,1)} %get-tuple-element.179.own), channel_id=1, source_target_pairs={{0,1},{1,0},{2,3},{3,2},{4,5},{5,4},{6,7},{7,6},{8,9},{9,8},{10,11... | collective-permute-start | bytes 786440 | tf_op jit(solution)/shard_map/ppermute | solution.py:35
  87.2 3.1 %collective-permute-start.21 = (bf16[512,256]{1,0:T(8,128)(2,1)S(1)}, bf16[512,256]{1,0:T(8,128)(2,1)S(1)}, u32[]{:S(2)}, u32[]{:S(2)}) collective-permute-start(bf16[512,256]{1,0:T(8,128)(2,1)S(1)} %collective-permute-done.19.far), channel_id=1, source_target_pairs={{0,1},{1,0},{2,3},{3,2},{4,5},{5,4},{6,7},{7,6},{8,9},{9,8},{10,11... | collective-permute-start | bytes 786440 | tf_op jit(solution)/shard_map/ppermute | solution.py:35
  88.2 9.1 %collective-permute-start.23 = (bf16[256,256]{1,0:T(8,128)(2,1)S(1)}, bf16[256,256]{1,0:T(8,128)(2,1)S(1)}, u32[]{:S(2)}, u32[]{:S(2)}) collective-permute-start(bf16[256,256]{1,0:T(8,128)(2,1)S(1)} %add_convert_fusion.12), channel_id=1, source_target_pairs={{0,64},{1,65},{2,66},{3,67},{4,68},{5,69},{6,70},{7,71},{8,72},{9,... | collective-permute-start | bytes 393224 | tf_op jit(solution)/shard_map/ppermute | solution.py:35
  94.0 21.1 %collective-permute-start.25 = (bf16[1024,256]{1,0:T(8,128)(2,1)S(1)}, bf16[1024,256]{1,0:T(8,128)(2,1)S(1)}, u32[]{:S(2)}, u32[]{:S(2)}) collective-permute-start(bf16[1024,256]{1,0:T(8,128)(2,1)S(1)} %get-tuple-element.161), channel_id=1, source_target_pairs={{0,4},{1,17},{2,6},{3,19},{4,8},{5,21},{6,10},{7,23},{8,12},{9,25}... | collective-permute-start | bytes 1572872 | tf_op jit(solution)/shard_map/ppermute | solution.py:35
  96.2 18.9 %collective-permute-start.26 = (bf16[1024,256]{1,0:T(8,128)(2,1)S(1)}, bf16[1024,256]{1,0:T(8,128)(2,1)S(1)}, u32[]{:S(2)}, u32[]{:S(2)}) collective-permute-start(bf16[1024,256]{1,0:T(8,128)(2,1)S(1)} %get-tuple-element.162), channel_id=1, source_target_pairs={{0,12},{1,49},{2,14},{3,51},{4,0},{5,53},{6,2},{7,55},{8,4},{9,57}... | collective-permute-start | bytes 1572872 | tf_op jit(solution)/shard_map/ppermute | solution.py:35
  97.3 8.1 %collective-permute-start.24 = (bf16[256,256]{1,0:T(8,128)(2,1)S(1)}, bf16[256,256]{1,0:T(8,128)(2,1)S(1)}, u32[]{:S(2)}, u32[]{:S(2)}) collective-permute-start(bf16[256,256]{1,0:T(8,128)(2,1)S(1)} %add_convert_fusion.11), channel_id=1, source_target_pairs={{0,2},{1,3},{2,0},{3,1},{4,6},{5,7},{6,4},{7,5},{8,10},{9,11},{10,... | collective-permute-start | bytes 393224 | tf_op jit(solution)/shard_map/ppermute | solution.py:35
  108.4 14.1 %collective-permute-start.27 = (bf16[1280,256]{1,0:T(8,128)(2,1)S(1)}, bf16[1280,256]{1,0:T(8,128)(2,1)S(1)}, u32[]{:S(2)}, u32[]{:S(2)}) collective-permute-start(bf16[1280,256]{1,0:T(8,128)(2,1)S(1)} %get-tuple-element.173), channel_id=1, source_target_pairs={{0,4},{1,17},{2,6},{3,19},{4,8},{5,21},{6,10},{7,23},{8,12},{9,25}... | collective-permute-start | bytes 1966088 | tf_op jit(solution)/shard_map/ppermute | solution.py:35
  108.8 13.6 %collective-permute-start.28 = (bf16[1280,256]{1,0:T(8,128)(2,1)S(1)}, bf16[1280,256]{1,0:T(8,128)(2,1)S(1)}, u32[]{:S(2)}, u32[]{:S(2)}) collective-permute-start(bf16[1280,256]{1,0:T(8,128)(2,1)S(1)} %get-tuple-element.174), channel_id=1, source_target_pairs={{0,12},{1,49},{2,14},{3,51},{4,0},{5,53},{6,2},{7,55},{8,4},{9,57}... | collective-permute-start | bytes 1966088 | tf_op jit(solution)/shard_map/ppermute | solution.py:35
  115.6 16.1 %collective-permute-start.29 = (bf16[2048,256]{1,0:T(8,128)(2,1)S(1)}, bf16[2048,256]{1,0:T(8,128)(2,1)S(1)}, u32[]{:S(2)}, u32[]{:S(2)}) collective-permute-start(bf16[2048,256]{1,0:T(8,128)(2,1)S(1)} %pad_maximum_fusion.3), channel_id=1, source_target_pairs={{0,4},{1,17},{2,6},{3,19},{4,8},{5,21},{6,10},{7,23},{8,12},{9,25}... | collective-permute-start | bytes 3145736 | tf_op jit(solution)/shard_map/ppermute | solution.py:35
  116.4 15.3 %collective-permute-start.30 = (bf16[2048,256]{1,0:T(8,128)(2,1)S(1)}, bf16[2048,256]{1,0:T(8,128)(2,1)S(1)}, u32[]{:S(2)}, u32[]{:S(2)}) collective-permute-start(bf16[2048,256]{1,0:T(8,128)(2,1)S(1)} %pad_maximum_fusion.4), channel_id=1, source_target_pairs={{0,12},{1,49},{2,14},{3,51},{4,0},{5,53},{6,2},{7,55},{8,4},{9,57}... | collective-permute-start | bytes 3145736 | tf_op jit(solution)/shard_map/ppermute | solution.py:35
  122.5 1.3 copy-start.6
  124.0 23.0 %collective-permute-start.34 = (bf16[2304,256]{1,0:T(8,128)(2,1)S(1)}, bf16[2304,256]{1,0:T(8,128)(2,1)}, u32[]{:S(2)}, u32[]{:S(2)}) collective-permute-start(bf16[2304,256]{1,0:T(8,128)(2,1)S(1)} %pad_maximum_fusion), channel_id=1, source_target_pairs={{0,4},{1,17},{2,6},{3,19},{4,8},{5,21},{6,10},{7,23},{8,12},{9,25}... | collective-permute-start | bytes 3538952 | tf_op jit(solution)/shard_map/ppermute | solution.py:35
  124.6 22.4 %collective-permute-start.35 = (bf16[2048,256]{1,0:T(8,128)(2,1)}, bf16[2048,256]{1,0:T(8,128)(2,1)}, u32[]{:S(2)}, u32[]{:S(2)}) collective-permute-start(bf16[2048,256]{1,0:T(8,128)(2,1)} %pad_maximum_fusion.5), channel_id=1, source_target_pairs={{0,12},{1,49},{2,14},{3,51},{4,0},{5,53},{6,2},{7,55},{8,4},{9,57}... | collective-permute-start | bytes 3145736 | tf_op jit(solution)/shard_map/ppermute | solution.py:35
  133.0 10.3 %collective-permute-start.31 = (bf16[512,256]{1,0:T(8,128)(2,1)}, bf16[512,256]{1,0:T(8,128)(2,1)}, u32[]{:S(2)}, u32[]{:S(2)}) collective-permute-start(bf16[512,256]{1,0:T(8,128)(2,1)} %get-tuple-element.204), channel_id=1, source_target_pairs={{0,48},{1,13},{2,50},{3,15},{4,52},{5,1},{6,54},{7,3},{8,56},{9,5}... | collective-permute-start | bytes 786440 | tf_op jit(solution)/shard_map/ppermute | solution.py:35
  136.2 10.8 %collective-permute-start.32 = (bf16[512,256]{1,0:T(8,128)(2,1)}, bf16[512,256]{1,0:T(8,128)(2,1)}, u32[]{:S(2)}, u32[]{:S(2)}) collective-permute-start(bf16[512,256]{1,0:T(8,128)(2,1)} %get-tuple-element.203), channel_id=1, source_target_pairs={{0,16},{1,5},{2,18},{3,7},{4,20},{5,9},{6,22},{7,11},{8,24},{9,13}... | collective-permute-start | bytes 786440 | tf_op jit(solution)/shard_map/ppermute | solution.py:35
  136.2 10.8 %collective-permute-start.33 = (bf16[512,256]{1,0:T(8,128)(2,1)}, bf16[512,256]{1,0:T(8,128)(2,1)S(1)}, u32[]{:S(2)}, u32[]{:S(2)}) collective-permute-start(bf16[512,256]{1,0:T(8,128)(2,1)} %get-tuple-element.202), channel_id=1, source_target_pairs={{0,64},{1,65},{2,66},{3,67},{4,68},{5,69},{6,70},{7,71},{8,72},{9,... | collective-permute-start | bytes 786440 | tf_op jit(solution)/shard_map/ppermute | solution.py:35
  149.9 18.0 %copy-start.7 = (f32[512,256]{1,0:T(8,128)S(1)}, f32[512,256]{1,0:T(8,128)}, u32[]{:S(2)}) copy-start(f32[512,256]{1,0:T(8,128)} %get-tuple-element.144) | copy-start | bytes 1572868
  150.8 12.2 %collective-permute-start.37 = (bf16[768,256]{1,0:T(8,128)(2,1)}, bf16[768,256]{1,0:T(8,128)(2,1)S(1)}, u32[]{:S(2)}, u32[]{:S(2)}) collective-permute-start(bf16[768,256]{1,0:T(8,128)(2,1)} %get-tuple-element.210), channel_id=1, source_target_pairs={{0,48},{1,13},{2,50},{3,15},{4,52},{5,1},{6,54},{7,3},{8,56},{9,5}... | collective-permute-start | bytes 1179656 | tf_op jit(solution)/shard_map/ppermute | solution.py:35
  153.2 13.5 %collective-permute-start.38 = (bf16[768,256]{1,0:T(8,128)(2,1)}, bf16[768,256]{1,0:T(8,128)(2,1)}, u32[]{:S(2)}, u32[]{:S(2)}) collective-permute-start(bf16[768,256]{1,0:T(8,128)(2,1)} %get-tuple-element.211), channel_id=1, source_target_pairs={{0,16},{1,5},{2,18},{3,7},{4,20},{5,9},{6,22},{7,11},{8,24},{9,13}... | collective-permute-start | bytes 1179656 | tf_op jit(solution)/shard_map/ppermute | solution.py:35
  153.2 13.5 %collective-permute-start.39 = (bf16[768,256]{1,0:T(8,128)(2,1)S(1)}, bf16[768,256]{1,0:T(8,128)(2,1)}, u32[]{:S(2)}, u32[]{:S(2)}) collective-permute-start(bf16[768,256]{1,0:T(8,128)(2,1)S(1)} %get-tuple-element.212), channel_id=1, source_target_pairs={{0,32},{1,9},{2,34},{3,11},{4,36},{5,13},{6,38},{7,15},{8,40},{9,1... | collective-permute-start | bytes 1179656 | tf_op jit(solution)/shard_map/ppermute | solution.py:35
  156.4 11.5 %collective-permute-start.36 = (bf16[512,256]{1,0:T(8,128)(2,1)S(1)}, bf16[512,256]{1,0:T(8,128)(2,1)S(1)}, u32[]{:S(2)}, u32[]{:S(2)}) collective-permute-start(bf16[512,256]{1,0:T(8,128)(2,1)S(1)} %add_convert_fusion.8), channel_id=1, source_target_pairs={{0,64},{1,65},{2,66},{3,67},{4,68},{5,69},{6,70},{7,71},{8,72},{9,... | collective-permute-start | bytes 786440 | tf_op jit(solution)/shard_map/ppermute | solution.py:35
  167.8 2.3 %collective-permute-start.40 = (f32[256,256]{1,0:T(8,128)S(1)}, f32[256,256]{1,0:T(8,128)S(1)}, u32[]{:S(2)}, u32[]{:S(2)}) collective-permute-start(f32[256,256]{1,0:T(8,128)S(1)} %convert_multiply_fusion), channel_id=1, source_target_pairs={{0,1},{1,0},{2,3},{3,2},{4,5},{5,4},{6,7},{7,6},{8,9},{9,8},{10,11... | collective-permute-start | bytes 786440 | tf_op jit(solution)/shard_map/ppermute | solution.py:35
  (3 other events, 2.5 us)

commit v4 on v3

--- a/solution.py
+++ b/solution.py
@@ -45,22 +45,6 @@
 
 def swap_low(value):
     return move(value, lambda z, x, y, h, c: (z + 1, x, y, h, c))
-
-
-def swap_x(value):
-    return move(value, lambda z, x, y, h, c: (z, x ^ 1, y, h, c))
-
-
-def swap_xx(value):
-    return move(value, lambda z, x, y, h, c: (z, x + 2, y, h, c))
-
-
-def swap_y(value):
-    return move(value, lambda z, x, y, h, c: (z, x, y ^ 1, h, c))
-
-
-def swap_yy(value):
-    return move(value, lambda z, x, y, h, c: (z, x, y + 2, h, c))
 
 
 def move_p(value, by):
@@ -136,23 +120,26 @@
     return mask.astype(jnp.float32).astype(jnp.bfloat16)
 
 
-def each_group(first, last, meta_ref, masks_ref, buf, sems, body):
-    def fetch(group):
-        slot = lax.rem(group, DEPTH)
-        for u in range(GROUP):
-            tile = unpack(meta_ref[group * GROUP + u])[0]
-            pltpu.make_async_copy(masks_ref.at[tile], buf.at[slot, u], sems.at[slot]).start()
-
+def fetch_tiles(group, meta_ref, masks_ref, buf, sems):
+    slot = lax.rem(group, DEPTH)
+    for u in range(GROUP):
+        tile = unpack(meta_ref[group * GROUP + u])[0]
+        pltpu.make_async_copy(masks_ref.at[tile], buf.at[slot, u], sems.at[slot]).start()
+
+
+def first_groups(first, last, *fetch_args):
     for ahead in range(DEPTH - 1):
 
         @pl.when(first + ahead < last)
         def _():
-            fetch(first + ahead)
-
+            fetch_tiles(first + ahead, *fetch_args)
+
+
+def each_group(first, last, meta_ref, masks_ref, buf, sems, body):
     def turn(group, carry):
         @pl.when(group + DEPTH - 1 < last)
         def _():
-            fetch(group + DEPTH - 1)
+            fetch_tiles(group + DEPTH - 1, meta_ref, masks_ref, buf, sems)
 
         slot = lax.rem(group, DEPTH)
         pltpu.make_async_copy(masks_ref.at[pl.ds(0, GROUP)], buf.at[slot], sems.at[slot]).wait()
@@ -172,6 +159,8 @@
         keep_ref, give_ref, feats, buf, sems, total = refs
     else:
         total, feats, buf, sems = refs
+    first, last = bounds_ref[begin], bounds_ref[end]
+    first_groups(first, last, meta_ref, masks_ref, buf, sems)
     start = 0
     for piece in pieces:
         feats[start : start + piece.shape[0], :] = piece[...]
@@ -188,7 +177,7 @@
             )
             total[pl.ds(pl.multiple_of(row * TILE, TILE), TILE), :] += part
 
-    each_group(bounds_ref[begin], bounds_ref[end], meta_ref, masks_ref, buf, sems, body)
+    each_group(first, last, meta_ref, masks_ref, buf, sems, body)
     if last_call:
         quarter = keep_ref.shape[1]
         core, high = bounds_ref[CLASSES + 1], bounds_ref[CLASSES + 2]
@@ -236,15 +225,27 @@
 
 
 def backward_kernel(which, count, meta_ref, bounds_ref, masks_ref, own, far, near, cross, *refs):
-    extra, refs = (refs[0], refs[1:]) if which == 2 else (None, refs)
-    outs = refs[:count]
-    grads, buf, sems, total = refs[count:]
+    arrived, refs = (refs[:2], refs[2:]) if which % 2 else (None, refs)
+    outs, refs = refs[:count], refs[count:]
+    if which == 1:
+        passed, refs = refs[0], refs[1:]
+    grads, buf, sems, total = refs
     quarter = own.shape[0]
     core, high = bounds_ref[CLASSES + 1], bounds_ref[CLASSES + 2]
+    first, last = bounds_ref[which], bounds_ref[which + 1]
+    first_groups(first, last, meta_ref, masks_ref, buf, sems)
     for piece, h, c in ((own, 0, 0), (far, 1, 0), (near, 0, 1), (cross, 1, 1)):
         place = ((high + h) % 2) * 2 + (core + c) % 2
         grads[pl.ds(pl.multiple_of(place * quarter, quarter), quarter), :] = piece[...]
-    total[...] = jnp.zeros_like(total)
+    if arrived is None:
+        total[...] = jnp.zeros_like(total)
+    else:
+        below, above = arrived
+        edge = CLASS_BLOCKS * TILE // 4
+        total[:edge, :] = jnp.zeros((edge, total.shape[1]), jnp.float32)
+        total[edge : 2 * edge, :] = above[:edge, :].astype(jnp.float32)
+        total[2 * edge : 3 * edge, :] = below[:edge, :].astype(jnp.float32)
+        total[3 * edge :, :] = jnp.zeros((edge + TILE, total.shape[1]), jnp.float32)
 
     def body(group, slot):
         for u in range(GROUP):
@@ -257,30 +258,33 @@
             )
             total[pl.ds(pl.multiple_of(block * TILE, TILE), TILE), :] += part
 
-    each_group(bounds_ref[which], bounds_ref[which + 1], meta_ref, masks_ref, buf, sems, body)
-    start = 0
-    for out in outs:
-        size = out.shape[0] if extra is None else out.shape[0] - extra.shape[0]
-        out[:size, :] = total[start : start + size, :].astype(jnp.bfloat16)
-        start += size
-        if extra is not None:
-            out[size:, :] = extra[...]
-
-
-def backward_class(which, meta, bounds, masks, grads, *extra):
+    each_group(first, last, meta_ref, masks_ref, buf, sems, body)
+    size = CLASS_BLOCKS * TILE // (2 if which in (0, 1, 3) else 4)
+    for k, out in enumerate(outs):
+        out[:size, :] = total[k * size : (k + 1) * size, :].astype(jnp.bfloat16)
+    if which == 1:
+        behind = below.shape[0] - edge
+        outs[1][size:, :] = below[edge:, :]
+        passed[:behind, :] = below[edge:, :]
+        passed[behind:, :] = above[edge:, :]
+
+
+def backward_class(which, meta, bounds, masks, grads, *arrived):
     quarter, width = grads[0].shape
     vmem = pl.BlockSpec(memory_space=pltpu.VMEM)
     smem = pl.BlockSpec(memory_space=pltpu.SMEM)
     held = pl.BlockSpec(memory_space=pltpu.HBM)
     count = 2
     blocks = CLASS_BLOCKS // 2 if which in (2, 4) else CLASS_BLOCKS
-    behind = sum(value.shape[0] for value in extra)
-    piece = jax.ShapeDtypeStruct((blocks * TILE // count + behind, width), jnp.bfloat16)
+    sizes = [blocks * TILE // count] * count
+    if which == 1:
+        behind = arrived[0].shape[0] - sizes[0] // 2
+        sizes = [sizes[0], sizes[1] + behind, 2 * behind]
     return pl.pallas_call(
         functools.partial(backward_kernel, which, count),
-        in_specs=[smem, smem, held] + [vmem] * (4 + len(extra)),
-        out_specs=[vmem] * count,
-        out_shape=[piece] * count,
+        in_specs=[smem, smem, held] + [vmem] * (4 + len(arrived)),
+        out_specs=[vmem] * len(sizes),
+        out_shape=[jax.ShapeDtypeStruct((size, width), jnp.bfloat16) for size in sizes],
         scratch_shapes=[
             pltpu.VMEM((4 * quarter + TILE, width), jnp.bfloat16),
             pltpu.VMEM((DEPTH, GROUP, TILE, TILE), jnp.int32),
@@ -290,69 +294,226 @@
         compiler_params=params(41),
         cost_estimate=pl.CostEstimate(flops=0, bytes_accessed=16 * MIB, transcendentals=0),
         name=f"backward_class{which}",
-    )(meta, bounds, masks, *grads, *extra)
+    )(meta, bounds, masks, *grads, *arrived)
+
+
+def before_kernel(feat_ref, self_ref, neigh_ref, cot_ref, keep_ref, pre_ref, neigh_out, cot_out, sum_ref):
+    pre_ref[...] = jnp.dot(feat_ref[...], self_ref[...], preferred_element_type=jnp.float32)
+    neigh_out[...] = neigh_ref[...]
+    cot_out[...] = cot_ref[...]
+    sum_ref[...] = keep_ref[0]
+
+
+def before_dense(features, self_weight, neigh_weight, cotangent, keep):
+    rows, width = features.shape
+    vmem = pl.BlockSpec(memory_space=pltpu.VMEM)
+    return pl.pallas_call(
+        before_kernel,
+        in_specs=[vmem] * 5,
+        out_specs=[vmem] * 4,
+        out_shape=[
+            jax.ShapeDtypeStruct((rows, width), jnp.float32),
+            jax.ShapeDtypeStruct((width, width), jnp.bfloat16),
+            jax.ShapeDtypeStruct((rows, width), jnp.bfloat16),
+            jax.ShapeDtypeStruct((rows, width), jnp.bfloat16),
+        ],
+        compiler_params=params(32),
+        cost_estimate=pl.CostEstimate(
+            flops=2 * rows * width * width, bytes_accessed=2 * MIB, transcendentals=0
+        ),
+        name="before_dense",
+    )(features, self_weight, neigh_weight, cotangent, keep)
 
 
 def dense_kernel(
-    feat_hbm, self_hbm, neigh_hbm, cot_hbm, scale_ref, keep_ref, near_ref, far_ref,
-    out_ref, back_ref, mean_ref, weight_ref,
-    feat_ref, self_ref, neigh_ref, cot_ref, sems,
+    pre_ref, neigh_ref, cot_ref, degree_ref, keep_ref, near_ref, far_ref,
+    mean_ref, grad_ref, agg_ref, out_ref,
 ):
-    rows_first = (((0,), (0,)), ((), ()))
     cols_both = (((1,), (1,)), ((), ()))
     f32 = jnp.float32
-    pairs_in = (
-        (feat_hbm, feat_ref), (self_hbm, self_ref), (neigh_hbm, neigh_ref), (cot_hbm, cot_ref)
-    )
-    copies = [pltpu.make_async_copy(a, b, sems.at[k]) for k, (a, b) in enumerate(pairs_in)]
-    for copy in copies:
-        copy.start()
-    summed = keep_ref[0].astype(f32) + near_ref[0].astype(f32) + far_ref[...].astype(f32)
-    scale = jnp.concatenate([scale_ref[...]] * (self_hbm.shape[1] // TILE), axis=1)
+    inverse = lax.rsqrt(jnp.maximum(degree_ref[...], 1.0))
+    width = pre_ref.shape[1]
+    columns = [
+        jnp.broadcast_to(inverse[r : r + 1, :], (TILE, TILE)).T for r in range(inverse.shape[0])
+    ]
+    scale = jnp.concatenate([jnp.concatenate(columns, axis=0)] * (width // TILE), axis=1)
+    summed = keep_ref[...].astype(f32) + near_ref[0].astype(f32) + far_ref[...].astype(f32)
     agg = (summed * scale).astype(jnp.bfloat16)
-    for copy in copies:
-        copy.wait()
-    feats = feat_ref[...]
-    pre = jnp.dot(feats, self_ref[...], preferred_element_type=f32) + jnp.dot(
-        agg, neigh_ref[...], preferred_element_type=f32
-    )
+    pre = pre_ref[...] + jnp.dot(agg, neigh_ref[...], preferred_element_type=f32)
     sig = jax.nn.sigmoid(pre)
     out_ref[...] = (pre * sig).astype(jnp.bfloat16)
     grad = (cot_ref[...].astype(f32) * sig * (1.0 + pre * (1.0 - sig))).astype(jnp.bfloat16)
     mean = lax.dot_general(grad, neigh_ref[...], cols_both, preferred_element_type=f32) * scale
     mean_ref[...] = mean.astype(jnp.bfloat16)
-    width = feats.shape[1]
-    weight_ref[:width, :] = lax.dot_general(feats, grad, rows_first, preferred_element_type=f32)
-    weight_ref[width:, :] = lax.dot_general(agg, grad, rows_first, preferred_element_type=f32)
-    back_ref[...] = lax.dot_general(grad, self_ref[...], cols_both, preferred_element_type=f32)
-
-
-def dense(features, self_weight, neigh_weight, cotangent, scale, keep, near, far):
-    rows, width = features.shape
+    grad_ref[...] = grad
+    agg_ref[...] = agg
+
+
+def dense(pre, neigh_weight, cotangent, degree, keep, near, far):
+    rows, width = pre.shape
     vmem = pl.BlockSpec(memory_space=pltpu.VMEM)
     return pl.pallas_call(
         dense_kernel,
-        in_specs=[pl.BlockSpec(memory_space=pl.ANY)] * 4 + [vmem] * 4,
+        in_specs=[vmem] * 7,
         out_specs=[vmem] * 4,
-        scratch_shapes=[
-            pltpu.VMEM((rows, width), jnp.bfloat16),
-            pltpu.VMEM((width, width), jnp.bfloat16),
-            pltpu.VMEM((width, width), jnp.bfloat16),
-            pltpu.VMEM((rows, width), jnp.bfloat16),
-            pltpu.SemaphoreType.DMA((4,)),
-        ],
-        out_shape=[
-            jax.ShapeDtypeStruct((rows, width), jnp.bfloat16),
-            jax.ShapeDtypeStruct((rows, width), jnp.float32),
-            jax.ShapeDtypeStruct((rows, width), jnp.bfloat16),
-            jax.ShapeDtypeStruct((2 * width, width), jnp.float32),
-        ],
-        compiler_params=params(56),
+        out_shape=[jax.ShapeDtypeStruct((rows, width), jnp.bfloat16)] * 4,
+        compiler_params=params(32),
         cost_estimate=pl.CostEstimate(
-            flops=6 * 2 * rows * width * width, bytes_accessed=4 * MIB, transcendentals=rows * width
+            flops=2 * 2 * rows * width * width, bytes_accessed=4 * MIB, transcendentals=rows * width
         ),
         name="dense",
-    )(features, self_weight, neigh_weight, cotangent, scale, keep, near, far)
+    )(pre, neigh_weight, cotangent, degree, keep, near, far)
+
+
+def weights_kernel(core_ref, feat_ref, agg_ref, grad_ref, mine_ref, theirs_ref):
+    rows_first = (((0,), (0,)), ((), ()))
+    f32 = jnp.float32
+    grad = grad_ref[...]
+    parts = [
+        lax.dot_general(value[...], grad, rows_first, preferred_element_type=f32)
+        for value in (feat_ref, agg_ref)
+    ]
+    on_first = core_ref[0] == 0
+    mine_ref[...] = jnp.where(on_first, parts[0], parts[1])
+    theirs_ref[...] = jnp.where(on_first, parts[1], parts[0])
+
+
+def weight_parts(core, features, agg, grad):
+    rows, width = features.shape
+    vmem = pl.BlockSpec(memory_space=pltpu.VMEM)
+    return pl.pallas_call(
+        weights_kernel,
+        in_specs=[pl.BlockSpec(memory_space=pltpu.SMEM)] + [vmem] * 3,
+        out_specs=[vmem] * 2,
+        out_shape=[
+            jax.ShapeDtypeStruct((width, width), jnp.float32),
+            jax.ShapeDtypeStruct((width, width), jnp.float32),
+        ],
+        compiler_params=params(32),
+        cost_estimate=pl.CostEstimate(
+            flops=2 * 2 * rows * width * width, bytes_accessed=2 * MIB, transcendentals=0
+        ),
+        name="weight_parts",
+    )(core.reshape(1), features, agg, grad)
+
+
+def ring_sum(own, below, above, across, odd):
+    own, below, above, across = (v.astype(jnp.float32) for v in (own, below, above, across))
+    beside, beyond = jnp.where(odd, below, above), jnp.where(odd, above, below)
+    return (own + beside) + (beyond + across)
+
+
+def join_kernel(here_ref, below_ref, above_ref, *outs):
+    rows = outs[0].shape[0]
+    for k, out in enumerate(outs):
+        part = slice(k * rows, (k + 1) * rows)
+        out[...] = (
+            here_ref[part, :].astype(jnp.float32)
+            + below_ref[part, :].astype(jnp.float32)
+            + above_ref[part, :].astype(jnp.float32)
+        ).astype(jnp.bfloat16)
+
+
+def join(here, below, above):
+    total, width = here.shape
+    vmem = pl.BlockSpec(memory_space=pltpu.VMEM)
+    return pl.pallas_call(
+        join_kernel,
+        in_specs=[vmem] * 3,
+        out_specs=[vmem] * 4,
+        out_shape=[jax.ShapeDtypeStruct((total // 4, width), jnp.bfloat16)] * 4,
+        compiler_params=params(32),
+        cost_estimate=pl.CostEstimate(flops=0, bytes_accessed=4 * MIB, transcendentals=0),
+        name="join",
+    )(here, below, above)
+
+
+def back_kernel(after_ref, grad_ref, self_ref, out_ref):
+    cols_both = (((1,), (1,)), ((), ()))
+    out_ref[...] = lax.dot_general(
+        grad_ref[...], self_ref[...], cols_both, preferred_element_type=jnp.float32
+    )
+
+
+def self_back(after, grad, self_weight):
+    vmem = pl.BlockSpec(memory_space=pltpu.VMEM)
+    return pl.pallas_call(
+        back_kernel,
+        in_specs=[pl.BlockSpec(memory_space=pl.ANY), vmem, vmem],
+        out_specs=vmem,
+        out_shape=jax.ShapeDtypeStruct(grad.shape, jnp.float32),
+        compiler_params=params(32),
+        cost_estimate=pl.CostEstimate(flops=0, bytes_accessed=MIB, transcendentals=0),
+        name="self_back",
+    )(after, grad, self_weight)
+
+
+def last_join_kernel(
+    odd_ref, here_ref, below_ref, above_ref, back_ref, low_ref, weight_ref, sides_ref,
+    rest_ref, down_ref, up_ref, across_ref, sum_ref,
+):
+    f32 = jnp.float32
+    rows, total, count = back_ref.shape[0], here_ref.shape[0], weight_ref.shape[0]
+    weight = ring_sum(
+        weight_ref[...], sides_ref[:count, :], sides_ref[count:, :], below_ref[total:, :], odd_ref[0] == 1
+    ).astype(jnp.bfloat16)
+    sum_ref[...] = weight
+    for k, out in enumerate((rest_ref, down_ref, up_ref, across_ref)):
+        part = slice(k * rows, (k + 1) * rows)
+        value = here_ref[part, :].astype(f32) + below_ref[part, :].astype(f32) + above_ref[part, :].astype(f32)
+        if k == 0:
+            out[...] = value + back_ref[...]
+            continue
+        if k == 3:
+            value = value + low_ref[...].astype(f32)
+        out[:rows, :] = value.astype(jnp.bfloat16)
+        out[rows:, :] = weight
+
+
+def last_join(odd, here, below, above, back, low, weight, weight_sides):
+    rows, width = back.shape
+    vmem = pl.BlockSpec(memory_space=pltpu.VMEM)
+    message = jax.ShapeDtypeStruct((rows + weight.shape[0], width), jnp.bfloat16)
+    return pl.pallas_call(
+        last_join_kernel,
+        in_specs=[pl.BlockSpec(memory_space=pltpu.SMEM)] + [vmem] * 7,
+        out_specs=[vmem] * 5,
+        out_shape=[
+            jax.ShapeDtypeStruct((rows, width), jnp.float32),
+            message, message, message,
+            jax.ShapeDtypeStruct(weight.shape, jnp.bfloat16),
+        ],
+        compiler_params=params(32),
+        cost_estimate=pl.CostEstimate(flops=0, bytes_accessed=6 * MIB, transcendentals=0),
+        name="last_join",
+    )(odd, here, below, above, back, low, weight, weight_sides)
+
+
+def finish_kernel(norm, odd_ref, rest_ref, low_ref, down_ref, up_ref, across_ref, weight_ref, out_ref, sum_ref):
+    rows = rest_ref.shape[0]
+    arrived = (down_ref, up_ref, across_ref)
+    total = rest_ref[...] + low_ref[...].astype(jnp.float32)
+    for ref in arrived:
+        total += ref[:rows, :].astype(jnp.float32)
+    out_ref[...] = total.astype(jnp.bfloat16)
+    above, below, across = (ref[rows:, :] for ref in arrived)
+    sum_ref[...] = ring_sum(weight_ref[...], below, above, across, odd_ref[0] == 1) * norm
+
+
+def finish(norm, odd, rest, low, from_above, from_below, from_across, weight):
+    vmem = pl.BlockSpec(memory_space=pltpu.VMEM)
+    return pl.pallas_call(
+        functools.partial(finish_kernel, norm),
+        in_specs=[pl.BlockSpec(memory_space=pltpu.SMEM)] + [vmem] * 6,
+        out_specs=[vmem] * 2,
+        out_shape=[
+            jax.ShapeDtypeStruct(rest.shape, jnp.bfloat16),
+            jax.ShapeDtypeStruct(weight.shape, jnp.float32),
+        ],
+        compiler_params=params(32),
+        cost_estimate=pl.CostEstimate(flops=0, bytes_accessed=3 * MIB, transcendentals=0),
+        name="finish",
+    )(odd, rest, low, from_above, from_below, from_across, weight)
 
 
 def plan_tiles(tile_rows, tile_cols, tile_sums, row_blocks):
@@ -444,79 +605,58 @@
     own_degree = lax.dynamic_slice_in_dim(
         degree, (high * 2 + core) * (row_blocks // 4), row_blocks // 4, 0
     )
-    scale = jnp.broadcast_to(
-        lax.rsqrt(jnp.maximum(own_degree, 1.0)).reshape(rows, 1), (rows, TILE)
-    )
 
     near = swap_core(give)
     far = swap_high(add(keep[1], near[1]))
-    output, back, mean, weight = dense(
-        features, self_weight, neigh_weight, cotangent, scale, keep, near, far
-    )
-    def fold(weight, exchange):
-        sent = weight.astype(jnp.bfloat16)
-        return sent.astype(jnp.float32) + exchange(sent).astype(jnp.float32)
-
-    def ring_sum(own, below, above, across, odd):
-        own, below, above, across = (v.astype(jnp.float32) for v in (own, below, above, across))
-        beside, beyond = jnp.where(odd, below, above), jnp.where(odd, above, below)
-        return ((own + beside) + (beyond + across)).astype(jnp.bfloat16)
+    pre, neigh_near, cot_near, kept = before_dense(
+        features, self_weight, neigh_weight, cotangent, keep
+    )
+    mean, grad, agg, output = dense(pre, neigh_near, cot_near, own_degree, kept, near, far)
 
     mean_far = swap_high(mean)
     mean_near = swap_core(mean)
     grads = (mean, mean_far, mean_near, swap_core(mean_far))
-    weight_mine = lax.dynamic_slice_in_dim(weight, core * width, width, 0)
-    weight_theirs = lax.dynamic_slice_in_dim(weight, (1 - core) * width, width, 0)
-    weight = fold(fold(weight_mine + swap_core(weight_theirs), swap_low), swap_high)
-    weight = weight.astype(jnp.bfloat16)
+    weight_mine, weight_theirs = weight_parts(core, features, agg, grad)
+    weight = (weight_mine + swap_core(weight_theirs)).astype(jnp.bfloat16)
+    weight = add(weight, swap_low(weight))
+    weight = add(weight, swap_high(weight))
     row_index = lax.axis_index("row")
     odd_x, odd_y = row_index // 4 % 2 == 1, row_index % 2 == 1
     odd_p, odd_q = jnp.where(core == 0, odd_x, odd_y), jnp.where(core == 0, odd_y, odd_x)
 
-    def backward(which, grads, *extra):
-        return backward_class(which, meta, bounds, tile_masks, grads, *extra)
+    def backward(which, grads, *arrived):
+        return backward_class(which, meta, bounds, tile_masks, grads, *arrived)
 
     far10, far11 = backward(4, grads)
     far10, far11, *grads = tie(far10, far11, *grads)
     below1, above1 = move_q(far10, 1), move_q(far11, -1)
-    far00, far01 = backward(2, grads, weight)
+    far00, far01 = backward(2, grads)
     far00, far01, *grads = tie(far00, far01, *grads)
+    far00, far01 = jnp.concatenate([far00, weight]), jnp.concatenate([far01, weight])
     below0, above0 = move_q(far00, 1), move_q(far01, -1)
-    down, up = backward(3, grads)
-    down, up, below1, above1 = tie(down, up, below1, above1)
-    to_above = jnp.concatenate([add(up[:edge], below1), up[edge:]])
-    to_below = jnp.concatenate([down[:edge], add(down[edge:], above1)])
-    to_above, to_below, *grads = tie(to_above, to_below, *grads)
-    from_below1, from_above1 = move_q(to_above, 1), move_q(to_below, -1)
-    down, up = backward(1, grads)
-    down, up, below0, above0 = tie(down, up, below0, above0)
-    to_above = jnp.concatenate([add(up[:edge], below0[:edge]), up[edge:], below0[edge:]])
-    to_below = jnp.concatenate([down[:edge], add(down[edge:], above0[:edge])])
-    to_above, to_below, *grads = tie(to_above, to_below, *grads)
-    from_below0, from_above0 = move_q(to_above, 1), move_q(to_below, -1)
+    down, up = backward(3, grads, below1, above1)
+    from_below1, from_above1 = move_q(up, 1), move_q(down, -1)
+    down, up, weight_sides = backward(1, grads, below0, above0)
+    from_below0, from_above0 = move_q(up, 1), move_q(down, -1)
     here0, here1 = backward(0, grads)
     here0, here1, from_below1, from_above1 = tie(here0, here1, from_below1, from_above1)
-    total = add(here1, from_below1, from_above1)
-    parts = [total[k * rows : (k + 1) * rows] for k in range(4)]
+    odd_q, odd_p = (v.astype(jnp.int32).reshape(1) for v in (odd_q, odd_p))
+    parts = join(here1, from_below1, from_above1)
     moved = (move_p(parts[1], -1), move_p(parts[2], 1))
     low_far = swap_low(parts[3])
+    back = self_back(parts[0], grad, self_weight)
     own_part, *moved, low_far = tie(parts[0], *moved, low_far)
     low_own = swap_low(add(own_part, *moved))
     low_far, from_below0, from_above0 = tie(low_far, from_below0, from_above0)
-    weight = ring_sum(weight, below0[edge:], above0[edge:], from_below0[2 * edge :], odd_q)
-    total = add(here0[rows:], from_below0[rows : 2 * edge], from_above0[rows:])
-    down = jnp.concatenate([total[:rows], weight])
-    up = jnp.concatenate([total[rows : 2 * rows], weight])
-    across = jnp.concatenate([add(total[2 * rows :], low_far), weight])
+    rest, down, up, across, weight = last_join(
+        odd_q, here0, from_below0, from_above0, back, low_far,
+        weight, weight_sides,
+    )
     from_above, from_below, from_across = move_p(down, -1), move_p(up, 1), move_p(across, 2)
-    weight = ring_sum(weight, from_below[rows:], from_above[rows:], from_across[rows:], odd_p)
-    weight = weight.astype(jnp.float32)
-    incoming = sum(
-        value[:rows].astype(jnp.float32)
-        for value in (here0, from_below0, from_above0, low_own, from_above, from_below, from_across)
-    )
-    grad_feat = (back + incoming).astype(jnp.bfloat16)
-    weight = weight * ((rows * lax.axis_size(BOTH)) ** (-0.5))
+    norm = (rows * lax.axis_size(BOTH)) ** (-0.5)
+    grad_feat, weight = finish(
+        norm, odd_p, rest, low_own, from_above, from_below, from_across, weight
+    )
     weight_other = swap_core(weight)
     self_total = jnp.where(core == 0, weight, weight_other)
     neigh_total = jnp.where(core == 0, weight_other, weight)

time: 173 us -> 168 us (0.971)
  other arithmetic: 13.5 us -> 3.38 us
  starting transfers between devices: 62.4 us -> 53.1 us
  waiting for transfers between devices: 42.5 us -> 50.3 us
  Pallas kernels: 46.6 us -> 52.4 us
    ppermute x41, starting transfers between devices: 62.4 us -> 53.1 us  [move(): return lax.ppermute(value, BOTH, pairs(step))]
    ppermute x41, waiting for transfers between devices: 42.5 us -> 50.3 us  [move(): return lax.ppermute(value, BOTH, pairs(step))]
    convert_element_type x5 -> x1, other arithmetic: 4.26 us -> 0.04 us  [local(): weight = (weight_mine + swap_core(weight_theirs)).astype(jnp.bfloat16)]
    unnamed x20 -> x30, local copies, waits for them, and re-layouts: 1.67 us -> 5.32 us
    convert_element_type x8 -> x4, other arithmetic: 3.98 us -> 1.26 us  [add(): sum((value.astype(jnp.float32) for value in values)).astype(jnp.bfloat16)]
    pallas_call x5, Pallas kernels: 16 us -> 18.6 us  [backward_class(): pl.pallas_call(functools.partial(backward_kernel, which, count), in_specs...]
    concatenate x5 -> x1, other arithmetic: 2.24 us -> 0.09 us  [local(): jnp.concatenate([far01, weight])]
    pallas_call x1 -> x7, Pallas kernels: 4.31 us -> 6.15 us  [the longest x1 2.25 us: last_join(): pl.pallas_call(last_join_kernel, in_specs=[pl.BlockSpec(memory_space=pltp...]
  transfers between devices with their start and end apart: 41 -> 41, of which waited for: 14 -> 17; matrix products, arithmetic and copies ran while one was open for 6% -> 2% of each run, Pallas kernels for 23% -> 27%
where the time goes in v4:
time: 168 us; the launch traced here: 166 us
  starting transfers between devices  53.1 us (32%)
  Pallas kernels  52.4 us (31%)
  waiting for transfers between devices  50.3 us (30%)
  local copies, waits for them, and re-layouts  5.46 us (3%)
  other arithmetic  3.38 us (2%)
    ppermute x41, starting transfers between devices, move(): return lax.ppermute(value, BOTH, pairs(step))  53.1 us
    ppermute x41, waiting for transfers between devices, move(): return lax.ppermute(value, BOTH, pairs(step))  50.3 us
    pallas_call x5, Pallas kernels, backward_class(): pl.pallas_call(functools.partial(backward_kernel, which, count), in_specs...  18.6 us
    pallas_call x5, Pallas kernels, forward_class(): pl.pallas_call(functools.partial(forward_kernel, begin, end, len(pieces),...  16.2 us
    pallas_call x2, Pallas kernels, degrees(): pl.pallas_call(functools.partial(degree_kernel, part * slots), in_specs=[...  11.4 us
    unnamed x30, local copies, waits for them, and re-layouts  5.32 us
  transfers between devices with their start and end apart: 41, of which 17 were waited for; matrix products, arithmetic and copies ran while one was open for 2% of the time, Pallas kernels for 27%

profile of v4, /device:TPU:0, one launch (start us, length us, event | category | flops | bytes accessed | tf_op | source)
XLA Modules:
  0.0 165.7 jit_solution(1476411103259369786)
XLA Ops:
  0.6 1.6 collective-permute-start
  2.3 1.7 %collective-permute-start.1 = (bf16[512,256]{1,0:T(8,128)(2,1)}, bf16[512,256]{1,0:T(8,128)(2,1)S(1)}, u32[]{:S(2)}, u32[]{:S(2)}) collective-permute-start(bf16[512,256]{1,0:T(8,128)(2,1)} %feat_ref.3), channel_id=1, source_target_pairs={{0,48},{1,13},{2,50},{3,15},{4,52},{5,1},{6,54},{7,3},{8,56},{9,5}... | collective-permute-start | bytes 786440 | tf_op jit(solution)/shard_map/ppermute | solution.py:35
  3.9 1.9 %collective-permute-start.2 = (bf16[512,256]{1,0:T(8,128)(2,1)}, bf16[512,256]{1,0:T(8,128)(2,1)S(1)}, u32[]{:S(2)}, u32[]{:S(2)}) collective-permute-start(bf16[512,256]{1,0:T(8,128)(2,1)} %feat_ref.3), channel_id=1, source_target_pairs={{0,32},{1,9},{2,34},{3,11},{4,36},{5,13},{6,38},{7,15},{8,40},{9,1... | collective-permute-start | bytes 786440 | tf_op jit(solution)/shard_map/ppermute | solution.py:35
  5.8 1.9 %collective-permute-start.3 = (bf16[512,256]{1,0:T(8,128)(2,1)}, bf16[512,256]{1,0:T(8,128)(2,1)S(1)}, u32[]{:S(2)}, u32[]{:S(2)}) collective-permute-start(bf16[512,256]{1,0:T(8,128)(2,1)} %feat_ref.3), channel_id=1, source_target_pairs={{0,64},{1,65},{2,66},{3,67},{4,68},{5,69},{6,70},{7,71},{8,72},{9,... | collective-permute-start | bytes 786440 | tf_op jit(solution)/shard_map/ppermute | solution.py:35
  8.4 5.7 %degrees0.1 = (f32[160,128]{1,0:T(8,128)S(1)}, f32[16,128]{1,0:T(8,128)S(1)}) custom-call(s32[320]{0:T(512)S(1)} %copy-done.12, s32[320,128,128]{2,1,0:T(8,128)} %masks_ref.23), custom_call_target="tpu_custom_call" | custom-call | bytes 20971520 | tf_op jit(solution)/shard_map/degrees0/pallas_call | solution.py:96
  15.3 2.3 %collective-permute-start.5 = (bf16[512,256]{1,0:T(8,128)(2,1)S(1)}, bf16[512,256]{1,0:T(8,128)(2,1)S(1)}, u32[]{:S(2)}, u32[]{:S(2)}) collective-permute-start(bf16[512,256]{1,0:T(8,128)(2,1)S(1)} %collective-permute-done.3), channel_id=1, source_target_pairs={{0,48},{1,13},{2,50},{3,15},{4,52},{5,1},{6,54},{7,3},{8,56},{9,5}... | collective-permute-start | bytes 786440 | tf_op jit(solution)/shard_map/ppermute | solution.py:35
  18.7 2.0 %collective-permute-start.10 = (bf16[2048,256]{1,0:T(8,128)(2,1)S(1)}, bf16[2048,256]{1,0:T(8,128)(2,1)S(1)}, u32[]{:S(2)}, u32[]{:S(2)}) collective-permute-start(bf16[2048,256]{1,0:T(8,128)(2,1)S(1)} %pad_maximum_fusion.refs_0_), channel_id=1, source_target_pairs={{0,12},{1,49},{2,14},{3,51},{4,0},{5,53},{6,2},{7,55},{8,4},{9,57}... | collective-permute-start | bytes 3145736 | tf_op jit(solution)/shard_map/ppermute | solution.py:35
  20.8 5.7 %degrees1.1 = (f32[160,128]{1,0:T(8,128)S(1)}, f32[16,128]{1,0:T(8,128)S(1)}) custom-call(s32[320]{0:T(512)S(1)} %copy-done.13, s32[320,128,128]{2,1,0:T(8,128)} %masks_ref.23), custom_call_target="tpu_custom_call" | custom-call | bytes 20971520 | tf_op jit(solution)/shard_map/degrees1/pallas_call | solution.py:96
  27.4 2.6 %collective-permute-start.8 = (bf16[2048,256]{1,0:T(8,128)(2,1)S(1)}, bf16[2048,256]{1,0:T(8,128)(2,1)S(1)}, u32[]{:S(2)}, u32[]{:S(2)}) collective-permute-start(bf16[2048,256]{1,0:T(8,128)(2,1)S(1)} %pad_maximum_fusion.1.refs_1_), channel_id=1, source_target_pairs={{0,12},{1,49},{2,14},{3,51},{4,0},{5,53},{6,2},{7,55},{8,4},{9,57}... | collective-permute-start | bytes 3145736 | tf_op jit(solution)/shard_map/ppermute | solution.py:35
  31.0 3.7 %forward_class0.1.refs_2_ = f32[2176,256]{1,0:T(8,128)S(1)} custom-call(s32[400]{0:T(512)S(1)} %broadcast_add_fusion.meta_ref, s32[8]{0:T(128)S(1)} %pad_add_fusion.bounds_ref, s32[320,128,128]{2,1,0:T(8,128)} %masks_ref.23, bf16[2048,256]{1,0:T(8,128)(2,1)S(1)} %pad_maximum_fusion.refs_0_, bf16[2048,256]{1,0:T(8,128)(2,1)S(1)} %pad_maximum_fusion.1.refs_1_), custom_call_target="tpu_custom_call" | custom-call | bytes 16777216 | tf_op jit(solution)/shard_map/forward_class0/pallas_call | solution.py:214
  34.8 2.0 %collective-permute-done.9.refs_0_ = bf16[2048,256]{1,0:T(8,128)(2,1)S(1)} collective-permute-done((bf16[2048,256]{1,0:T(8,128)(2,1)S(1)}, bf16[2048,256]{1,0:T(8,128)(2,1)S(1)}, u32[]{:S(2)}, u32[]{:S(2)}) %collective-permute-start.9) | collective-permute-done | bytes 1048608 | tf_op jit(solution)/shard_map/ppermute | solution.py:35
  36.8 3.2 %forward_class1.1.refs_2_ = f32[2176,256]{1,0:T(8,128)S(1)} custom-call(s32[400]{0:T(512)S(1)} %broadcast_add_fusion.meta_ref, s32[8]{0:T(128)S(1)} %pad_add_fusion.bounds_ref, s32[320,128,128]{2,1,0:T(8,128)} %masks_ref.23, bf16[2048,256]{1,0:T(8,128)(2,1)S(1)} %collective-permute-done.9.refs_0_, ...), custom_call_target="tpu_custom_call", output_to_operand_aliasing={{}: (5, {})} | custom-call | bytes 16777216 | tf_op jit(solution)/shard_map/forward_class1/pallas_call | solution.py:214
  40.7 2.7 %collective-permute-start.14 = (bf16[1024,256]{1,0:T(8,128)(2,1)S(1)}, bf16[1024,256]{1,0:T(8,128)(2,1)S(1)}, u32[]{:S(2)}, u32[]{:S(2)}) collective-permute-start(bf16[1024,256]{1,0:T(8,128)(2,1)S(1)} %slice.23), channel_id=1, source_target_pairs={{0,12},{1,49},{2,14},{3,51},{4,0},{5,53},{6,2},{7,55},{8,4},{9,57}... | collective-permute-start | bytes 1572872 | tf_op jit(solution)/shard_map/ppermute | solution.py:35
  43.4 4.6 %collective-permute-done.7.refs_0_ = bf16[2048,256]{1,0:T(8,128)(2,1)S(1)} collective-permute-done((bf16[2048,256]{1,0:T(8,128)(2,1)S(1)}, bf16[2048,256]{1,0:T(8,128)(2,1)S(1)}, u32[]{:S(2)}, u32[]{:S(2)}) %collective-permute-start.7) | collective-permute-done | bytes 1048608 | tf_op jit(solution)/shard_map/ppermute | solution.py:35
  48.2 3.2 %collective-permute-start.12 = (bf16[1024,256]{1,0:T(8,128)(2,1)S(1)}, bf16[1024,256]{1,0:T(8,128)(2,1)S(1)}, u32[]{:S(2)}, u32[]{:S(2)}) collective-permute-start(bf16[1024,256]{1,0:T(8,128)(2,1)S(1)} %slice.25), channel_id=1, source_target_pairs={{0,12},{1,49},{2,14},{3,51},{4,0},{5,53},{6,2},{7,55},{8,4},{9,57}... | collective-permute-start | bytes 1572872 | tf_op jit(solution)/shard_map/ppermute | solution.py:35
  51.4 3.2 %forward_class3.1.refs_2_ = f32[2176,256]{1,0:T(8,128)S(1)} custom-call(s32[400]{0:T(512)S(1)} %broadcast_add_fusion.meta_ref, s32[8]{0:T(128)S(1)} %pad_add_fusion.bounds_ref, s32[320,128,128]{2,1,0:T(8,128)} %masks_ref.23, bf16[2048,256]{1,0:T(8,128)(2,1)S(1)} %collective-permute-done.7.refs_0_, ...), custom_call_target="tpu_custom_call", output_to_operand_aliasing={{}: (5, {})} | custom-call | bytes 16777216 | tf_op jit(solution)/shard_map/forward_class3/pallas_call | solution.py:214
  54.6 2.8 %forward_class2.1.refs_2_ = f32[2176,256]{1,0:T(8,128)S(1)} custom-call(s32[400]{0:T(512)S(1)} %broadcast_add_fusion.meta_ref, s32[8]{0:T(128)S(1)} %pad_add_fusion.bounds_ref, s32[320,128,128]{2,1,0:T(8,128)} %masks_ref.23, bf16[1024,256]{1,0:T(8,128)(2,1)S(1)} %collective-permute-done.13.refs_0_, ...), custom_call_target="tpu_custom_call", output_to_operand_aliasing={{}: (5, {})} | custom-call | bytes 16777216 | tf_op jit(solution)/shard_map/forward_class2/pallas_call | solution.py:214
  57.5 1.7 %collective-permute-done.11.refs_0_ = bf16[1024,256]{1,0:T(8,128)(2,1)S(1)} collective-permute-done((bf16[1024,256]{1,0:T(8,128)(2,1)S(1)}, bf16[1024,256]{1,0:T(8,128)(2,1)S(1)}, u32[]{:S(2)}, u32[]{:S(2)}) %collective-permute-start.11) | collective-permute-done | bytes 524320 | tf_op jit(solution)/shard_map/ppermute | solution.py:35
  59.2 3.2 %forward_class4.1 = (bf16[2,512,256]{2,1,0:T(8,128)(2,1)S(1)}, bf16[2,512,256]{2,1,0:T(8,128)(2,1)S(1)}) custom-call(s32[400]{0:T(512)S(1)} %broadcast_add_fusion.meta_ref, s32[8]{0:T(128)S(1)} %pad_add_fusion.bounds_ref, s32[320,128,128]{2,1,0:T(8,128)} %masks_ref.23, bf16[1024,256]{1,0:T(8,128)(2,1)S(1)} %collective-permute-done.11.refs_0_, ...), custom_call_target="tpu_custom_call" | custom-call | bytes 16777216 | tf_op jit(solution)/shard_map/forward_class4/pallas_call | solution.py:214
  62.6 1.9 %collective-permute-done.17.near_ref = bf16[2,512,256]{2,1,0:T(8,128)(2,1)S(1)} collective-permute-done((bf16[2,512,256]{2,1,0:T(8,128)(2,1)S(1)}, bf16[2,512,256]{2,1,0:T(8,128)(2,1)S(1)}, u32[]{:S(2)}, u32[]{:S(2)}) %collective-permute-start.17) | collective-permute-done | bytes 524320 | tf_op jit(solution)/shard_map/ppermute | solution.py:35
  64.5 3.1 %collective-permute-start.18 = (bf16[512,256]{1,0:T(8,128)(2,1)S(1)}, bf16[512,256]{1,0:T(8,128)(2,1)S(1)}, u32[]{:S(2)}, u32[]{:S(2)}) collective-permute-start(bf16[512,256]{1,0:T(8,128)(2,1)S(1)} %fusion.1), channel_id=1, source_target_pairs={{0,2},{1,3},{2,0},{3,1},{4,6},{5,7},{6,4},{7,5},{8,10},{9,11},{10,... | collective-permute-start | bytes 786440 | tf_op jit(solution)/shard_map/ppermute | solution.py:35
  69.3 5.3 %collective-permute-done.16 = f32[16,128]{1,0:T(8,128)S(1)} collective-permute-done((f32[16,128]{1,0:T(8,128)S(1)}, f32[16,128]{1,0:T(8,128)S(1)}, u32[]{:S(2)}, u32[]{:S(2)}) %collective-permute-start.16) | collective-permute-done | bytes 8224 | tf_op jit(solution)/shard_map/ppermute | solution.py:35
  76.5 3.1 %collective-permute-start.19 = (bf16[512,256]{1,0:T(8,128)(2,1)S(1)}, bf16[512,256]{1,0:T(8,128)(2,1)S(1)}, u32[]{:S(2)}, u32[]{:S(2)}) collective-permute-start(bf16[512,256]{1,0:T(8,128)(2,1)S(1)} %get-tuple-element.155.own), channel_id=1, source_target_pairs={{0,2},{1,3},{2,0},{3,1},{4,6},{5,7},{6,4},{7,5},{8,10},{9,11},{10,... | collective-permute-start | bytes 786440 | tf_op jit(solution)/shard_map/ppermute | solution.py:35
  79.6 2.0 %collective-permute-start.30 = (bf16[256,256]{1,0:T(8,128)(2,1)S(1)}, bf16[256,256]{1,0:T(8,128)(2,1)S(1)}, u32[]{:S(2)}, u32[]{:S(2)}) collective-permute-start(bf16[256,256]{1,0:T(8,128)(2,1)S(1)} %add_convert_fusion.4), channel_id=1, source_target_pairs={{0,64},{1,65},{2,66},{3,67},{4,68},{5,69},{6,70},{7,71},{8,72},{9,... | collective-permute-start | bytes 393224 | tf_op jit(solution)/shard_map/ppermute | solution.py:35
  81.6 5.5 %collective-permute-done.19.far = bf16[512,256]{1,0:T(8,128)(2,1)S(1)} collective-permute-done((bf16[512,256]{1,0:T(8,128)(2,1)S(1)}, bf16[512,256]{1,0:T(8,128)(2,1)S(1)}, u32[]{:S(2)}, u32[]{:S(2)}) %collective-permute-start.19) | collective-permute-done | bytes 262176 | tf_op jit(solution)/shard_map/ppermute | solution.py:35
  87.2 3.7 %collective-permute-done.30 = bf16[256,256]{1,0:T(8,128)(2,1)S(1)} collective-permute-done((bf16[256,256]{1,0:T(8,128)(2,1)S(1)}, bf16[256,256]{1,0:T(8,128)(2,1)S(1)}, u32[]{:S(2)}, u32[]{:S(2)}) %collective-permute-start.30) | collective-permute-done | bytes 131104 | tf_op jit(solution)/shard_map/ppermute | solution.py:35
  92.0 3.3 %backward_class4.1 = (bf16[1024,256]{1,0:T(8,128)(2,1)S(1)}, bf16[1024,256]{1,0:T(8,128)(2,1)S(1)}) custom-call(s32[400]{0:T(512)S(1)} %broadcast_add_fusion.meta_ref, s32[8]{0:T(128)S(1)} %pad_add_fusion.bounds_ref, s32[320,128,128]{2,1,0:T(8,128)} %masks_ref.23, bf16[512,256]{1,0:T(8,128)(2,1)S(1)} %get-tuple-element.155.own, ...), custom_call_target="tpu_custom_call" | custom-call | bytes 16777216 | tf_op jit(solution)/shard_map/backward_class4/pallas_call | solution.py:283
  95.2 2.9 %backward_class2.1 = (bf16[1024,256]{1,0:T(8,128)(2,1)S(1)}, bf16[1024,256]{1,0:T(8,128)(2,1)S(1)}) custom-call(s32[400]{0:T(512)S(1)} %broadcast_add_fusion.meta_ref, s32[8]{0:T(128)S(1)} %pad_add_fusion.bounds_ref, s32[320,128,128]{2,1,0:T(8,128)} %masks_ref.23, bf16[512,256]{1,0:T(8,128)(2,1)S(1)} %get-tuple-element.155.own, ...), custom_call_target="tpu_custom_call" | custom-call | bytes 16777216 | tf_op jit(solution)/shard_map/backward_class2/pallas_call | solution.py:283
  98.3 3.2 %collective-permute-start.23 = (bf16[1024,256]{1,0:T(8,128)(2,1)S(1)}, bf16[1024,256]{1,0:T(8,128)(2,1)S(1)}, u32[]{:S(2)}, u32[]{:S(2)}) collective-permute-start(bf16[1024,256]{1,0:T(8,128)(2,1)S(1)} %get-tuple-element.162), channel_id=1, source_target_pairs={{0,12},{1,49},{2,14},{3,51},{4,0},{5,53},{6,2},{7,55},{8,4},{9,57}... | collective-permute-start | bytes 1572872 | tf_op jit(solution)/shard_map/ppermute | solution.py:35
  101.7 3.2 %collective-permute-start.33 = (bf16[1280,256]{1,0:T(8,128)(2,1)S(1)}, bf16[1280,256]{1,0:T(8,128)(2,1)S(1)}, u32[]{:S(2)}, u32[]{:S(2)}) collective-permute-start(bf16[1280,256]{1,0:T(8,128)(2,1)S(1)} %get-tuple-element.200), channel_id=1, source_target_pairs={{0,12},{1,49},{2,14},{3,51},{4,0},{5,53},{6,2},{7,55},{8,4},{9,57}... | collective-permute-start | bytes 1966088 | tf_op jit(solution)/shard_map/ppermute | solution.py:35
  105.0 3.7 %collective-permute-done.22.refs_0_ = bf16[1024,256]{1,0:T(8,128)(2,1)S(1)} collective-permute-done((bf16[1024,256]{1,0:T(8,128)(2,1)S(1)}, bf16[1024,256]{1,0:T(8,128)(2,1)S(1)}, u32[]{:S(2)}, u32[]{:S(2)}) %collective-permute-start.22) | collective-permute-done | bytes 524320 | tf_op jit(solution)/shard_map/ppermute | solution.py:35
  108.7 3.5 %backward_class3.1 = (bf16[2048,256]{1,0:T(8,128)(2,1)S(1)}, bf16[2048,256]{1,0:T(8,128)(2,1)S(1)}) custom-call(s32[400]{0:T(512)S(1)} %broadcast_add_fusion.meta_ref, s32[8]{0:T(128)S(1)} %pad_add_fusion.bounds_ref, s32[320,128,128]{2,1,0:T(8,128)} %masks_ref.23, bf16[512,256]{1,0:T(8,128)(2,1)S(1)} %get-tuple-element.155.own, ...), custom_call_target="tpu_custom_call" | custom-call | bytes 16777216 | tf_op jit(solution)/shard_map/backward_class3/pallas_call | solution.py:283
  112.2 1.7 %collective-permute-start.24 = (bf16[2048,256]{1,0:T(8,128)(2,1)S(1)}, bf16[2048,256]{1,0:T(8,128)(2,1)S(1)}, u32[]{:S(2)}, u32[]{:S(2)}) collective-permute-start(bf16[2048,256]{1,0:T(8,128)(2,1)S(1)} %get-tuple-element.163), channel_id=1, source_target_pairs={{0,4},{1,17},{2,6},{3,19},{4,8},{5,21},{6,10},{7,23},{8,12},{9,25}... | collective-permute-start | bytes 3145736 | tf_op jit(solution)/shard_map/ppermute | solution.py:35
  113.9 2.8 %collective-permute-start.25 = (bf16[2048,256]{1,0:T(8,128)(2,1)S(1)}, bf16[2048,256]{1,0:T(8,128)(2,1)S(1)}, u32[]{:S(2)}, u32[]{:S(2)}) collective-permute-start(bf16[2048,256]{1,0:T(8,128)(2,1)S(1)} %get-tuple-element.164), channel_id=1, source_target_pairs={{0,12},{1,49},{2,14},{3,51},{4,0},{5,53},{6,2},{7,55},{8,4},{9,57}... | collective-permute-start | bytes 3145736 | tf_op jit(solution)/shard_map/ppermute | solution.py:35
  116.7 4.8 %backward_class1.1 = (bf16[2048,256]{1,0:T(8,128)(2,1)}, bf16[2304,256]{1,0:T(8,128)(2,1)}, bf16[512,256]{1,0:T(8,128)(2,1)S(1)}) custom-call(s32[400]{0:T(512)S(1)} %broadcast_add_fusion.meta_ref, s32[8]{0:T(128)S(1)} %pad_add_fusion.bounds_ref, s32[320,128,128]{2,1,0:T(8,128)} %masks_ref.23, bf16[512,256]{1,0:T(8,128)(2,1)S(1)} %get-tuple-element.155.own, ...), custom_call_target="tpu_custom_call" | custom-call | bytes 16777216 | tf_op jit(solution)/shard_map/backward_class1/pallas_call | solution.py:283
  121.5 1.4 collective-permute-start.34
  123.0 1.9 %collective-permute-start.35 = (bf16[2048,256]{1,0:T(8,128)(2,1)}, bf16[2048,256]{1,0:T(8,128)(2,1)S(1)}, u32[]{:S(2)}, u32[]{:S(2)}) collective-permute-start(bf16[2048,256]{1,0:T(8,128)(2,1)} %get-tuple-element.181), channel_id=1, source_target_pairs={{0,12},{1,49},{2,14},{3,51},{4,0},{5,53},{6,2},{7,55},{8,4},{9,57}... | collective-permute-start | bytes 3145736 | tf_op jit(solution)/shard_map/ppermute | solution.py:35
  124.9 4.0 %backward_class0.1 = (bf16[2048,256]{1,0:T(8,128)(2,1)S(1)}, bf16[2048,256]{1,0:T(8,128)(2,1)S(1)}) custom-call(s32[400]{0:T(512)S(1)} %broadcast_add_fusion.meta_ref, s32[8]{0:T(128)S(1)} %pad_add_fusion.bounds_ref, s32[320,128,128]{2,1,0:T(8,128)} %masks_ref.23, bf16[512,256]{1,0:T(8,128)(2,1)S(1)} %get-tuple-element.155.own, ...), custom_call_target="tpu_custom_call" | custom-call | bytes 16777216 | tf_op jit(solution)/shard_map/backward_class0/pallas_call | solution.py:283
  131.2 2.0 %collective-permute-start.27 = (bf16[512,256]{1,0:T(8,128)(2,1)}, bf16[512,256]{1,0:T(8,128)(2,1)}, u32[]{:S(2)}, u32[]{:S(2)}) collective-permute-start(bf16[512,256]{1,0:T(8,128)(2,1)} %get-tuple-element.171), channel_id=1, source_target_pairs={{0,16},{1,5},{2,18},{3,7},{4,20},{5,9},{6,22},{7,11},{8,24},{9,13}... | collective-permute-start | bytes 786440 | tf_op jit(solution)/shard_map/ppermute | solution.py:35
  136.0 3.5 %collective-permute-done.26 = bf16[512,256]{1,0:T(8,128)(2,1)} collective-permute-done((bf16[512,256]{1,0:T(8,128)(2,1)}, bf16[512,256]{1,0:T(8,128)(2,1)}, u32[]{:S(2)}, u32[]{:S(2)}) %collective-permute-start.26) | collective-permute-done | bytes 262176 | tf_op jit(solution)/shard_map/ppermute | solution.py:35
  139.5 2.4 %collective-permute-done.27 = bf16[512,256]{1,0:T(8,128)(2,1)} collective-permute-done((bf16[512,256]{1,0:T(8,128)(2,1)}, bf16[512,256]{1,0:T(8,128)(2,1)}, u32[]{:S(2)}, u32[]{:S(2)}) %collective-permute-start.27) | collective-permute-done | bytes 262176 | tf_op jit(solution)/shard_map/ppermute | solution.py:35
  141.9 1.2 collective-permute-done.35.above_ref
  143.2 1.7 %collective-permute-done.34.below_ref = bf16[2304,256]{1,0:T(8,128)(2,1)S(1)} collective-permute-done((bf16[2304,256]{1,0:T(8,128)(2,1)}, bf16[2304,256]{1,0:T(8,128)(2,1)S(1)}, u32[]{:S(2)}, u32[]{:S(2)}) %collective-permute-start.34) | collective-permute-done | bytes 1179680 | tf_op jit(solution)/shard_map/ppermute | solution.py:35
  145.8 2.2 %last_join.1 = (f32[512,256]{1,0:T(8,128)S(1)}, bf16[768,256]{1,0:T(8,128)(2,1)}, bf16[768,256]{1,0:T(8,128)(2,1)}, bf16[768,256]{1,0:T(8,128)(2,1)}, bf16[256,256]{1,0:T(8,128)(2,1)S(1)}) custom-call(s32[1]{0:T(128)} %bitcast.4.odd_ref, bf16[2048,256]{1,0:T(8,128)(2,1)S(1)} %get-tuple-element.165.here_ref, ...), custom_call_target="tpu_custom_call" | custom-call | bytes 6291456 | tf_op jit(solution)/shard_map/last_join/pallas_call | solution.py:477
  148.0 2.0 %collective-permute-start.38 = (bf16[768,256]{1,0:T(8,128)(2,1)}, bf16[768,256]{1,0:T(8,128)(2,1)S(1)}, u32[]{:S(2)}, u32[]{:S(2)}) collective-permute-start(bf16[768,256]{1,0:T(8,128)(2,1)} %get-tuple-element.191), channel_id=1, source_target_pairs={{0,16},{1,5},{2,18},{3,7},{4,20},{5,9},{6,22},{7,11},{8,24},{9,13}... | collective-permute-start | bytes 1179656 | tf_op jit(solution)/shard_map/ppermute | solution.py:35
  151.8 5.9 %collective-permute-done.36.low_ref = bf16[512,256]{1,0:T(8,128)(2,1)S(1)} collective-permute-done((bf16[512,256]{1,0:T(8,128)(2,1)S(1)}, bf16[512,256]{1,0:T(8,128)(2,1)S(1)}, u32[]{:S(2)}, u32[]{:S(2)}) %collective-permute-start.36) | collective-permute-done | bytes 262176 | tf_op jit(solution)/shard_map/ppermute | solution.py:35
  157.7 3.8 %collective-permute-done.38.up_ref = bf16[768,256]{1,0:T(8,128)(2,1)S(1)} collective-permute-done((bf16[768,256]{1,0:T(8,128)(2,1)}, bf16[768,256]{1,0:T(8,128)(2,1)S(1)}, u32[]{:S(2)}, u32[]{:S(2)}) %collective-permute-start.38) | collective-permute-done | bytes 393248 | tf_op jit(solution)/shard_map/ppermute | solution.py:35
  163.4 1.5 collective-permute-done.40
  (111 shorter events, 21.0 us)
Async XLA Ops:
  0.6 13.6 %copy-start = (bf16[512,256]{1,0:T(8,128)(2,1)S(1)}, bf16[512,256]{1,0:T(8,128)(2,1)}, u32[]{:S(2)}) copy-start(bf16[512,256]{1,0:T(8,128)(2,1)} %feat_ref.3) | copy-start | bytes 786436
  0.6 13.5 %collective-permute-start = (bf16[512,256]{1,0:T(8,128)(2,1)}, bf16[512,256]{1,0:T(8,128)(2,1)S(1)}, u32[]{:S(2)}, u32[]{:S(2)}) collective-permute-start(bf16[512,256]{1,0:T(8,128)(2,1)} %feat_ref.3), channel_id=1, source_target_pairs={{0,16},{1,5},{2,18},{3,7},{4,20},{5,9},{6,22},{7,11},{8,24},{9,13}... | collective-permute-start | bytes 786440 | tf_op jit(solution)/shard_map/ppermute | solution.py:35
  2.3 11.9 %collective-permute-start.1 = (bf16[512,256]{1,0:T(8,128)(2,1)}, bf16[512,256]{1,0:T(8,128)(2,1)S(1)}, u32[]{:S(2)}, u32[]{:S(2)}) collective-permute-start(bf16[512,256]{1,0:T(8,128)(2,1)} %feat_ref.3), channel_id=1, source_target_pairs={{0,48},{1,13},{2,50},{3,15},{4,52},{5,1},{6,54},{7,3},{8,56},{9,5}... | collective-permute-start | bytes 786440 | tf_op jit(solution)/shard_map/ppermute | solution.py:35
  3.9 10.3 %collective-permute-start.2 = (bf16[512,256]{1,0:T(8,128)(2,1)}, bf16[512,256]{1,0:T(8,128)(2,1)S(1)}, u32[]{:S(2)}, u32[]{:S(2)}) collective-permute-start(bf16[512,256]{1,0:T(8,128)(2,1)} %feat_ref.3), channel_id=1, source_target_pairs={{0,32},{1,9},{2,34},{3,11},{4,36},{5,13},{6,38},{7,15},{8,40},{9,1... | collective-permute-start | bytes 786440 | tf_op jit(solution)/shard_map/ppermute | solution.py:35
  5.8 8.4 %collective-permute-start.3 = (bf16[512,256]{1,0:T(8,128)(2,1)}, bf16[512,256]{1,0:T(8,128)(2,1)S(1)}, u32[]{:S(2)}, u32[]{:S(2)}) collective-permute-start(bf16[512,256]{1,0:T(8,128)(2,1)} %feat_ref.3), channel_id=1, source_target_pairs={{0,64},{1,65},{2,66},{3,67},{4,68},{5,69},{6,70},{7,71},{8,72},{9,... | collective-permute-start | bytes 786440 | tf_op jit(solution)/shard_map/ppermute | solution.py:35
  14.2 6.6 %copy-start.13 = (s32[320]{0:T(512)S(1)}, s32[320]{0:T(512)}, u32[]{:S(2)}) copy-start(s32[320]{0:T(512)} %rows_ref.2) | copy-start | bytes 3844
  14.3 12.2 %collective-permute-start.4 = (bf16[512,256]{1,0:T(8,128)(2,1)S(1)}, bf16[512,256]{1,0:T(8,128)(2,1)S(1)}, u32[]{:S(2)}, u32[]{:S(2)}) collective-permute-start(bf16[512,256]{1,0:T(8,128)(2,1)S(1)} %collective-permute-done.3), channel_id=1, source_target_pairs={{0,16},{1,5},{2,18},{3,7},{4,20},{5,9},{6,22},{7,11},{8,24},{9,13}... | collective-permute-start | bytes 786440 | tf_op jit(solution)/shard_map/ppermute | solution.py:35
  15.3 11.2 %collective-permute-start.5 = (bf16[512,256]{1,0:T(8,128)(2,1)S(1)}, bf16[512,256]{1,0:T(8,128)(2,1)S(1)}, u32[]{:S(2)}, u32[]{:S(2)}) collective-permute-start(bf16[512,256]{1,0:T(8,128)(2,1)S(1)} %collective-permute-done.3), channel_id=1, source_target_pairs={{0,48},{1,13},{2,50},{3,15},{4,52},{5,1},{6,54},{7,3},{8,56},{9,5}... | collective-permute-start | bytes 786440 | tf_op jit(solution)/shard_map/ppermute | solution.py:35
  17.6 8.9 %collective-permute-start.6 = (bf16[512,256]{1,0:T(8,128)(2,1)S(1)}, bf16[512,256]{1,0:T(8,128)(2,1)S(1)}, u32[]{:S(2)}, u32[]{:S(2)}) collective-permute-start(bf16[512,256]{1,0:T(8,128)(2,1)S(1)} %collective-permute-done.2), channel_id=1, source_target_pairs={{0,64},{1,65},{2,66},{3,67},{4,68},{5,69},{6,70},{7,71},{8,72},{9,... | collective-permute-start | bytes 786440 | tf_op jit(solution)/shard_map/ppermute | solution.py:35
  18.7 16.0 %collective-permute-start.10 = (bf16[2048,256]{1,0:T(8,128)(2,1)S(1)}, bf16[2048,256]{1,0:T(8,128)(2,1)S(1)}, u32[]{:S(2)}, u32[]{:S(2)}) collective-permute-start(bf16[2048,256]{1,0:T(8,128)(2,1)S(1)} %pad_maximum_fusion.refs_0_), channel_id=1, source_target_pairs={{0,12},{1,49},{2,14},{3,51},{4,0},{5,53},{6,2},{7,55},{8,4},{9,57}... | collective-permute-start | bytes 3145736 | tf_op jit(solution)/shard_map/ppermute | solution.py:35
  20.7 16.0 %collective-permute-start.9 = (bf16[2048,256]{1,0:T(8,128)(2,1)S(1)}, bf16[2048,256]{1,0:T(8,128)(2,1)S(1)}, u32[]{:S(2)}, u32[]{:S(2)}) collective-permute-start(bf16[2048,256]{1,0:T(8,128)(2,1)S(1)} %pad_maximum_fusion.refs_0_), channel_id=1, source_target_pairs={{0,4},{1,17},{2,6},{3,19},{4,8},{5,21},{6,10},{7,23},{8,12},{9,25}... | collective-permute-start | bytes 3145736 | tf_op jit(solution)/shard_map/ppermute | solution.py:35
  26.6 21.4 %collective-permute-start.7 = (bf16[2048,256]{1,0:T(8,128)(2,1)S(1)}, bf16[2048,256]{1,0:T(8,128)(2,1)S(1)}, u32[]{:S(2)}, u32[]{:S(2)}) collective-permute-start(bf16[2048,256]{1,0:T(8,128)(2,1)S(1)} %pad_maximum_fusion.1.refs_1_), channel_id=1, source_target_pairs={{0,4},{1,17},{2,6},{3,19},{4,8},{5,21},{6,10},{7,23},{8,12},{9,25}... | collective-permute-start | bytes 3145736 | tf_op jit(solution)/shard_map/ppermute | solution.py:35
  27.4 20.6 %collective-permute-start.8 = (bf16[2048,256]{1,0:T(8,128)(2,1)S(1)}, bf16[2048,256]{1,0:T(8,128)(2,1)S(1)}, u32[]{:S(2)}, u32[]{:S(2)}) collective-permute-start(bf16[2048,256]{1,0:T(8,128)(2,1)S(1)} %pad_maximum_fusion.1.refs_1_), channel_id=1, source_target_pairs={{0,12},{1,49},{2,14},{3,51},{4,0},{5,53},{6,2},{7,55},{8,4},{9,57}... | collective-permute-start | bytes 3145736 | tf_op jit(solution)/shard_map/ppermute | solution.py:35
  40.1 14.5 %collective-permute-start.13 = (bf16[1024,256]{1,0:T(8,128)(2,1)S(1)}, bf16[1024,256]{1,0:T(8,128)(2,1)S(1)}, u32[]{:S(2)}, u32[]{:S(2)}) collective-permute-start(bf16[1024,256]{1,0:T(8,128)(2,1)S(1)} %slice.22), channel_id=1, source_target_pairs={{0,4},{1,17},{2,6},{3,19},{4,8},{5,21},{6,10},{7,23},{8,12},{9,25}... | collective-permute-start | bytes 1572872 | tf_op jit(solution)/shard_map/ppermute | solution.py:35
  40.7 13.9 %collective-permute-start.14 = (bf16[1024,256]{1,0:T(8,128)(2,1)S(1)}, bf16[1024,256]{1,0:T(8,128)(2,1)S(1)}, u32[]{:S(2)}, u32[]{:S(2)}) collective-permute-start(bf16[1024,256]{1,0:T(8,128)(2,1)S(1)} %slice.23), channel_id=1, source_target_pairs={{0,12},{1,49},{2,14},{3,51},{4,0},{5,53},{6,2},{7,55},{8,4},{9,57}... | collective-permute-start | bytes 1572872 | tf_op jit(solution)/shard_map/ppermute | solution.py:35
  48.1 11.1 %collective-permute-start.11 = (bf16[1024,256]{1,0:T(8,128)(2,1)S(1)}, bf16[1024,256]{1,0:T(8,128)(2,1)S(1)}, u32[]{:S(2)}, u32[]{:S(2)}) collective-permute-start(bf16[1024,256]{1,0:T(8,128)(2,1)S(1)} %slice.24), channel_id=1, source_target_pairs={{0,4},{1,17},{2,6},{3,19},{4,8},{5,21},{6,10},{7,23},{8,12},{9,25}... | collective-permute-start | bytes 1572872 | tf_op jit(solution)/shard_map/ppermute | solution.py:35
  48.2 11.1 %collective-permute-start.12 = (bf16[1024,256]{1,0:T(8,128)(2,1)S(1)}, bf16[1024,256]{1,0:T(8,128)(2,1)S(1)}, u32[]{:S(2)}, u32[]{:S(2)}) collective-permute-start(bf16[1024,256]{1,0:T(8,128)(2,1)S(1)} %slice.25), channel_id=1, source_target_pairs={{0,12},{1,49},{2,14},{3,51},{4,0},{5,53},{6,2},{7,55},{8,4},{9,57}... | collective-permute-start | bytes 1572872 | tf_op jit(solution)/shard_map/ppermute | solution.py:35
  57.5 17.2 %copy-start.7 = (bf16[256,256]{1,0:T(8,128)(2,1)S(1)}, bf16[256,256]{1,0:T(8,128)(2,1)}, u32[]{:S(2)}) copy-start(bf16[256,256]{1,0:T(8,128)(2,1)} %self_ref.3) | copy-start | bytes 393220
  57.5 17.2 %copy-start.8 = (bf16[512,256]{1,0:T(8,128)(2,1)S(1)}, bf16[512,256]{1,0:T(8,128)(2,1)}, u32[]{:S(2)}) copy-start(bf16[512,256]{1,0:T(8,128)(2,1)} %cot_ref.1) | copy-start | bytes 786436
  57.5 17.2 %copy-start.11 = (bf16[256,256]{1,0:T(8,128)(2,1)S(1)}, bf16[256,256]{1,0:T(8,128)(2,1)}, u32[]{:S(2)}) copy-start(bf16[256,256]{1,0:T(8,128)(2,1)} %neigh_ref.1) | copy-start | bytes 393220
  62.5 2.0 %collective-permute-start.17 = (bf16[2,512,256]{2,1,0:T(8,128)(2,1)S(1)}, bf16[2,512,256]{2,1,0:T(8,128)(2,1)S(1)}, u32[]{:S(2)}, u32[]{:S(2)}) collective-permute-start(bf16[2,512,256]{2,1,0:T(8,128)(2,1)S(1)} %get-tuple-element.144), channel_id=1, source_target_pairs={{0,1},{1,0},{2,3},{3,2},{4,5},{5,4},{6,7},{7,6},{8,9},{9,8},{10,11... | collective-permute-start | bytes 1572872 | tf_op jit(solution)/shard_map/ppermute | solution.py:35
  64.5 10.4 %collective-permute-start.18 = (bf16[512,256]{1,0:T(8,128)(2,1)S(1)}, bf16[512,256]{1,0:T(8,128)(2,1)S(1)}, u32[]{:S(2)}, u32[]{:S(2)}) collective-permute-start(bf16[512,256]{1,0:T(8,128)(2,1)S(1)} %fusion.1), channel_id=1, source_target_pairs={{0,2},{1,3},{2,0},{3,1},{4,6},{5,7},{6,4},{7,5},{8,10},{9,11},{10,... | collective-permute-start | bytes 786440 | tf_op jit(solution)/shard_map/ppermute | solution.py:35
  67.6 1.2 collective-permute-start.15
  68.8 5.8 %collective-permute-start.16 = (f32[16,128]{1,0:T(8,128)S(1)}, f32[16,128]{1,0:T(8,128)S(1)}, u32[]{:S(2)}, u32[]{:S(2)}) collective-permute-start(f32[16,128]{1,0:T(8,128)S(1)} %add.136), channel_id=1, source_target_pairs={{0,2},{1,3},{2,0},{3,1},{4,6},{5,7},{6,4},{7,5},{8,10},{9,11},{10,... | collective-permute-start | bytes 24584 | tf_op jit(solution)/shard_map/ppermute | solution.py:35
  76.0 15.9 %copy-start.1 = (bf16[512,256]{1,0:T(8,128)(2,1)}, bf16[512,256]{1,0:T(8,128)(2,1)S(1)}, u32[]{:S(2)}) copy-start(bf16[512,256]{1,0:T(8,128)(2,1)S(1)} %get-tuple-element.176.grad_ref) | copy-start | bytes 786436
  76.4 3.2 %collective-permute-start.29 = (f32[256,256]{1,0:T(8,128)S(1)}, f32[256,256]{1,0:T(8,128)S(1)}, u32[]{:S(2)}, u32[]{:S(2)}) collective-permute-start(f32[256,256]{1,0:T(8,128)S(1)} %get-tuple-element.178), channel_id=1, source_target_pairs={{0,1},{1,0},{2,3},{3,2},{4,5},{5,4},{6,7},{7,6},{8,9},{9,8},{10,11... | collective-permute-start | bytes 786440 | tf_op jit(solution)/shard_map/ppermute | solution.py:35
  76.5 10.7 %collective-permute-start.19 = (bf16[512,256]{1,0:T(8,128)(2,1)S(1)}, bf16[512,256]{1,0:T(8,128)(2,1)S(1)}, u32[]{:S(2)}, u32[]{:S(2)}) collective-permute-start(bf16[512,256]{1,0:T(8,128)(2,1)S(1)} %get-tuple-element.155.own), channel_id=1, source_target_pairs={{0,2},{1,3},{2,0},{3,1},{4,6},{5,7},{6,4},{7,5},{8,10},{9,11},{10,... | collective-permute-start | bytes 786440 | tf_op jit(solution)/shard_map/ppermute | solution.py:35
  79.6 11.3 %collective-permute-start.30 = (bf16[256,256]{1,0:T(8,128)(2,1)S(1)}, bf16[256,256]{1,0:T(8,128)(2,1)S(1)}, u32[]{:S(2)}, u32[]{:S(2)}) collective-permute-start(bf16[256,256]{1,0:T(8,128)(2,1)S(1)} %add_convert_fusion.4), channel_id=1, source_target_pairs={{0,64},{1,65},{2,66},{3,67},{4,68},{5,69},{6,70},{7,71},{8,72},{9,... | collective-permute-start | bytes 393224 | tf_op jit(solution)/shard_map/ppermute | solution.py:35
  81.6 10.3 %collective-permute-start.20 = (bf16[512,256]{1,0:T(8,128)(2,1)S(1)}, bf16[512,256]{1,0:T(8,128)(2,1)S(1)}, u32[]{:S(2)}, u32[]{:S(2)}) collective-permute-start(bf16[512,256]{1,0:T(8,128)(2,1)S(1)} %get-tuple-element.155.own), channel_id=1, source_target_pairs={{0,1},{1,0},{2,3},{3,2},{4,5},{5,4},{6,7},{7,6},{8,9},{9,8},{10,11... | collective-permute-start | bytes 786440 | tf_op jit(solution)/shard_map/ppermute | solution.py:35
  87.2 4.8 %collective-permute-start.21 = (bf16[512,256]{1,0:T(8,128)(2,1)S(1)}, bf16[512,256]{1,0:T(8,128)(2,1)S(1)}, u32[]{:S(2)}, u32[]{:S(2)}) collective-permute-start(bf16[512,256]{1,0:T(8,128)(2,1)S(1)} %collective-permute-done.19.far), channel_id=1, source_target_pairs={{0,1},{1,0},{2,3},{3,2},{4,5},{5,4},{6,7},{7,6},{8,9},{9,8},{10,11... | collective-permute-start | bytes 786440 | tf_op jit(solution)/shard_map/ppermute | solution.py:35
  91.0 10.5 %collective-permute-start.31 = (bf16[256,256]{1,0:T(8,128)(2,1)S(1)}, bf16[256,256]{1,0:T(8,128)(2,1)S(1)}, u32[]{:S(2)}, u32[]{:S(2)}) collective-permute-start(bf16[256,256]{1,0:T(8,128)(2,1)S(1)} %add_convert_fusion.3), channel_id=1, source_target_pairs={{0,2},{1,3},{2,0},{3,1},{4,6},{5,7},{6,4},{7,5},{8,10},{9,11},{10,... | collective-permute-start | bytes 393224 | tf_op jit(solution)/shard_map/ppermute | solution.py:35
  98.2 10.5 %collective-permute-start.22 = (bf16[1024,256]{1,0:T(8,128)(2,1)S(1)}, bf16[1024,256]{1,0:T(8,128)(2,1)S(1)}, u32[]{:S(2)}, u32[]{:S(2)}) collective-permute-start(bf16[1024,256]{1,0:T(8,128)(2,1)S(1)} %get-tuple-element.161), channel_id=1, source_target_pairs={{0,4},{1,17},{2,6},{3,19},{4,8},{5,21},{6,10},{7,23},{8,12},{9,25}... | collective-permute-start | bytes 1572872 | tf_op jit(solution)/shard_map/ppermute | solution.py:35
  98.3 10.4 %collective-permute-start.23 = (bf16[1024,256]{1,0:T(8,128)(2,1)S(1)}, bf16[1024,256]{1,0:T(8,128)(2,1)S(1)}, u32[]{:S(2)}, u32[]{:S(2)}) collective-permute-start(bf16[1024,256]{1,0:T(8,128)(2,1)S(1)} %get-tuple-element.162), channel_id=1, source_target_pairs={{0,12},{1,49},{2,14},{3,51},{4,0},{5,53},{6,2},{7,55},{8,4},{9,57}... | collective-permute-start | bytes 1572872 | tf_op jit(solution)/shard_map/ppermute | solution.py:35
  101.6 15.0 %collective-permute-start.32 = (bf16[1280,256]{1,0:T(8,128)(2,1)S(1)}, bf16[1280,256]{1,0:T(8,128)(2,1)S(1)}, u32[]{:S(2)}, u32[]{:S(2)}) collective-permute-start(bf16[1280,256]{1,0:T(8,128)(2,1)S(1)} %get-tuple-element.201), channel_id=1, source_target_pairs={{0,4},{1,17},{2,6},{3,19},{4,8},{5,21},{6,10},{7,23},{8,12},{9,25}... | collective-permute-start | bytes 1966088 | tf_op jit(solution)/shard_map/ppermute | solution.py:35
  101.7 15.0 %collective-permute-start.33 = (bf16[1280,256]{1,0:T(8,128)(2,1)S(1)}, bf16[1280,256]{1,0:T(8,128)(2,1)S(1)}, u32[]{:S(2)}, u32[]{:S(2)}) collective-permute-start(bf16[1280,256]{1,0:T(8,128)(2,1)S(1)} %get-tuple-element.200), channel_id=1, source_target_pairs={{0,12},{1,49},{2,14},{3,51},{4,0},{5,53},{6,2},{7,55},{8,4},{9,57}... | collective-permute-start | bytes 1966088 | tf_op jit(solution)/shard_map/ppermute | solution.py:35
  112.2 17.2 %collective-permute-start.24 = (bf16[2048,256]{1,0:T(8,128)(2,1)S(1)}, bf16[2048,256]{1,0:T(8,128)(2,1)S(1)}, u32[]{:S(2)}, u32[]{:S(2)}) collective-permute-start(bf16[2048,256]{1,0:T(8,128)(2,1)S(1)} %get-tuple-element.163), channel_id=1, source_target_pairs={{0,4},{1,17},{2,6},{3,19},{4,8},{5,21},{6,10},{7,23},{8,12},{9,25}... | collective-permute-start | bytes 3145736 | tf_op jit(solution)/shard_map/ppermute | solution.py:35
  113.9 15.5 %collective-permute-start.25 = (bf16[2048,256]{1,0:T(8,128)(2,1)S(1)}, bf16[2048,256]{1,0:T(8,128)(2,1)S(1)}, u32[]{:S(2)}, u32[]{:S(2)}) collective-permute-start(bf16[2048,256]{1,0:T(8,128)(2,1)S(1)} %get-tuple-element.164), channel_id=1, source_target_pairs={{0,12},{1,49},{2,14},{3,51},{4,0},{5,53},{6,2},{7,55},{8,4},{9,57}... | collective-permute-start | bytes 3145736 | tf_op jit(solution)/shard_map/ppermute | solution.py:35
  121.5 7.3 %copy-start.9 = (bf16[512,256]{1,0:T(8,128)(2,1)}, bf16[512,256]{1,0:T(8,128)(2,1)S(1)}, u32[]{:S(2)}) copy-start(bf16[512,256]{1,0:T(8,128)(2,1)S(1)} %get-tuple-element.185.sides_ref) | copy-start | bytes 786436
  121.5 23.3 %collective-permute-start.34 = (bf16[2304,256]{1,0:T(8,128)(2,1)}, bf16[2304,256]{1,0:T(8,128)(2,1)S(1)}, u32[]{:S(2)}, u32[]{:S(2)}) collective-permute-start(bf16[2304,256]{1,0:T(8,128)(2,1)} %get-tuple-element.180), channel_id=1, source_target_pairs={{0,4},{1,17},{2,6},{3,19},{4,8},{5,21},{6,10},{7,23},{8,12},{9,25}... | collective-permute-start | bytes 3538952 | tf_op jit(solution)/shard_map/ppermute | solution.py:35
  123.0 20.2 %collective-permute-start.35 = (bf16[2048,256]{1,0:T(8,128)(2,1)}, bf16[2048,256]{1,0:T(8,128)(2,1)S(1)}, u32[]{:S(2)}, u32[]{:S(2)}) collective-permute-start(bf16[2048,256]{1,0:T(8,128)(2,1)} %get-tuple-element.181), channel_id=1, source_target_pairs={{0,12},{1,49},{2,14},{3,51},{4,0},{5,53},{6,2},{7,55},{8,4},{9,57}... | collective-permute-start | bytes 3145736 | tf_op jit(solution)/shard_map/ppermute | solution.py:35
  131.2 8.3 %collective-permute-start.26 = (bf16[512,256]{1,0:T(8,128)(2,1)}, bf16[512,256]{1,0:T(8,128)(2,1)}, u32[]{:S(2)}, u32[]{:S(2)}) collective-permute-start(bf16[512,256]{1,0:T(8,128)(2,1)} %get-tuple-element.170), channel_id=1, source_target_pairs={{0,48},{1,13},{2,50},{3,15},{4,52},{5,1},{6,54},{7,3},{8,56},{9,5}... | collective-permute-start | bytes 786440 | tf_op jit(solution)/shard_map/ppermute | solution.py:35
  131.2 10.8 %collective-permute-start.27 = (bf16[512,256]{1,0:T(8,128)(2,1)}, bf16[512,256]{1,0:T(8,128)(2,1)}, u32[]{:S(2)}, u32[]{:S(2)}) collective-permute-start(bf16[512,256]{1,0:T(8,128)(2,1)} %get-tuple-element.171), channel_id=1, source_target_pairs={{0,16},{1,5},{2,18},{3,7},{4,20},{5,9},{6,22},{7,11},{8,24},{9,13}... | collective-permute-start | bytes 786440 | tf_op jit(solution)/shard_map/ppermute | solution.py:35
  133.2 8.7 %collective-permute-start.28 = (bf16[512,256]{1,0:T(8,128)(2,1)}, bf16[512,256]{1,0:T(8,128)(2,1)}, u32[]{:S(2)}, u32[]{:S(2)}) collective-permute-start(bf16[512,256]{1,0:T(8,128)(2,1)} %get-tuple-element.172), channel_id=1, source_target_pairs={{0,64},{1,65},{2,66},{3,67},{4,68},{5,69},{6,70},{7,71},{8,72},{9,... | collective-permute-start | bytes 786440 | tf_op jit(solution)/shard_map/ppermute | solution.py:35
  148.0 9.6 %collective-permute-start.37 = (bf16[768,256]{1,0:T(8,128)(2,1)}, bf16[768,256]{1,0:T(8,128)(2,1)S(1)}, u32[]{:S(2)}, u32[]{:S(2)}) collective-permute-start(bf16[768,256]{1,0:T(8,128)(2,1)} %get-tuple-element.190), channel_id=1, source_target_pairs={{0,48},{1,13},{2,50},{3,15},{4,52},{5,1},{6,54},{7,3},{8,56},{9,5}... | collective-permute-start | bytes 1179656 | tf_op jit(solution)/shard_map/ppermute | solution.py:35
  148.0 13.4 %collective-permute-start.38 = (bf16[768,256]{1,0:T(8,128)(2,1)}, bf16[768,256]{1,0:T(8,128)(2,1)S(1)}, u32[]{:S(2)}, u32[]{:S(2)}) collective-permute-start(bf16[768,256]{1,0:T(8,128)(2,1)} %get-tuple-element.191), channel_id=1, source_target_pairs={{0,16},{1,5},{2,18},{3,7},{4,20},{5,9},{6,22},{7,11},{8,24},{9,13}... | collective-permute-start | bytes 1179656 | tf_op jit(solution)/shard_map/ppermute | solution.py:35
  150.1 11.4 %collective-permute-start.39 = (bf16[768,256]{1,0:T(8,128)(2,1)}, bf16[768,256]{1,0:T(8,128)(2,1)S(1)}, u32[]{:S(2)}, u32[]{:S(2)}) collective-permute-start(bf16[768,256]{1,0:T(8,128)(2,1)} %get-tuple-element.192), channel_id=1, source_target_pairs={{0,32},{1,9},{2,34},{3,11},{4,36},{5,13},{6,38},{7,15},{8,40},{9,1... | collective-permute-start | bytes 1179656 | tf_op jit(solution)/shard_map/ppermute | solution.py:35
  151.2 6.5 %collective-permute-start.36 = (bf16[512,256]{1,0:T(8,128)(2,1)S(1)}, bf16[512,256]{1,0:T(8,128)(2,1)S(1)}, u32[]{:S(2)}, u32[]{:S(2)}) collective-permute-start(bf16[512,256]{1,0:T(8,128)(2,1)S(1)} %add_convert_fusion), channel_id=1, source_target_pairs={{0,64},{1,65},{2,66},{3,67},{4,68},{5,69},{6,70},{7,71},{8,72},{9,... | collective-permute-start | bytes 786440 | tf_op jit(solution)/shard_map/ppermute | solution.py:35
  163.4 1.5 collective-permute-start.40
  (8 other events, 12.1 us)

commit v5 on v4

--- a/solution.py
+++ b/solution.py
@@ -226,9 +226,13 @@
 
 def backward_kernel(which, count, meta_ref, bounds_ref, masks_ref, own, far, near, cross, *refs):
     arrived, refs = (refs[:2], refs[2:]) if which % 2 else (None, refs)
+    if which == 4:
+        weight, refs = refs[0], refs[1:]
     outs, refs = refs[:count], refs[count:]
-    if which == 1:
+    if which in (1, 4):
         passed, refs = refs[0], refs[1:]
+    if which == 4:
+        passed[...] = weight[...]
     grads, buf, sems, total = refs
     quarter = own.shape[0]
     core, high = bounds_ref[CLASSES + 1], bounds_ref[CLASSES + 2]
@@ -280,6 +284,8 @@
     if which == 1:
         behind = arrived[0].shape[0] - sizes[0] // 2
         sizes = [sizes[0], sizes[1] + behind, 2 * behind]
+    if which == 4:
+        sizes.append(arrived[0].shape[0])
     return pl.pallas_call(
         functools.partial(backward_kernel, which, count),
         in_specs=[smem, smem, held] + [vmem] * (4 + len(arrived)),
@@ -317,7 +323,7 @@
             jax.ShapeDtypeStruct((rows, width), jnp.bfloat16),
             jax.ShapeDtypeStruct((rows, width), jnp.bfloat16),
         ],
-        compiler_params=params(32),
+        compiler_params=params(16),
         cost_estimate=pl.CostEstimate(
             flops=2 * rows * width * width, bytes_accessed=2 * MIB, transcendentals=0
         ),
@@ -357,7 +363,7 @@
         in_specs=[vmem] * 7,
         out_specs=[vmem] * 4,
         out_shape=[jax.ShapeDtypeStruct((rows, width), jnp.bfloat16)] * 4,
-        compiler_params=params(32),
+        compiler_params=params(16),
         cost_estimate=pl.CostEstimate(
             flops=2 * 2 * rows * width * width, bytes_accessed=4 * MIB, transcendentals=rows * width
         ),
@@ -389,7 +395,7 @@
             jax.ShapeDtypeStruct((width, width), jnp.float32),
             jax.ShapeDtypeStruct((width, width), jnp.float32),
         ],
-        compiler_params=params(32),
+        compiler_params=params(16),
         cost_estimate=pl.CostEstimate(
             flops=2 * 2 * rows * width * width, bytes_accessed=2 * MIB, transcendentals=0
         ),
@@ -422,7 +428,7 @@
         in_specs=[vmem] * 3,
         out_specs=[vmem] * 4,
         out_shape=[jax.ShapeDtypeStruct((total // 4, width), jnp.bfloat16)] * 4,
-        compiler_params=params(32),
+        compiler_params=params(16),
         cost_estimate=pl.CostEstimate(flops=0, bytes_accessed=4 * MIB, transcendentals=0),
         name="join",
     )(here, below, above)
@@ -442,7 +448,7 @@
         in_specs=[pl.BlockSpec(memory_space=pl.ANY), vmem, vmem],
         out_specs=vmem,
         out_shape=jax.ShapeDtypeStruct(grad.shape, jnp.float32),
-        compiler_params=params(32),
+        compiler_params=params(16),
         cost_estimate=pl.CostEstimate(flops=0, bytes_accessed=MIB, transcendentals=0),
         name="self_back",
     )(after, grad, self_weight)
@@ -483,7 +489,7 @@
             message, message, message,
             jax.ShapeDtypeStruct(weight.shape, jnp.bfloat16),
         ],
-        compiler_params=params(32),
+        compiler_params=params(16),
         cost_estimate=pl.CostEstimate(flops=0, bytes_accessed=6 * MIB, transcendentals=0),
         name="last_join",
     )(odd, here, below, above, back, low, weight, weight_sides)
@@ -510,7 +516,7 @@
             jax.ShapeDtypeStruct(rest.shape, jnp.bfloat16),
             jax.ShapeDtypeStruct(weight.shape, jnp.float32),
         ],
-        compiler_params=params(32),
+        compiler_params=params(16),
         cost_estimate=pl.CostEstimate(flops=0, bytes_accessed=3 * MIB, transcendentals=0),
         name="finish",
     )(odd, rest, low, from_above, from_below, from_across, weight)
@@ -618,8 +624,7 @@
     grads = (mean, mean_far, mean_near, swap_core(mean_far))
     weight_mine, weight_theirs = weight_parts(core, features, agg, grad)
     weight = (weight_mine + swap_core(weight_theirs)).astype(jnp.bfloat16)
-    weight = add(weight, swap_low(weight))
-    weight = add(weight, swap_high(weight))
+    weight_low = swap_low(weight)
     row_index = lax.axis_index("row")
     odd_x, odd_y = row_index // 4 % 2 == 1, row_index % 2 == 1
     odd_p, odd_q = jnp.where(core == 0, odd_x, odd_y), jnp.where(core == 0, odd_y, odd_x)
@@ -627,7 +632,9 @@
     def backward(which, grads, *arrived):
         return backward_class(which, meta, bounds, tile_masks, grads, *arrived)
 
-    far10, far11 = backward(4, grads)
+    far10, far11, weight = backward(4, grads, weight)
+    weight = add(weight, weight_low)
+    weight = add(weight, swap_high(weight))
     far10, far11, *grads = tie(far10, far11, *grads)
     below1, above1 = move_q(far10, 1), move_q(far11, -1)
     far00, far01 = backward(2, grads)

time: 168 us -> 168 us (level)
  Pallas kernels: 52.4 us -> 48.9 us
  starting transfers between devices: 53.1 us -> 55.3 us
  waiting for transfers between devices: 50.3 us -> 52.2 us
    ppermute x41, starting transfers between devices: 53.1 us -> 55.3 us  [move(): return lax.ppermute(value, BOTH, pairs(step))]
    ppermute x41, waiting for transfers between devices: 50.3 us -> 52.2 us  [move(): return lax.ppermute(value, BOTH, pairs(step))]
    pallas_call x5, Pallas kernels: 18.6 us -> 16.8 us  [backward_class(): pl.pallas_call(functools.partial(backward_kernel, which, count), in_specs...]
    pallas_call x5, Pallas kernels: 16.2 us -> 14.5 us  [forward_class(): pl.pallas_call(functools.partial(forward_kernel, begin, end, len(pieces),...]
  transfers between devices with their start and end apart: 41 -> 41, of which waited for: 17 -> 18; matrix products, arithmetic and copies ran while one was open for 2% -> 2% of each run, Pallas kernels for 27% -> 25%
where the time goes in v5:
time: 168 us; the launch traced here: 166 us
  starting transfers between devices  55.3 us (33%)
  waiting for transfers between devices  52.2 us (31%)
  Pallas kernels  48.9 us (29%)
  local copies, waits for them, and re-layouts  5.46 us (3%)
  other arithmetic  3.39 us (2%)
    ppermute x41, starting transfers between devices, move(): return lax.ppermute(value, BOTH, pairs(step))  55.3 us
    ppermute x41, waiting for transfers between devices, move(): return lax.ppermute(value, BOTH, pairs(step))  52.2 us
    pallas_call x5, Pallas kernels, backward_class(): pl.pallas_call(functools.partial(backward_kernel, which, count), in_specs...  16.8 us
    pallas_call x5, Pallas kernels, forward_class(): pl.pallas_call(functools.partial(forward_kernel, begin, end, len(pieces),...  14.5 us
    pallas_call x2, Pallas kernels, degrees(): pl.pallas_call(functools.partial(degree_kernel, part * slots), in_specs=[...  11.4 us
    unnamed x30, local copies, waits for them, and re-layouts  5.32 us
  transfers between devices with their start and end apart: 41, of which 18 were waited for; matrix products, arithmetic and copies ran while one was open for 2% of the time, Pallas kernels for 25%

profile of v5, /device:TPU:0, one launch (start us, length us, event | category | flops | bytes accessed | tf_op | source)
XLA Modules:
  0.0 166.4 jit_solution(13605278435808752212)
XLA Ops:
  0.6 1.6 collective-permute-start
  2.3 1.7 collective-permute-start.1
  3.9 1.9 %collective-permute-start.2 = (bf16[512,256]{1,0:T(8,128)(2,1)}, bf16[512,256]{1,0:T(8,128)(2,1)S(1)}, u32[]{:S(2)}, u32[]{:S(2)}) collective-permute-start(bf16[512,256]{1,0:T(8,128)(2,1)} %feat_ref.3), channel_id=1, source_target_pairs={{0,32},{1,9},{2,34},{3,11},{4,36},{5,13},{6,38},{7,15},{8,40},{9,1... | collective-permute-start | bytes 786440 | tf_op jit(solution)/shard_map/ppermute | solution.py:35
  5.8 1.9 %collective-permute-start.3 = (bf16[512,256]{1,0:T(8,128)(2,1)}, bf16[512,256]{1,0:T(8,128)(2,1)S(1)}, u32[]{:S(2)}, u32[]{:S(2)}) collective-permute-start(bf16[512,256]{1,0:T(8,128)(2,1)} %feat_ref.3), channel_id=1, source_target_pairs={{0,64},{1,65},{2,66},{3,67},{4,68},{5,69},{6,70},{7,71},{8,72},{9,... | collective-permute-start | bytes 786440 | tf_op jit(solution)/shard_map/ppermute | solution.py:35
  8.4 5.7 %degrees0.1 = (f32[160,128]{1,0:T(8,128)S(1)}, f32[16,128]{1,0:T(8,128)S(1)}) custom-call(s32[320]{0:T(512)S(1)} %copy-done.12, s32[320,128,128]{2,1,0:T(8,128)} %masks_ref.23), custom_call_target="tpu_custom_call" | custom-call | bytes 20971520 | tf_op jit(solution)/shard_map/degrees0/pallas_call | solution.py:96
  15.3 2.3 %collective-permute-start.5 = (bf16[512,256]{1,0:T(8,128)(2,1)S(1)}, bf16[512,256]{1,0:T(8,128)(2,1)S(1)}, u32[]{:S(2)}, u32[]{:S(2)}) collective-permute-start(bf16[512,256]{1,0:T(8,128)(2,1)S(1)} %collective-permute-done.3), channel_id=1, source_target_pairs={{0,48},{1,13},{2,50},{3,15},{4,52},{5,1},{6,54},{7,3},{8,56},{9,5}... | collective-permute-start | bytes 786440 | tf_op jit(solution)/shard_map/ppermute | solution.py:35
  18.7 2.0 %collective-permute-start.10 = (bf16[2048,256]{1,0:T(8,128)(2,1)S(1)}, bf16[2048,256]{1,0:T(8,128)(2,1)S(1)}, u32[]{:S(2)}, u32[]{:S(2)}) collective-permute-start(bf16[2048,256]{1,0:T(8,128)(2,1)S(1)} %pad_maximum_fusion.refs_0_), channel_id=1, source_target_pairs={{0,12},{1,49},{2,14},{3,51},{4,0},{5,53},{6,2},{7,55},{8,4},{9,57}... | collective-permute-start | bytes 3145736 | tf_op jit(solution)/shard_map/ppermute | solution.py:35
  20.8 5.7 %degrees1.1 = (f32[160,128]{1,0:T(8,128)S(1)}, f32[16,128]{1,0:T(8,128)S(1)}) custom-call(s32[320]{0:T(512)S(1)} %copy-done.13, s32[320,128,128]{2,1,0:T(8,128)} %masks_ref.23), custom_call_target="tpu_custom_call" | custom-call | bytes 20971520 | tf_op jit(solution)/shard_map/degrees1/pallas_call | solution.py:96
  27.4 2.6 %collective-permute-start.8 = (bf16[2048,256]{1,0:T(8,128)(2,1)S(1)}, bf16[2048,256]{1,0:T(8,128)(2,1)S(1)}, u32[]{:S(2)}, u32[]{:S(2)}) collective-permute-start(bf16[2048,256]{1,0:T(8,128)(2,1)S(1)} %pad_maximum_fusion.1.refs_1_), channel_id=1, source_target_pairs={{0,12},{1,49},{2,14},{3,51},{4,0},{5,53},{6,2},{7,55},{8,4},{9,57}... | collective-permute-start | bytes 3145736 | tf_op jit(solution)/shard_map/ppermute | solution.py:35
  31.0 2.8 %forward_class0.1.refs_2_ = f32[2176,256]{1,0:T(8,128)S(1)} custom-call(s32[400]{0:T(512)S(1)} %broadcast_add_fusion.meta_ref, s32[8]{0:T(128)S(1)} %pad_add_fusion.bounds_ref, s32[320,128,128]{2,1,0:T(8,128)} %masks_ref.23, bf16[2048,256]{1,0:T(8,128)(2,1)S(1)} %pad_maximum_fusion.refs_0_, bf16[2048,256]{1,0:T(8,128)(2,1)S(1)} %pad_maximum_fusion.1.refs_1_), custom_call_target="tpu_custom_call" | custom-call | bytes 16777216 | tf_op jit(solution)/shard_map/forward_class0/pallas_call | solution.py:214
  33.8 2.9 %collective-permute-done.9.refs_0_ = bf16[2048,256]{1,0:T(8,128)(2,1)S(1)} collective-permute-done((bf16[2048,256]{1,0:T(8,128)(2,1)S(1)}, bf16[2048,256]{1,0:T(8,128)(2,1)S(1)}, u32[]{:S(2)}, u32[]{:S(2)}) %collective-permute-start.9) | collective-permute-done | bytes 1048608 | tf_op jit(solution)/shard_map/ppermute | solution.py:35
  36.8 2.8 %forward_class1.1.refs_2_ = f32[2176,256]{1,0:T(8,128)S(1)} custom-call(s32[400]{0:T(512)S(1)} %broadcast_add_fusion.meta_ref, s32[8]{0:T(128)S(1)} %pad_add_fusion.bounds_ref, s32[320,128,128]{2,1,0:T(8,128)} %masks_ref.23, bf16[2048,256]{1,0:T(8,128)(2,1)S(1)} %collective-permute-done.9.refs_0_, ...), custom_call_target="tpu_custom_call", output_to_operand_aliasing={{}: (5, {})} | custom-call | bytes 16777216 | tf_op jit(solution)/shard_map/forward_class1/pallas_call | solution.py:214
  39.7 3.2 %collective-permute-start.14 = (bf16[1024,256]{1,0:T(8,128)(2,1)S(1)}, bf16[1024,256]{1,0:T(8,128)(2,1)S(1)}, u32[]{:S(2)}, u32[]{:S(2)}) collective-permute-start(bf16[1024,256]{1,0:T(8,128)(2,1)S(1)} %slice.23), channel_id=1, source_target_pairs={{0,12},{1,49},{2,14},{3,51},{4,0},{5,53},{6,2},{7,55},{8,4},{9,57}... | collective-permute-start | bytes 1572872 | tf_op jit(solution)/shard_map/ppermute | solution.py:35
  42.9 5.1 %collective-permute-done.7.refs_0_ = bf16[2048,256]{1,0:T(8,128)(2,1)S(1)} collective-permute-done((bf16[2048,256]{1,0:T(8,128)(2,1)S(1)}, bf16[2048,256]{1,0:T(8,128)(2,1)S(1)}, u32[]{:S(2)}, u32[]{:S(2)}) %collective-permute-start.7) | collective-permute-done | bytes 1048608 | tf_op jit(solution)/shard_map/ppermute | solution.py:35
  48.2 3.2 %collective-permute-start.12 = (bf16[1024,256]{1,0:T(8,128)(2,1)S(1)}, bf16[1024,256]{1,0:T(8,128)(2,1)S(1)}, u32[]{:S(2)}, u32[]{:S(2)}) collective-permute-start(bf16[1024,256]{1,0:T(8,128)(2,1)S(1)} %slice.25), channel_id=1, source_target_pairs={{0,12},{1,49},{2,14},{3,51},{4,0},{5,53},{6,2},{7,55},{8,4},{9,57}... | collective-permute-start | bytes 1572872 | tf_op jit(solution)/shard_map/ppermute | solution.py:35
  51.4 2.8 %forward_class3.1.refs_2_ = f32[2176,256]{1,0:T(8,128)S(1)} custom-call(s32[400]{0:T(512)S(1)} %broadcast_add_fusion.meta_ref, s32[8]{0:T(128)S(1)} %pad_add_fusion.bounds_ref, s32[320,128,128]{2,1,0:T(8,128)} %masks_ref.23, bf16[2048,256]{1,0:T(8,128)(2,1)S(1)} %collective-permute-done.7.refs_0_, ...), custom_call_target="tpu_custom_call", output_to_operand_aliasing={{}: (5, {})} | custom-call | bytes 16777216 | tf_op jit(solution)/shard_map/forward_class3/pallas_call | solution.py:214
  54.2 3.0 %forward_class2.1.refs_2_ = f32[2176,256]{1,0:T(8,128)S(1)} custom-call(s32[400]{0:T(512)S(1)} %broadcast_add_fusion.meta_ref, s32[8]{0:T(128)S(1)} %pad_add_fusion.bounds_ref, s32[320,128,128]{2,1,0:T(8,128)} %masks_ref.23, bf16[1024,256]{1,0:T(8,128)(2,1)S(1)} %collective-permute-done.13.refs_0_, ...), custom_call_target="tpu_custom_call", output_to_operand_aliasing={{}: (5, {})} | custom-call | bytes 16777216 | tf_op jit(solution)/shard_map/forward_class2/pallas_call | solution.py:214
  57.2 2.0 %collective-permute-done.11.refs_0_ = bf16[1024,256]{1,0:T(8,128)(2,1)S(1)} collective-permute-done((bf16[1024,256]{1,0:T(8,128)(2,1)S(1)}, bf16[1024,256]{1,0:T(8,128)(2,1)S(1)}, u32[]{:S(2)}, u32[]{:S(2)}) %collective-permute-start.11) | collective-permute-done | bytes 524320 | tf_op jit(solution)/shard_map/ppermute | solution.py:35
  59.2 3.3 %forward_class4.1 = (bf16[2,512,256]{2,1,0:T(8,128)(2,1)S(1)}, bf16[2,512,256]{2,1,0:T(8,128)(2,1)S(1)}) custom-call(s32[400]{0:T(512)S(1)} %broadcast_add_fusion.meta_ref, s32[8]{0:T(128)S(1)} %pad_add_fusion.bounds_ref, s32[320,128,128]{2,1,0:T(8,128)} %masks_ref.23, bf16[1024,256]{1,0:T(8,128)(2,1)S(1)} %collective-permute-done.11.refs_0_, ...), custom_call_target="tpu_custom_call" | custom-call | bytes 16777216 | tf_op jit(solution)/shard_map/forward_class4/pallas_call | solution.py:214
  62.6 1.9 %collective-permute-done.17.near_ref = bf16[2,512,256]{2,1,0:T(8,128)(2,1)S(1)} collective-permute-done((bf16[2,512,256]{2,1,0:T(8,128)(2,1)S(1)}, bf16[2,512,256]{2,1,0:T(8,128)(2,1)S(1)}, u32[]{:S(2)}, u32[]{:S(2)}) %collective-permute-start.17) | collective-permute-done | bytes 524320 | tf_op jit(solution)/shard_map/ppermute | solution.py:35
  64.6 4.0 %collective-permute-start.18 = (bf16[512,256]{1,0:T(8,128)(2,1)S(1)}, bf16[512,256]{1,0:T(8,128)(2,1)S(1)}, u32[]{:S(2)}, u32[]{:S(2)}) collective-permute-start(bf16[512,256]{1,0:T(8,128)(2,1)S(1)} %fusion.1), channel_id=1, source_target_pairs={{0,2},{1,3},{2,0},{3,1},{4,6},{5,7},{6,4},{7,5},{8,10},{9,11},{10,... | collective-permute-start | bytes 786440 | tf_op jit(solution)/shard_map/ppermute | solution.py:35
  69.9 5.5 %collective-permute-done.16 = f32[16,128]{1,0:T(8,128)S(1)} collective-permute-done((f32[16,128]{1,0:T(8,128)S(1)}, f32[16,128]{1,0:T(8,128)S(1)}, u32[]{:S(2)}, u32[]{:S(2)}) %collective-permute-start.16) | collective-permute-done | bytes 8224 | tf_op jit(solution)/shard_map/ppermute | solution.py:35
  76.8 3.2 %collective-permute-start.19 = (bf16[512,256]{1,0:T(8,128)(2,1)S(1)}, bf16[512,256]{1,0:T(8,128)(2,1)S(1)}, u32[]{:S(2)}, u32[]{:S(2)}) collective-permute-start(bf16[512,256]{1,0:T(8,128)(2,1)S(1)} %get-tuple-element.160.own), channel_id=1, source_target_pairs={{0,2},{1,3},{2,0},{3,1},{4,6},{5,7},{6,4},{7,5},{8,10},{9,11},{10,... | collective-permute-start | bytes 786440 | tf_op jit(solution)/shard_map/ppermute | solution.py:35
  80.9 5.2 %collective-permute-done.19.far = bf16[512,256]{1,0:T(8,128)(2,1)S(1)} collective-permute-done((bf16[512,256]{1,0:T(8,128)(2,1)S(1)}, bf16[512,256]{1,0:T(8,128)(2,1)S(1)}, u32[]{:S(2)}, u32[]{:S(2)}) %collective-permute-start.19) | collective-permute-done | bytes 262176 | tf_op jit(solution)/shard_map/ppermute | solution.py:35
  87.6 3.3 %backward_class4.1 = (bf16[1024,256]{1,0:T(8,128)(2,1)S(1)}, bf16[1024,256]{1,0:T(8,128)(2,1)S(1)}, bf16[256,256]{1,0:T(8,128)(2,1)S(1)}) custom-call(s32[400]{0:T(512)S(1)} %broadcast_add_fusion.meta_ref, s32[8]{0:T(128)S(1)} %pad_add_fusion.bounds_ref, s32[320,128,128]{2,1,0:T(8,128)} %masks_ref.23, bf16[512,256]{1,0:T(8,128)(2,1)S(1)} %get-tuple-element.160.own, ...), custom_call_target="tpu_custom_call" | custom-call | bytes 16777216 | tf_op jit(solution)/shard_map/backward_class4/pallas_call | solution.py:289
  90.9 1.2 collective-permute-done.30
  92.2 3.0 %collective-permute-start.31 = (bf16[256,256]{1,0:T(8,128)(2,1)S(1)}, bf16[256,256]{1,0:T(8,128)(2,1)S(1)}, u32[]{:S(2)}, u32[]{:S(2)}) collective-permute-start(bf16[256,256]{1,0:T(8,128)(2,1)S(1)} %add_convert_fusion.3), channel_id=1, source_target_pairs={{0,2},{1,3},{2,0},{3,1},{4,6},{5,7},{6,4},{7,5},{8,10},{9,11},{10,... | collective-permute-start | bytes 393224 | tf_op jit(solution)/shard_map/ppermute | solution.py:35
  95.2 3.1 %backward_class2.1 = (bf16[1024,256]{1,0:T(8,128)(2,1)S(1)}, bf16[1024,256]{1,0:T(8,128)(2,1)S(1)}) custom-call(s32[400]{0:T(512)S(1)} %broadcast_add_fusion.meta_ref, s32[8]{0:T(128)S(1)} %pad_add_fusion.bounds_ref, s32[320,128,128]{2,1,0:T(8,128)} %masks_ref.23, bf16[512,256]{1,0:T(8,128)(2,1)S(1)} %get-tuple-element.160.own, ...), custom_call_target="tpu_custom_call" | custom-call | bytes 16777216 | tf_op jit(solution)/shard_map/backward_class2/pallas_call | solution.py:289
  98.4 3.2 %collective-permute-start.24 = (bf16[1024,256]{1,0:T(8,128)(2,1)S(1)}, bf16[1024,256]{1,0:T(8,128)(2,1)S(1)}, u32[]{:S(2)}, u32[]{:S(2)}) collective-permute-start(bf16[1024,256]{1,0:T(8,128)(2,1)S(1)} %get-tuple-element.167), channel_id=1, source_target_pairs={{0,12},{1,49},{2,14},{3,51},{4,0},{5,53},{6,2},{7,55},{8,4},{9,57}... | collective-permute-start | bytes 1572872 | tf_op jit(solution)/shard_map/ppermute | solution.py:35
  101.8 3.2 %collective-permute-start.33 = (bf16[1280,256]{1,0:T(8,128)(2,1)S(1)}, bf16[1280,256]{1,0:T(8,128)(2,1)S(1)}, u32[]{:S(2)}, u32[]{:S(2)}) collective-permute-start(bf16[1280,256]{1,0:T(8,128)(2,1)S(1)} %get-tuple-element.202), channel_id=1, source_target_pairs={{0,12},{1,49},{2,14},{3,51},{4,0},{5,53},{6,2},{7,55},{8,4},{9,57}... | collective-permute-start | bytes 1966088 | tf_op jit(solution)/shard_map/ppermute | solution.py:35
  105.0 3.7 %collective-permute-done.23.refs_0_ = bf16[1024,256]{1,0:T(8,128)(2,1)S(1)} collective-permute-done((bf16[1024,256]{1,0:T(8,128)(2,1)S(1)}, bf16[1024,256]{1,0:T(8,128)(2,1)S(1)}, u32[]{:S(2)}, u32[]{:S(2)}) %collective-permute-start.23) | collective-permute-done | bytes 524320 | tf_op jit(solution)/shard_map/ppermute | solution.py:35
  108.7 3.0 %backward_class3.1 = (bf16[2048,256]{1,0:T(8,128)(2,1)S(1)}, bf16[2048,256]{1,0:T(8,128)(2,1)S(1)}) custom-call(s32[400]{0:T(512)S(1)} %broadcast_add_fusion.meta_ref, s32[8]{0:T(128)S(1)} %pad_add_fusion.bounds_ref, s32[320,128,128]{2,1,0:T(8,128)} %masks_ref.23, bf16[512,256]{1,0:T(8,128)(2,1)S(1)} %get-tuple-element.160.own, ...), custom_call_target="tpu_custom_call" | custom-call | bytes 16777216 | tf_op jit(solution)/shard_map/backward_class3/pallas_call | solution.py:289
  111.8 1.9 %collective-permute-start.25 = (bf16[2048,256]{1,0:T(8,128)(2,1)S(1)}, bf16[2048,256]{1,0:T(8,128)(2,1)S(1)}, u32[]{:S(2)}, u32[]{:S(2)}) collective-permute-start(bf16[2048,256]{1,0:T(8,128)(2,1)S(1)} %get-tuple-element.168), channel_id=1, source_target_pairs={{0,4},{1,17},{2,6},{3,19},{4,8},{5,21},{6,10},{7,23},{8,12},{9,25}... | collective-permute-start | bytes 3145736 | tf_op jit(solution)/shard_map/ppermute | solution.py:35
  113.7 3.6 %collective-permute-start.26 = (bf16[2048,256]{1,0:T(8,128)(2,1)S(1)}, bf16[2048,256]{1,0:T(8,128)(2,1)S(1)}, u32[]{:S(2)}, u32[]{:S(2)}) collective-permute-start(bf16[2048,256]{1,0:T(8,128)(2,1)S(1)} %get-tuple-element.169), channel_id=1, source_target_pairs={{0,12},{1,49},{2,14},{3,51},{4,0},{5,53},{6,2},{7,55},{8,4},{9,57}... | collective-permute-start | bytes 3145736 | tf_op jit(solution)/shard_map/ppermute | solution.py:35
  117.3 4.3 %backward_class1.1 = (bf16[2048,256]{1,0:T(8,128)(2,1)}, bf16[2304,256]{1,0:T(8,128)(2,1)}, bf16[512,256]{1,0:T(8,128)(2,1)S(1)}) custom-call(s32[400]{0:T(512)S(1)} %broadcast_add_fusion.meta_ref, s32[8]{0:T(128)S(1)} %pad_add_fusion.bounds_ref, s32[320,128,128]{2,1,0:T(8,128)} %masks_ref.23, bf16[512,256]{1,0:T(8,128)(2,1)S(1)} %get-tuple-element.160.own, ...), custom_call_target="tpu_custom_call" | custom-call | bytes 16777216 | tf_op jit(solution)/shard_map/backward_class1/pallas_call | solution.py:289
  122.1 3.4 %collective-permute-start.35 = (bf16[2048,256]{1,0:T(8,128)(2,1)}, bf16[2048,256]{1,0:T(8,128)(2,1)S(1)}, u32[]{:S(2)}, u32[]{:S(2)}) collective-permute-start(bf16[2048,256]{1,0:T(8,128)(2,1)} %get-tuple-element.183), channel_id=1, source_target_pairs={{0,12},{1,49},{2,14},{3,51},{4,0},{5,53},{6,2},{7,55},{8,4},{9,57}... | collective-permute-start | bytes 3145736 | tf_op jit(solution)/shard_map/ppermute | solution.py:35
  125.5 3.0 %backward_class0.1 = (bf16[2048,256]{1,0:T(8,128)(2,1)S(1)}, bf16[2048,256]{1,0:T(8,128)(2,1)S(1)}) custom-call(s32[400]{0:T(512)S(1)} %broadcast_add_fusion.meta_ref, s32[8]{0:T(128)S(1)} %pad_add_fusion.bounds_ref, s32[320,128,128]{2,1,0:T(8,128)} %masks_ref.23, bf16[512,256]{1,0:T(8,128)(2,1)S(1)} %get-tuple-element.160.own, ...), custom_call_target="tpu_custom_call" | custom-call | bytes 16777216 | tf_op jit(solution)/shard_map/backward_class0/pallas_call | solution.py:289
  128.5 1.5 collective-permute-done.25.below_ref
  131.8 2.0 %collective-permute-start.28 = (bf16[512,256]{1,0:T(8,128)(2,1)}, bf16[512,256]{1,0:T(8,128)(2,1)}, u32[]{:S(2)}, u32[]{:S(2)}) collective-permute-start(bf16[512,256]{1,0:T(8,128)(2,1)} %get-tuple-element.176), channel_id=1, source_target_pairs={{0,16},{1,5},{2,18},{3,7},{4,20},{5,9},{6,22},{7,11},{8,24},{9,13}... | collective-permute-start | bytes 786440 | tf_op jit(solution)/shard_map/ppermute | solution.py:35
  136.0 3.0 %collective-permute-done.27 = bf16[512,256]{1,0:T(8,128)(2,1)} collective-permute-done((bf16[512,256]{1,0:T(8,128)(2,1)}, bf16[512,256]{1,0:T(8,128)(2,1)}, u32[]{:S(2)}, u32[]{:S(2)}) %collective-permute-start.27) | collective-permute-done | bytes 262176 | tf_op jit(solution)/shard_map/ppermute | solution.py:35
  139.0 1.9 %collective-permute-done.28 = bf16[512,256]{1,0:T(8,128)(2,1)} collective-permute-done((bf16[512,256]{1,0:T(8,128)(2,1)}, bf16[512,256]{1,0:T(8,128)(2,1)}, u32[]{:S(2)}, u32[]{:S(2)}) %collective-permute-start.28) | collective-permute-done | bytes 262176 | tf_op jit(solution)/shard_map/ppermute | solution.py:35
  140.9 2.8 %collective-permute-done.35.above_ref = bf16[2048,256]{1,0:T(8,128)(2,1)S(1)} collective-permute-done((bf16[2048,256]{1,0:T(8,128)(2,1)}, bf16[2048,256]{1,0:T(8,128)(2,1)S(1)}, u32[]{:S(2)}, u32[]{:S(2)}) %collective-permute-start.35) | collective-permute-done | bytes 1048608 | tf_op jit(solution)/shard_map/ppermute | solution.py:35
  143.8 1.7 %collective-permute-done.34.below_ref = bf16[2304,256]{1,0:T(8,128)(2,1)S(1)} collective-permute-done((bf16[2304,256]{1,0:T(8,128)(2,1)}, bf16[2304,256]{1,0:T(8,128)(2,1)S(1)}, u32[]{:S(2)}, u32[]{:S(2)}) %collective-permute-start.34) | collective-permute-done | bytes 1179680 | tf_op jit(solution)/shard_map/ppermute | solution.py:35
  146.4 2.2 %last_join.1 = (f32[512,256]{1,0:T(8,128)S(1)}, bf16[768,256]{1,0:T(8,128)(2,1)}, bf16[768,256]{1,0:T(8,128)(2,1)}, bf16[768,256]{1,0:T(8,128)(2,1)}, bf16[256,256]{1,0:T(8,128)(2,1)S(1)}) custom-call(s32[1]{0:T(128)} %bitcast.4.odd_ref, bf16[2048,256]{1,0:T(8,128)(2,1)S(1)} %get-tuple-element.170.here_ref, ...), custom_call_target="tpu_custom_call" | custom-call | bytes 6291456 | tf_op jit(solution)/shard_map/last_join/pallas_call | solution.py:483
  148.7 2.0 %collective-permute-start.38 = (bf16[768,256]{1,0:T(8,128)(2,1)}, bf16[768,256]{1,0:T(8,128)(2,1)S(1)}, u32[]{:S(2)}, u32[]{:S(2)}) collective-permute-start(bf16[768,256]{1,0:T(8,128)(2,1)} %get-tuple-element.193), channel_id=1, source_target_pairs={{0,16},{1,5},{2,18},{3,7},{4,20},{5,9},{6,22},{7,11},{8,24},{9,13}... | collective-permute-start | bytes 1179656 | tf_op jit(solution)/shard_map/ppermute | solution.py:35
  151.9 6.3 %collective-permute-done.36.low_ref = bf16[512,256]{1,0:T(8,128)(2,1)S(1)} collective-permute-done((bf16[512,256]{1,0:T(8,128)(2,1)S(1)}, bf16[512,256]{1,0:T(8,128)(2,1)S(1)}, u32[]{:S(2)}, u32[]{:S(2)}) %collective-permute-start.36) | collective-permute-done | bytes 262176 | tf_op jit(solution)/shard_map/ppermute | solution.py:35
  158.3 3.8 %collective-permute-done.38.up_ref = bf16[768,256]{1,0:T(8,128)(2,1)S(1)} collective-permute-done((bf16[768,256]{1,0:T(8,128)(2,1)}, bf16[768,256]{1,0:T(8,128)(2,1)S(1)}, u32[]{:S(2)}, u32[]{:S(2)}) %collective-permute-start.38) | collective-permute-done | bytes 393248 | tf_op jit(solution)/shard_map/ppermute | solution.py:35
  164.0 1.5 collective-permute-done.40
  (111 shorter events, 20.0 us)
Async XLA Ops:
  0.6 13.6 %copy-start = (bf16[512,256]{1,0:T(8,128)(2,1)S(1)}, bf16[512,256]{1,0:T(8,128)(2,1)}, u32[]{:S(2)}) copy-start(bf16[512,256]{1,0:T(8,128)(2,1)} %feat_ref.3) | copy-start | bytes 786436
  0.6 13.5 %collective-permute-start = (bf16[512,256]{1,0:T(8,128)(2,1)}, bf16[512,256]{1,0:T(8,128)(2,1)S(1)}, u32[]{:S(2)}, u32[]{:S(2)}) collective-permute-start(bf16[512,256]{1,0:T(8,128)(2,1)} %feat_ref.3), channel_id=1, source_target_pairs={{0,16},{1,5},{2,18},{3,7},{4,20},{5,9},{6,22},{7,11},{8,24},{9,13}... | collective-permute-start | bytes 786440 | tf_op jit(solution)/shard_map/ppermute | solution.py:35
  2.3 11.9 %collective-permute-start.1 = (bf16[512,256]{1,0:T(8,128)(2,1)}, bf16[512,256]{1,0:T(8,128)(2,1)S(1)}, u32[]{:S(2)}, u32[]{:S(2)}) collective-permute-start(bf16[512,256]{1,0:T(8,128)(2,1)} %feat_ref.3), channel_id=1, source_target_pairs={{0,48},{1,13},{2,50},{3,15},{4,52},{5,1},{6,54},{7,3},{8,56},{9,5}... | collective-permute-start | bytes 786440 | tf_op jit(solution)/shard_map/ppermute | solution.py:35
  3.9 10.3 %collective-permute-start.2 = (bf16[512,256]{1,0:T(8,128)(2,1)}, bf16[512,256]{1,0:T(8,128)(2,1)S(1)}, u32[]{:S(2)}, u32[]{:S(2)}) collective-permute-start(bf16[512,256]{1,0:T(8,128)(2,1)} %feat_ref.3), channel_id=1, source_target_pairs={{0,32},{1,9},{2,34},{3,11},{4,36},{5,13},{6,38},{7,15},{8,40},{9,1... | collective-permute-start | bytes 786440 | tf_op jit(solution)/shard_map/ppermute | solution.py:35
  5.8 8.4 %collective-permute-start.3 = (bf16[512,256]{1,0:T(8,128)(2,1)}, bf16[512,256]{1,0:T(8,128)(2,1)S(1)}, u32[]{:S(2)}, u32[]{:S(2)}) collective-permute-start(bf16[512,256]{1,0:T(8,128)(2,1)} %feat_ref.3), channel_id=1, source_target_pairs={{0,64},{1,65},{2,66},{3,67},{4,68},{5,69},{6,70},{7,71},{8,72},{9,... | collective-permute-start | bytes 786440 | tf_op jit(solution)/shard_map/ppermute | solution.py:35
  14.2 6.6 %copy-start.13 = (s32[320]{0:T(512)S(1)}, s32[320]{0:T(512)}, u32[]{:S(2)}) copy-start(s32[320]{0:T(512)} %rows_ref.2) | copy-start | bytes 3844
  14.3 12.2 %collective-permute-start.4 = (bf16[512,256]{1,0:T(8,128)(2,1)S(1)}, bf16[512,256]{1,0:T(8,128)(2,1)S(1)}, u32[]{:S(2)}, u32[]{:S(2)}) collective-permute-start(bf16[512,256]{1,0:T(8,128)(2,1)S(1)} %collective-permute-done.3), channel_id=1, source_target_pairs={{0,16},{1,5},{2,18},{3,7},{4,20},{5,9},{6,22},{7,11},{8,24},{9,13}... | collective-permute-start | bytes 786440 | tf_op jit(solution)/shard_map/ppermute | solution.py:35
  15.3 11.2 %collective-permute-start.5 = (bf16[512,256]{1,0:T(8,128)(2,1)S(1)}, bf16[512,256]{1,0:T(8,128)(2,1)S(1)}, u32[]{:S(2)}, u32[]{:S(2)}) collective-permute-start(bf16[512,256]{1,0:T(8,128)(2,1)S(1)} %collective-permute-done.3), channel_id=1, source_target_pairs={{0,48},{1,13},{2,50},{3,15},{4,52},{5,1},{6,54},{7,3},{8,56},{9,5}... | collective-permute-start | bytes 786440 | tf_op jit(solution)/shard_map/ppermute | solution.py:35
  17.6 8.9 %collective-permute-start.6 = (bf16[512,256]{1,0:T(8,128)(2,1)S(1)}, bf16[512,256]{1,0:T(8,128)(2,1)S(1)}, u32[]{:S(2)}, u32[]{:S(2)}) collective-permute-start(bf16[512,256]{1,0:T(8,128)(2,1)S(1)} %collective-permute-done.2), channel_id=1, source_target_pairs={{0,64},{1,65},{2,66},{3,67},{4,68},{5,69},{6,70},{7,71},{8,72},{9,... | collective-permute-start | bytes 786440 | tf_op jit(solution)/shard_map/ppermute | solution.py:35
  18.7 15.1 %collective-permute-start.10 = (bf16[2048,256]{1,0:T(8,128)(2,1)S(1)}, bf16[2048,256]{1,0:T(8,128)(2,1)S(1)}, u32[]{:S(2)}, u32[]{:S(2)}) collective-permute-start(bf16[2048,256]{1,0:T(8,128)(2,1)S(1)} %pad_maximum_fusion.refs_0_), channel_id=1, source_target_pairs={{0,12},{1,49},{2,14},{3,51},{4,0},{5,53},{6,2},{7,55},{8,4},{9,57}... | collective-permute-start | bytes 3145736 | tf_op jit(solution)/shard_map/ppermute | solution.py:35
  20.7 16.0 %collective-permute-start.9 = (bf16[2048,256]{1,0:T(8,128)(2,1)S(1)}, bf16[2048,256]{1,0:T(8,128)(2,1)S(1)}, u32[]{:S(2)}, u32[]{:S(2)}) collective-permute-start(bf16[2048,256]{1,0:T(8,128)(2,1)S(1)} %pad_maximum_fusion.refs_0_), channel_id=1, source_target_pairs={{0,4},{1,17},{2,6},{3,19},{4,8},{5,21},{6,10},{7,23},{8,12},{9,25}... | collective-permute-start | bytes 3145736 | tf_op jit(solution)/shard_map/ppermute | solution.py:35
  26.6 21.4 %collective-permute-start.7 = (bf16[2048,256]{1,0:T(8,128)(2,1)S(1)}, bf16[2048,256]{1,0:T(8,128)(2,1)S(1)}, u32[]{:S(2)}, u32[]{:S(2)}) collective-permute-start(bf16[2048,256]{1,0:T(8,128)(2,1)S(1)} %pad_maximum_fusion.1.refs_1_), channel_id=1, source_target_pairs={{0,4},{1,17},{2,6},{3,19},{4,8},{5,21},{6,10},{7,23},{8,12},{9,25}... | collective-permute-start | bytes 3145736 | tf_op jit(solution)/shard_map/ppermute | solution.py:35
  27.4 20.6 %collective-permute-start.8 = (bf16[2048,256]{1,0:T(8,128)(2,1)S(1)}, bf16[2048,256]{1,0:T(8,128)(2,1)S(1)}, u32[]{:S(2)}, u32[]{:S(2)}) collective-permute-start(bf16[2048,256]{1,0:T(8,128)(2,1)S(1)} %pad_maximum_fusion.1.refs_1_), channel_id=1, source_target_pairs={{0,12},{1,49},{2,14},{3,51},{4,0},{5,53},{6,2},{7,55},{8,4},{9,57}... | collective-permute-start | bytes 3145736 | tf_op jit(solution)/shard_map/ppermute | solution.py:35
  39.6 14.5 %collective-permute-start.13 = (bf16[1024,256]{1,0:T(8,128)(2,1)S(1)}, bf16[1024,256]{1,0:T(8,128)(2,1)S(1)}, u32[]{:S(2)}, u32[]{:S(2)}) collective-permute-start(bf16[1024,256]{1,0:T(8,128)(2,1)S(1)} %slice.22), channel_id=1, source_target_pairs={{0,4},{1,17},{2,6},{3,19},{4,8},{5,21},{6,10},{7,23},{8,12},{9,25}... | collective-permute-start | bytes 1572872 | tf_op jit(solution)/shard_map/ppermute | solution.py:35
  39.7 14.5 %collective-permute-start.14 = (bf16[1024,256]{1,0:T(8,128)(2,1)S(1)}, bf16[1024,256]{1,0:T(8,128)(2,1)S(1)}, u32[]{:S(2)}, u32[]{:S(2)}) collective-permute-start(bf16[1024,256]{1,0:T(8,128)(2,1)S(1)} %slice.23), channel_id=1, source_target_pairs={{0,12},{1,49},{2,14},{3,51},{4,0},{5,53},{6,2},{7,55},{8,4},{9,57}... | collective-permute-start | bytes 1572872 | tf_op jit(solution)/shard_map/ppermute | solution.py:35
  48.1 11.1 %collective-permute-start.11 = (bf16[1024,256]{1,0:T(8,128)(2,1)S(1)}, bf16[1024,256]{1,0:T(8,128)(2,1)S(1)}, u32[]{:S(2)}, u32[]{:S(2)}) collective-permute-start(bf16[1024,256]{1,0:T(8,128)(2,1)S(1)} %slice.24), channel_id=1, source_target_pairs={{0,4},{1,17},{2,6},{3,19},{4,8},{5,21},{6,10},{7,23},{8,12},{9,25}... | collective-permute-start | bytes 1572872 | tf_op jit(solution)/shard_map/ppermute | solution.py:35
  48.2 11.1 %collective-permute-start.12 = (bf16[1024,256]{1,0:T(8,128)(2,1)S(1)}, bf16[1024,256]{1,0:T(8,128)(2,1)S(1)}, u32[]{:S(2)}, u32[]{:S(2)}) collective-permute-start(bf16[1024,256]{1,0:T(8,128)(2,1)S(1)} %slice.25), channel_id=1, source_target_pairs={{0,12},{1,49},{2,14},{3,51},{4,0},{5,53},{6,2},{7,55},{8,4},{9,57}... | collective-permute-start | bytes 1572872 | tf_op jit(solution)/shard_map/ppermute | solution.py:35
  57.1 18.2 %copy-start.7 = (bf16[256,256]{1,0:T(8,128)(2,1)S(1)}, bf16[256,256]{1,0:T(8,128)(2,1)}, u32[]{:S(2)}) copy-start(bf16[256,256]{1,0:T(8,128)(2,1)} %self_ref.3) | copy-start | bytes 393220
  57.2 18.2 %copy-start.8 = (bf16[512,256]{1,0:T(8,128)(2,1)S(1)}, bf16[512,256]{1,0:T(8,128)(2,1)}, u32[]{:S(2)}) copy-start(bf16[512,256]{1,0:T(8,128)(2,1)} %cot_ref.1) | copy-start | bytes 786436
  57.2 18.2 %copy-start.11 = (bf16[256,256]{1,0:T(8,128)(2,1)S(1)}, bf16[256,256]{1,0:T(8,128)(2,1)}, u32[]{:S(2)}) copy-start(bf16[256,256]{1,0:T(8,128)(2,1)} %neigh_ref.1) | copy-start | bytes 393220
  62.5 2.0 %collective-permute-start.17 = (bf16[2,512,256]{2,1,0:T(8,128)(2,1)S(1)}, bf16[2,512,256]{2,1,0:T(8,128)(2,1)S(1)}, u32[]{:S(2)}, u32[]{:S(2)}) collective-permute-start(bf16[2,512,256]{2,1,0:T(8,128)(2,1)S(1)} %get-tuple-element.145), channel_id=1, source_target_pairs={{0,1},{1,0},{2,3},{3,2},{4,5},{5,4},{6,7},{7,6},{8,9},{9,8},{10,11... | collective-permute-start | bytes 1572872 | tf_op jit(solution)/shard_map/ppermute | solution.py:35
  64.6 11.1 %collective-permute-start.18 = (bf16[512,256]{1,0:T(8,128)(2,1)S(1)}, bf16[512,256]{1,0:T(8,128)(2,1)S(1)}, u32[]{:S(2)}, u32[]{:S(2)}) collective-permute-start(bf16[512,256]{1,0:T(8,128)(2,1)S(1)} %fusion.1), channel_id=1, source_target_pairs={{0,2},{1,3},{2,0},{3,1},{4,6},{5,7},{6,4},{7,5},{8,10},{9,11},{10,... | collective-permute-start | bytes 786440 | tf_op jit(solution)/shard_map/ppermute | solution.py:35
  68.6 1.2 collective-permute-start.15
  69.8 5.6 %collective-permute-start.16 = (f32[16,128]{1,0:T(8,128)S(1)}, f32[16,128]{1,0:T(8,128)S(1)}, u32[]{:S(2)}, u32[]{:S(2)}) collective-permute-start(f32[16,128]{1,0:T(8,128)S(1)} %add.136), channel_id=1, source_target_pairs={{0,2},{1,3},{2,0},{3,1},{4,6},{5,7},{6,4},{7,5},{8,10},{9,11},{10,... | collective-permute-start | bytes 24584 | tf_op jit(solution)/shard_map/ppermute | solution.py:35
  76.8 10.0 %copy-start.1 = (bf16[512,256]{1,0:T(8,128)(2,1)}, bf16[512,256]{1,0:T(8,128)(2,1)S(1)}, u32[]{:S(2)}) copy-start(bf16[512,256]{1,0:T(8,128)(2,1)S(1)} %get-tuple-element.149.grad_ref) | copy-start | bytes 786436
  76.8 9.3 %collective-permute-start.19 = (bf16[512,256]{1,0:T(8,128)(2,1)S(1)}, bf16[512,256]{1,0:T(8,128)(2,1)S(1)}, u32[]{:S(2)}, u32[]{:S(2)}) collective-permute-start(bf16[512,256]{1,0:T(8,128)(2,1)S(1)} %get-tuple-element.160.own), channel_id=1, source_target_pairs={{0,2},{1,3},{2,0},{3,1},{4,6},{5,7},{6,4},{7,5},{8,10},{9,11},{10,... | collective-permute-start | bytes 786440 | tf_op jit(solution)/shard_map/ppermute | solution.py:35
  80.4 5.8 %collective-permute-start.22 = (f32[256,256]{1,0:T(8,128)S(1)}, f32[256,256]{1,0:T(8,128)S(1)}, u32[]{:S(2)}, u32[]{:S(2)}) collective-permute-start(f32[256,256]{1,0:T(8,128)S(1)} %get-tuple-element.151), channel_id=1, source_target_pairs={{0,1},{1,0},{2,3},{3,2},{4,5},{5,4},{6,7},{7,6},{8,9},{9,8},{10,11... | collective-permute-start | bytes 786440 | tf_op jit(solution)/shard_map/ppermute | solution.py:35
  80.4 6.3 %collective-permute-start.20 = (bf16[512,256]{1,0:T(8,128)(2,1)S(1)}, bf16[512,256]{1,0:T(8,128)(2,1)S(1)}, u32[]{:S(2)}, u32[]{:S(2)}) collective-permute-start(bf16[512,256]{1,0:T(8,128)(2,1)S(1)} %get-tuple-element.160.own), channel_id=1, source_target_pairs={{0,1},{1,0},{2,3},{3,2},{4,5},{5,4},{6,7},{7,6},{8,9},{9,8},{10,11... | collective-permute-start | bytes 786440 | tf_op jit(solution)/shard_map/ppermute | solution.py:35
  86.1 1.5 collective-permute-start.21
  86.2 6.0 %collective-permute-start.30 = (bf16[256,256]{1,0:T(8,128)(2,1)S(1)}, bf16[256,256]{1,0:T(8,128)(2,1)S(1)}, u32[]{:S(2)}, u32[]{:S(2)}) collective-permute-start(bf16[256,256]{1,0:T(8,128)(2,1)S(1)} %add_convert_fusion.4.refs_0_), channel_id=1, source_target_pairs={{0,64},{1,65},{2,66},{3,67},{4,68},{5,69},{6,70},{7,71},{8,72},{9,... | collective-permute-start | bytes 393224 | tf_op jit(solution)/shard_map/ppermute | solution.py:35
  92.2 9.4 %collective-permute-start.31 = (bf16[256,256]{1,0:T(8,128)(2,1)S(1)}, bf16[256,256]{1,0:T(8,128)(2,1)S(1)}, u32[]{:S(2)}, u32[]{:S(2)}) collective-permute-start(bf16[256,256]{1,0:T(8,128)(2,1)S(1)} %add_convert_fusion.3), channel_id=1, source_target_pairs={{0,2},{1,3},{2,0},{3,1},{4,6},{5,7},{6,4},{7,5},{8,10},{9,11},{10,... | collective-permute-start | bytes 393224 | tf_op jit(solution)/shard_map/ppermute | solution.py:35
  98.3 10.5 %collective-permute-start.23 = (bf16[1024,256]{1,0:T(8,128)(2,1)S(1)}, bf16[1024,256]{1,0:T(8,128)(2,1)S(1)}, u32[]{:S(2)}, u32[]{:S(2)}) collective-permute-start(bf16[1024,256]{1,0:T(8,128)(2,1)S(1)} %get-tuple-element.166), channel_id=1, source_target_pairs={{0,4},{1,17},{2,6},{3,19},{4,8},{5,21},{6,10},{7,23},{8,12},{9,25}... | collective-permute-start | bytes 1572872 | tf_op jit(solution)/shard_map/ppermute | solution.py:35
  98.4 10.4 %collective-permute-start.24 = (bf16[1024,256]{1,0:T(8,128)(2,1)S(1)}, bf16[1024,256]{1,0:T(8,128)(2,1)S(1)}, u32[]{:S(2)}, u32[]{:S(2)}) collective-permute-start(bf16[1024,256]{1,0:T(8,128)(2,1)S(1)} %get-tuple-element.167), channel_id=1, source_target_pairs={{0,12},{1,49},{2,14},{3,51},{4,0},{5,53},{6,2},{7,55},{8,4},{9,57}... | collective-permute-start | bytes 1572872 | tf_op jit(solution)/shard_map/ppermute | solution.py:35
  101.7 15.6 %collective-permute-start.32 = (bf16[1280,256]{1,0:T(8,128)(2,1)S(1)}, bf16[1280,256]{1,0:T(8,128)(2,1)S(1)}, u32[]{:S(2)}, u32[]{:S(2)}) collective-permute-start(bf16[1280,256]{1,0:T(8,128)(2,1)S(1)} %get-tuple-element.203), channel_id=1, source_target_pairs={{0,4},{1,17},{2,6},{3,19},{4,8},{5,21},{6,10},{7,23},{8,12},{9,25}... | collective-permute-start | bytes 1966088 | tf_op jit(solution)/shard_map/ppermute | solution.py:35
  101.8 15.5 %collective-permute-start.33 = (bf16[1280,256]{1,0:T(8,128)(2,1)S(1)}, bf16[1280,256]{1,0:T(8,128)(2,1)S(1)}, u32[]{:S(2)}, u32[]{:S(2)}) collective-permute-start(bf16[1280,256]{1,0:T(8,128)(2,1)S(1)} %get-tuple-element.202), channel_id=1, source_target_pairs={{0,12},{1,49},{2,14},{3,51},{4,0},{5,53},{6,2},{7,55},{8,4},{9,57}... | collective-permute-start | bytes 1966088 | tf_op jit(solution)/shard_map/ppermute | solution.py:35
  111.8 18.2 %collective-permute-start.25 = (bf16[2048,256]{1,0:T(8,128)(2,1)S(1)}, bf16[2048,256]{1,0:T(8,128)(2,1)S(1)}, u32[]{:S(2)}, u32[]{:S(2)}) collective-permute-start(bf16[2048,256]{1,0:T(8,128)(2,1)S(1)} %get-tuple-element.168), channel_id=1, source_target_pairs={{0,4},{1,17},{2,6},{3,19},{4,8},{5,21},{6,10},{7,23},{8,12},{9,25}... | collective-permute-start | bytes 3145736 | tf_op jit(solution)/shard_map/ppermute | solution.py:35
  113.7 16.3 %collective-permute-start.26 = (bf16[2048,256]{1,0:T(8,128)(2,1)S(1)}, bf16[2048,256]{1,0:T(8,128)(2,1)S(1)}, u32[]{:S(2)}, u32[]{:S(2)}) collective-permute-start(bf16[2048,256]{1,0:T(8,128)(2,1)S(1)} %get-tuple-element.169), channel_id=1, source_target_pairs={{0,12},{1,49},{2,14},{3,51},{4,0},{5,53},{6,2},{7,55},{8,4},{9,57}... | collective-permute-start | bytes 3145736 | tf_op jit(solution)/shard_map/ppermute | solution.py:35
  121.7 6.9 %copy-start.9 = (bf16[512,256]{1,0:T(8,128)(2,1)}, bf16[512,256]{1,0:T(8,128)(2,1)S(1)}, u32[]{:S(2)}) copy-start(bf16[512,256]{1,0:T(8,128)(2,1)S(1)} %get-tuple-element.187.sides_ref) | copy-start | bytes 786436
  121.7 23.8 %collective-permute-start.34 = (bf16[2304,256]{1,0:T(8,128)(2,1)}, bf16[2304,256]{1,0:T(8,128)(2,1)S(1)}, u32[]{:S(2)}, u32[]{:S(2)}) collective-permute-start(bf16[2304,256]{1,0:T(8,128)(2,1)} %get-tuple-element.182), channel_id=1, source_target_pairs={{0,4},{1,17},{2,6},{3,19},{4,8},{5,21},{6,10},{7,23},{8,12},{9,25}... | collective-permute-start | bytes 3538952 | tf_op jit(solution)/shard_map/ppermute | solution.py:35
  122.1 21.7 %collective-permute-start.35 = (bf16[2048,256]{1,0:T(8,128)(2,1)}, bf16[2048,256]{1,0:T(8,128)(2,1)S(1)}, u32[]{:S(2)}, u32[]{:S(2)}) collective-permute-start(bf16[2048,256]{1,0:T(8,128)(2,1)} %get-tuple-element.183), channel_id=1, source_target_pairs={{0,12},{1,49},{2,14},{3,51},{4,0},{5,53},{6,2},{7,55},{8,4},{9,57}... | collective-permute-start | bytes 3145736 | tf_op jit(solution)/shard_map/ppermute | solution.py:35
  131.8 7.2 %collective-permute-start.27 = (bf16[512,256]{1,0:T(8,128)(2,1)}, bf16[512,256]{1,0:T(8,128)(2,1)}, u32[]{:S(2)}, u32[]{:S(2)}) collective-permute-start(bf16[512,256]{1,0:T(8,128)(2,1)} %get-tuple-element.175), channel_id=1, source_target_pairs={{0,48},{1,13},{2,50},{3,15},{4,52},{5,1},{6,54},{7,3},{8,56},{9,5}... | collective-permute-start | bytes 786440 | tf_op jit(solution)/shard_map/ppermute | solution.py:35
  131.8 9.1 %collective-permute-start.28 = (bf16[512,256]{1,0:T(8,128)(2,1)}, bf16[512,256]{1,0:T(8,128)(2,1)}, u32[]{:S(2)}, u32[]{:S(2)}) collective-permute-start(bf16[512,256]{1,0:T(8,128)(2,1)} %get-tuple-element.176), channel_id=1, source_target_pairs={{0,16},{1,5},{2,18},{3,7},{4,20},{5,9},{6,22},{7,11},{8,24},{9,13}... | collective-permute-start | bytes 786440 | tf_op jit(solution)/shard_map/ppermute | solution.py:35
  133.8 7.1 %collective-permute-start.29 = (bf16[512,256]{1,0:T(8,128)(2,1)}, bf16[512,256]{1,0:T(8,128)(2,1)}, u32[]{:S(2)}, u32[]{:S(2)}) collective-permute-start(bf16[512,256]{1,0:T(8,128)(2,1)} %get-tuple-element.177), channel_id=1, source_target_pairs={{0,64},{1,65},{2,66},{3,67},{4,68},{5,69},{6,70},{7,71},{8,72},{9,... | collective-permute-start | bytes 786440 | tf_op jit(solution)/shard_map/ppermute | solution.py:35
  148.6 9.6 %collective-permute-start.37 = (bf16[768,256]{1,0:T(8,128)(2,1)}, bf16[768,256]{1,0:T(8,128)(2,1)S(1)}, u32[]{:S(2)}, u32[]{:S(2)}) collective-permute-start(bf16[768,256]{1,0:T(8,128)(2,1)} %get-tuple-element.192), channel_id=1, source_target_pairs={{0,48},{1,13},{2,50},{3,15},{4,52},{5,1},{6,54},{7,3},{8,56},{9,5}... | collective-permute-start | bytes 1179656 | tf_op jit(solution)/shard_map/ppermute | solution.py:35
  148.7 13.4 %collective-permute-start.38 = (bf16[768,256]{1,0:T(8,128)(2,1)}, bf16[768,256]{1,0:T(8,128)(2,1)S(1)}, u32[]{:S(2)}, u32[]{:S(2)}) collective-permute-start(bf16[768,256]{1,0:T(8,128)(2,1)} %get-tuple-element.193), channel_id=1, source_target_pairs={{0,16},{1,5},{2,18},{3,7},{4,20},{5,9},{6,22},{7,11},{8,24},{9,13}... | collective-permute-start | bytes 1179656 | tf_op jit(solution)/shard_map/ppermute | solution.py:35
  150.7 11.4 %collective-permute-start.39 = (bf16[768,256]{1,0:T(8,128)(2,1)}, bf16[768,256]{1,0:T(8,128)(2,1)S(1)}, u32[]{:S(2)}, u32[]{:S(2)}) collective-permute-start(bf16[768,256]{1,0:T(8,128)(2,1)} %get-tuple-element.194), channel_id=1, source_target_pairs={{0,32},{1,9},{2,34},{3,11},{4,36},{5,13},{6,38},{7,15},{8,40},{9,1... | collective-permute-start | bytes 1179656 | tf_op jit(solution)/shard_map/ppermute | solution.py:35
  151.8 6.5 %collective-permute-start.36 = (bf16[512,256]{1,0:T(8,128)(2,1)S(1)}, bf16[512,256]{1,0:T(8,128)(2,1)S(1)}, u32[]{:S(2)}, u32[]{:S(2)}) collective-permute-start(bf16[512,256]{1,0:T(8,128)(2,1)S(1)} %add_convert_fusion), channel_id=1, source_target_pairs={{0,64},{1,65},{2,66},{3,67},{4,68},{5,69},{6,70},{7,71},{8,72},{9,... | collective-permute-start | bytes 786440 | tf_op jit(solution)/shard_map/ppermute | solution.py:35
  164.0 1.5 collective-permute-start.40
  (8 other events, 12.1 us)
